TPU v7x, 32 devices: a whole 2x2x4 slice. The times are simulated.
32 devices in a mesh: gx: 4 (over y, core), gy: 8 (over z, x).
Axes of the slice: x: 2, y: 2, z: 4, core: 2. Of those that a mesh axis runs over, the one named last changes fastest.
Arguments:
- features: bfloat16 [256, 110592], P('gx', 'gy'), may hold values from -6 to 6
- first_weight: bfloat16 [110592, 768], P(('gy', 'gx')), may hold values from -0.01953125 to 0.01953125
- second_weight: bfloat16 [768, 512], replicated, may hold values from -0.21875 to 0.21875
- centres: bfloat16 [155648, 512], P(('gx', 'gy')), may hold values from -6 to 6
- active: int32 [155648], P(('gx', 'gy')), may hold values from 0 to 16127, as said below
- labels: int32 [256], replicated, may hold values from 0 to 516095, as said below
Outputs:
- loss: float32 [], replicated
- grad_first: bfloat16 [110592, 768], P(('gy', 'gx'))
- grad_second: bfloat16 [768, 512], replicated
- grad_centres: bfloat16 [155648, 512], P(('gx', 'gy'))
Inputs may be any that keep to these rules, and one draw needn't show every extreme that they name: Each shard's 4864 entries are distinct and increasing; entry c names class (c // 4864) * 16128 + active[c]. `labels`: every image's class is among the sampled classes, so exactly one centre matches it.
All inputs are finite; a program needn't handle non-finite values.
Results may differ from a plain program's by a relative error of at most 0.0075.
Values may be sent and summed in bfloat16 or wider, within the bound.
No kernel may reach another device: no remote copies, remote signals or barrier semaphores. Data moves between devices by JAX's collectives and lax.ppermute only.
A program may use at most 128 MiB of HBM per device.

v0:
```python
import jax
import jax.numpy as jnp
from jax import lax
from jax.sharding import PartitionSpec as P

CLS_DEV = 16128


LOGIT_SCALE = 64.0
COS_MARGIN = 0.4
NORM_EPSILON = 1e-06


def shards(features, first_weight, second_weight, centres, active, labels):
    gy_count = lax.axis_size("gy")
    device = lax.axis_index("gx") * gy_count + lax.axis_index("gy")
    image_count = labels.shape[0]
    spread = lax.all_to_all(features, "gx", split_axis=1, concat_axis=0, tiled=True)
    block_rows = spread
    hidden = lax.psum_scatter(
        jnp.dot(block_rows, first_weight, preferred_element_type=jnp.float32),
        ("gx", "gy"),
        scatter_dimension=0,
        tiled=True,
    )
    activation, gelu_back = jax.vjp(jax.nn.gelu, hidden)
    act_half = activation.astype(jnp.bfloat16)
    embedding = jnp.dot(act_half, second_weight, preferred_element_type=jnp.float32)
    inv_embed = lax.rsqrt(jnp.sum(embedding * embedding, axis=1, keepdims=True) + NORM_EPSILON)
    unit = embedding * inv_embed
    unit_half = unit.astype(jnp.bfloat16)
    unit_all = lax.all_gather(unit_half, ("gx", "gy"), axis=0, tiled=True)
    cen = centres.astype(jnp.float32)
    inv_cen = lax.rsqrt(jnp.sum(cen * cen, axis=1, keepdims=True) + NORM_EPSILON)
    normed = cen * inv_cen
    normed_half = normed.astype(jnp.bfloat16)
    cosine = jnp.dot(unit_all, normed_half.T, preferred_element_type=jnp.float32)
    classes = device * CLS_DEV + active
    matches = labels[:, None] == classes[None, :]
    positive = matches.astype(jnp.float32)
    logits = LOGIT_SCALE * (cosine - COS_MARGIN * positive)
    exp_terms = jnp.exp(logits - LOGIT_SCALE)
    row_total = jnp.sum(exp_terms, axis=1)
    row_target = jnp.sum(positive * logits, axis=1)
    weighted = jnp.dot(
        exp_terms.astype(jnp.bfloat16), normed_half, preferred_element_type=jnp.float32
    )
    found = jnp.any(matches, axis=1)
    where_found = jnp.argmax(matches.astype(jnp.int32), axis=1)
    picked = normed_half[where_found].astype(jnp.float32) * found[:, None].astype(jnp.float32)
    totals, target = lax.psum((row_total, row_target), ("gx", "gy"))
    factor = LOGIT_SCALE / image_count
    term = factor * (weighted / totals[:, None] - picked)
    grad_unit = lax.psum_scatter(term, ("gx", "gy"), scatter_dimension=0, tiled=True)
    coeff = (factor * (exp_terms / totals[:, None] - positive)).astype(jnp.bfloat16)
    grad_normed = jnp.dot(coeff.T, unit_all, preferred_element_type=jnp.float32)
    grad_cen = inv_cen * (
        grad_normed - normed * jnp.sum(grad_normed * normed, axis=1, keepdims=True)
    )
    loss = jnp.mean(LOGIT_SCALE + jnp.log(totals) - target)
    grad_embed = inv_embed * (grad_unit - unit * jnp.sum(grad_unit * unit, axis=1, keepdims=True))
    grad_embed_half = grad_embed.astype(jnp.bfloat16)
    second_term = jnp.dot(act_half.T, grad_embed_half, preferred_element_type=jnp.float32)
    grad_second = lax.psum(second_term, ("gx", "gy"))
    grad_act = jnp.dot(grad_embed_half, second_weight.T, preferred_element_type=jnp.float32)
    (grad_hidden,) = gelu_back(grad_act)
    grad_hidden_half = grad_hidden.astype(jnp.bfloat16)
    block_rows = spread
    grad_first = jnp.dot(
        block_rows.T,
        lax.all_gather(grad_hidden_half, ("gx", "gy"), axis=0, tiled=True),
        preferred_element_type=jnp.float32,
    )
    return (
        loss,
        grad_first.astype(jnp.bfloat16),
        grad_second.astype(jnp.bfloat16),
        grad_cen.astype(jnp.bfloat16),
    )


def solution(mesh):
    placed = (
        P("gx", "gy"),
        P(("gy", "gx"), None),
        P(),
        P(("gx", "gy"), None),
        P(("gx", "gy")),
        P(),
    )
    return jax.shard_map(
        shards,
        mesh=mesh,
        in_specs=placed,
        out_specs=(P(), P(("gy", "gx"), None), P(), P(("gx", "gy"), None)),
        check_vma=False,
    )
```

profile of v0, /device:TPU:0, one launch (start us, length us, event | category | flops | bytes accessed | tf_op | source)
XLA Modules:
  0.0 548.7 jit_solution(17739436933802246167)
XLA Ops:
  7.2 2.9 copy.30
  10.1 4.2 all-to-all-start
  14.4 7.5 %copy.24 = bf16[4864,512]{0,1:T(8,128)(2,1)} copy(bf16[4864,512]{1,0:T(8,128)(2,1)} %param.9) | data formatting | bytes 9961472 | tf_op args[3]
  21.9 3.4 fusion.7
  25.3 5.5 %fusion.2 = bf16[4864,512]{0,1:T(8,128)(2,1)} fusion(bf16[4864,512]{0,1:T(8,128)(2,1)} %copy.24, f32[4864]{0:T(1024)S(1)} %add_rsqrt_fusion), kind=kLoop, calls=%fused_computation.5 | loop fusion | flops 7471104 | bytes 9980928 | tf_op jit(solution)/shard_map/convert_element_type | solution.py:36
  30.8 7.6 %copy.25 = bf16[4864,512]{1,0:T(8,128)(2,1)} copy(bf16[4864,512]{0,1:T(8,128)(2,1)} %fusion.2) | data formatting | bytes 9961472 | tf_op jit(solution)/shard_map/convert_element_type | solution.py:36
  38.4 0.8 compare_reduce_fusion
  39.2 5.0 fusion.48
  44.2 0.0 reduce-scatter.3.cloned.1.call-update
  44.2 0.0 reduce-scatter.5.cloned.1.call-start
  44.3 2.7 fusion.11
  47.0 5.0 gather_fusion
  52.0 90.4 %reduce-scatter.3.cloned.1.call-done = f32[8,768]{1,0:T(8,128)} async-done(((f32[256,768]{1,0:T(8,128)}), f32[8,768]{1,0:T(8,128)}) %reduce-scatter.3.cloned.1.call-update) | async-done | bytes 24592 | tf_op jit(solution)/shard_map/reduce_scatter | solution.py:20
  142.4 1.1 multiply_reduce_fusion.1
  143.4 0.1 multiply_convert_fusion.2
  143.5 66.1 %all_gather.6 = bf16[256,512]{1,0:T(8,128)(2,1)S(1)} all-gather(bf16[8,512]{1,0:T(8,128)(2,1)S(1)} %multiply_convert_fusion.2), channel_id=1, replica_groups=mesh['gx'=4,'gy'=8] {'gx','gy'}, dimensions={0}, use_global_device_ids=true | all-gather | bytes 270336 | tf_op jit(solution)/shard_map/all_gather | solution.py:32
  209.6 7.0 %fusion.16 = (f32[256]{0:T(256)S(1)}, f32[256]{0:T(256)S(1)}, f32[256,4864]{1,0:T(8,128)}) fusion(s32[4864]{0:T(1024)S(1)} %broadcast_add_fusion, s32[256]{0:T(256)S(1)} %copy-done.5, bf16[256,512]{1,0:T(8,128)(2,1)S(1)} %all_gather.6, bf16[4864,512]{0,1:T(8,128)(2,1)} %fusion.2), kind=kOutput, calls=%fused_computation.27 | convolution fusion | flops 1285029376 | bytes 10246144 | tf_op jit(solution)/shard_map/dot_general | solution.py:37
  216.6 37.3 %psum.21 = f32[256]{0:T(256)S(1)} all-reduce(f32[256]{0:T(256)S(1)} %get-tuple-element.22), channel_id=1, replica_groups=mesh['gx'=4,'gy'=8] {'gx','gy'}, use_global_device_ids=true, to_apply=%region_4.0 | all-reduce | flops 256 | bytes 2048 | tf_op jit(solution)/shard_map/psum | solution.py:51
  254.0 10.9 %fusion.3 = (f32[4864]{0:T(1024)S(1)}, f32[4864,512]{0,1:T(8,128)}) fusion(bf16[4864,512]{0,1:T(8,128)(2,1)} %copy.24, f32[4864]{0:T(1024)S(1)} %add_rsqrt_fusion, bf16[256,512]{1,0:T(8,128)(2,1)} %copy-done.2, f32[256,4864]{1,0:T(8,128)} %get-tuple-element.28, f32[256]{0:T(256)S(1)} %psum.21, s32[4864]{0:T(1024)S(1)} %broadcast_add_fusion, ...), kind=kOutput, calls=%fused_computation.11 | convolution fusion | flops 1293741312 | bytes 20245504 | tf_op jit(solution)/shard_map/dot_general | solution.py:56
  264.9 2.4 fusion.33
  267.2 9.3 %fusion.6 = bf16[4864,512]{0,1:T(8,128)(2,1)} fusion(f32[4864,512]{0,1:T(8,128)} %get-tuple-element.30, bf16[4864,512]{0,1:T(8,128)(2,1)} %copy.24, f32[4864]{0:T(1024)S(1)} %get-tuple-element.29, f32[4864]{0:T(1024)S(1)} %add_rsqrt_fusion), kind=kLoop, calls=%fused_computation.14 | loop fusion | flops 14942208 | bytes 19961856 | tf_op jit(solution)/shard_map/convert_element_type | solution.py:78
  276.6 7.6 %copy.27 = bf16[4864,512]{1,0:T(8,128)(2,1)} copy(bf16[4864,512]{0,1:T(8,128)(2,1)} %fusion.6) | data formatting | bytes 9961472
  284.1 118.4 %reduce-scatter.5.cloned.1.call-done = f32[8,512]{1,0:T(8,128)} async-done(((f32[256,512]{1,0:T(8,128)}), f32[8,512]{1,0:T(8,128)}) %reduce-scatter.5.cloned.1.call-update) | async-done | bytes 16400 | tf_op jit(solution)/shard_map/reduce_scatter | solution.py:54
  402.5 0.9 multiply_reduce_fusion
  403.4 0.8 multiply_convert_fusion.1
  404.2 0.3 fusion.42
  404.5 65.7 %all_gather.7 = bf16[256,768]{1,0:T(8,128)(2,1)S(1)} all-gather(bf16[8,768]{1,0:T(8,128)(2,1)S(1)} %fusion.42), channel_id=1, replica_groups=mesh['gx'=4,'gy'=8] {'gx','gy'}, dimensions={0}, use_global_device_ids=true | all-gather | bytes 405504 | tf_op jit(solution)/shard_map/all_gather | solution.py:71
  470.3 3.9 fusion.9
  474.2 8.0 %copy.26 = bf16[3456,768]{1,0:T(8,128)(2,1)} copy(bf16[3456,768]{0,1:T(8,128)(2,1)} %fusion.9) | data formatting | bytes 10616832
  482.2 0.4 fusion.46
  482.7 56.8 %all-reduce.2 = (f32[256]{0:T(256)S(1)}, bf16[768,512]{1,0:T(8,128)(2,1)}) all-reduce(f32[256]{0:T(256)S(1)} %get-tuple-element.23, f32[768,512]{1,0:T(8,128)S(1)} %fusion.46), channel_id=1, replica_groups=mesh['gx'=4,'gy'=8] {'gx','gy'}, use_global_device_ids=true, to_apply=%region_6.0 | all-reduce | flops 393472 | bytes 2361344 | tf_op jit(solution)/shard_map/psum | solution.py:51
  539.4 0.6 subtract_reduce_fusion
  (28 shorter events, 0.1 us)
Async XLA Ops:
  7.2 135.2 %copy-start = (bf16[768,512]{1,0:T(8,128)(2,1)S(1)}, bf16[768,512]{1,0:T(8,128)(2,1)}, u32[]{:S(2)}) copy-start(bf16[768,512]{1,0:T(8,128)(2,1)} %param.8) | copy-start | bytes 2359300
  10.1 29.1 %all-to-all-start = ((bf16[64,4,3456]{2,0,1:T(8,128)(2,1)}), bf16[64,4,3456]{2,0,1:T(8,128)(2,1)S(1)}, u32[]{:S(2)}, u32[]{:S(2)}) async-start(bf16[64,4,3456]{2,0,1:T(8,128)(2,1)} %bitcast.25), calls=%async_computation | async-start | bytes 3538944 | tf_op jit(solution)/shard_map/all_to_all | solution.py:18
  14.4 128.0 %reduce-scatter.3.cloned.1.call-start = ((), (), s32[]{:S(2)}) async-start(), calls=%async_computation.3 | async-start | bytes 811008 | tf_op jit(solution)/shard_map/reduce_scatter | solution.py:20
  30.8 7.6 %copy-start.4 = (s32[4864]{0:T(1024)S(1)}, s32[4864]{0:T(1024)}, u32[]{:S(2)}) copy-start(s32[4864]{0:T(1024)} %param.10) | copy-start | bytes 58372
  30.8 7.6 %copy-start.5 = (s32[256]{0:T(256)S(1)}, s32[256]{0:T(256)}, u32[]{:S(2)}) copy-start(s32[256]{0:T(256)} %param.11) | copy-start | bytes 3076
  44.2 358.3 %reduce-scatter.5.cloned.1.call-start = ((), (), s32[]{:S(2)}) async-start(), calls=%async_computation.4 | async-start | bytes 540672 | tf_op jit(solution)/shard_map/reduce_scatter | solution.py:54
  209.6 7.0 %copy-start.2 = (bf16[256,512]{1,0:T(8,128)(2,1)}, bf16[256,512]{1,0:T(8,128)(2,1)S(1)}, u32[]{:S(2)}) copy-start(bf16[256,512]{1,0:T(8,128)(2,1)S(1)} %all_gather.6) | copy-start | bytes 786436
  209.6 55.2 %slice-start = ((s8[4980736]{0:T(1024)(128)(4,1)}), s8[786432]{0:T(1024)(128)(4,1)S(1)}, s32[]{:S(2)}) async-start(s8[4980736]{0:T(1024)(128)(4,1)} %bitcast.21), calls=%async_computation.5 | async-start | bytes 1572864
  254.0 10.9 %slice-start.1 = ((s8[4980736]{0:T(1024)(128)(4,1)}), s8[4194304]{0:T(1024)(128)(4,1)S(1)}, s32[]{:S(2)}) async-start(s8[4980736]{0:T(1024)(128)(4,1)} %bitcast.21), calls=%async_computation.6 | async-start | bytes 8388608
  254.0 10.9 %copy-start.1 = (bf16[256,512]{1,0:T(8,128)(2,1)S(1)}, bf16[256,512]{1,0:T(8,128)(2,1)}, u32[]{:S(2)}) copy-start(bf16[256,512]{1,0:T(8,128)(2,1)} %gather_fusion) | copy-start | bytes 786436
  254.0 10.9 %copy-start.6 = (f32[256,4864]{1,0:T(8,128)S(1)}, f32[256,4864]{1,0:T(8,128)}, u32[]{:S(2)}) copy-start(f32[256,4864]{1,0:T(8,128)} %get-tuple-element.28) | copy-start | bytes 14942212
  276.6 127.7 %copy-start.3 = (f32[8,768]{1,0:T(8,128)S(1)}, f32[8,768]{1,0:T(8,128)}, u32[]{:S(2)}) copy-start(f32[8,768]{1,0:T(8,128)} %reduce-scatter.3.cloned.1.call-done) | copy-start | bytes 73732
Sparse Core Ops, SparseCore 0:
  44.3 97.9 reduce-scatter.2
  267.4 135.1 reduce-scatter.4
where the time goes:
time: 550 us; the launch traced here: 549 us
  blocking collectives  226 us (41%)
  waiting for transfers between devices  209 us (38%)
  local copies, waits for them, and re-layouts  38.7 us (7%)
  matrix products  30.9 us (6%)
  other arithmetic  24.1 us (4%)
  between operations  15.9 us (3%)
    reduce_scatter x1, waiting for transfers between devices, shards(): lax.psum_scatter(term, ('gx', 'gy'), scatter_dimension=0, tiled=True)  118 us
    psum x2, blocking collectives, shards(): totals, target = lax.psum((row_total, row_target), ('gx', 'gy'))  94.1 us
    reduce_scatter x1, waiting for transfers between devices, shards(): lax.psum_scatter(jnp.dot(block_rows, first_weight, preferred_element_type...  90.4 us
    all_gather x1, blocking collectives, shards(): unit_all = lax.all_gather(unit_half, ('gx', 'gy'), axis=0, tiled=True)  66.1 us
    all_gather x1, blocking collectives, shards(): lax.all_gather(grad_hidden_half, ('gx', 'gy'), axis=0, tiled=True)  65.7 us
    unnamed x21, local copies, waits for them, and re-layouts  23.2 us
  transfers between devices with their start and end apart: 3, of which 2 were waited for; matrix products, arithmetic and copies ran while one was open for 9% of the time, Pallas kernels for 0%

commit v1 on v0

v1 whole, which is shorter than its diff:
```python
import jax
import jax.numpy as jnp
from jax import lax
from jax.sharding import Mesh, PartitionSpec as P

CLS_DEV = 16128


LOGIT_SCALE = 64.0
COS_MARGIN = 0.4
NORM_EPSILON = 1e-06

PIECE_SCALE = 2.0**64

F32, BF16 = jnp.float32, jnp.bfloat16


def core_swap(x):
    return lax.ppermute(x, "core", [(0, 1), (1, 0)])


def pieces(x):
    high = lax.reduce_precision(x, 8, 7)
    rest = x - high
    middle = lax.reduce_precision(rest, 8, 7)
    return [part.astype(BF16) for part in (high, middle, rest - middle)]


def shards(features, first_weight, second_weight, centres, active, labels):
    rows, gy_count = lax.axis_size("row"), lax.axis_size("gy")
    y, core, gy = lax.axis_index("row"), lax.axis_index("core"), lax.axis_index("gy")
    chips = rows * gy_count
    chip = y * gy_count + gy
    device = (y * 2 + core) * gy_count + gy
    image_count = labels.shape[0]
    half = image_count // 2
    group = features.shape[0]
    own = half // chips
    depth = first_weight.shape[0]

    blocks = {}
    for dy in range(rows):
        for dc in range(2):
            if dy == 0 and dc == 0:
                target = y * 2 + core
                blocks[dy, dc] = lax.dynamic_slice_in_dim(features, target * depth, depth, axis=1)
                continue
            target = ((y + dy) % rows) * 2 + (core ^ dc)
            part = lax.dynamic_slice_in_dim(features, target * depth, depth, axis=1)
            perm = [
                (a * 2 + b, ((a + dy) % rows) * 2 + (b ^ dc)) for a in range(rows) for b in range(2)
            ]
            blocks[dy, dc] = lax.ppermute(part, ("row", "core"), perm)
    order = (y - jnp.arange(rows)) % rows
    halves = []
    for dc in range(2):
        stack = jnp.stack([blocks[dy, dc] for dy in range(rows)])
        if rows == 2:
            stack = jnp.where(y == 0, stack, stack[::-1])
        else:
            stack = stack[order]
        halves.append(stack.reshape(half, depth))
    block_rows = jnp.concatenate(halves)

    marks = labels.reshape(rows, 2, group).transpose(1, 0, 2)
    marks = jnp.where(core == 0, marks, marks[::-1]).reshape(image_count)

    cen = centres.astype(F32)
    inv_cen = lax.rsqrt(jnp.sum(cen * cen, axis=1, keepdims=True) + NORM_EPSILON)
    normed = cen * inv_cen
    normed_half = normed.astype(BF16)
    classes = device * CLS_DEV + active
    positive = (marks[:, None] == classes[None, :]).astype(F32)
    picked = jnp.dot(positive.astype(BF16), normed_half, preferred_element_type=F32).astype(BF16)
    picked = picked[:half] + core_swap(picked[half:])
    picked = lax.all_to_all(picked.reshape(chips, own, -1), ("row", "gy"), 0, 0, tiled=True)
    picked = jnp.sum(picked.astype(F32), axis=0)

    part = jnp.dot(block_rows, first_weight, preferred_element_type=F32)
    part = (part[:half] + core_swap(part[half:])).astype(BF16)
    part = lax.all_to_all(part.reshape(chips, own, -1), ("row", "gy"), 0, 0, tiled=True)
    hidden = jnp.sum(part.astype(F32), axis=0).astype(BF16)
    hidden = jnp.broadcast_to(hidden[None], (chips,) + hidden.shape)
    hidden = lax.all_to_all(hidden, ("row", "gy"), 0, 0, tiled=True).reshape(half, -1)
    hidden = jnp.concatenate([hidden, core_swap(hidden)]).astype(F32)

    activation, gelu_back = jax.vjp(jax.nn.gelu, hidden)
    act_half = activation.astype(BF16)
    embedding = jnp.dot(act_half, second_weight, preferred_element_type=F32)
    inv_embed = lax.rsqrt(jnp.sum(embedding * embedding, axis=1, keepdims=True) + NORM_EPSILON)
    unit = embedding * inv_embed
    unit_half = unit.astype(BF16)

    cosine = jnp.dot(unit_half, normed_half.T, preferred_element_type=F32)
    logits = LOGIT_SCALE * (cosine - COS_MARGIN * positive)
    exp_terms = jnp.exp(logits - LOGIT_SCALE)
    row_total = jnp.sum(exp_terms, axis=1)
    row_target = jnp.sum(positive * logits, axis=1)
    weighted = jnp.dot(exp_terms.astype(BF16), normed_half, preferred_element_type=F32)

    weighted = weighted[:half] + core_swap(weighted[half:])
    sums = jnp.stack([row_total * PIECE_SCALE, row_target])
    sums = sums + jnp.roll(core_swap(sums), half, axis=1)
    total_pieces, target_pieces = pieces(sums[0]), pieces(sums[1])
    nothing = jnp.zeros((2 * image_count,), BF16)
    riding = jnp.concatenate(total_pieces + target_pieces + [nothing]).reshape(own, -1)
    riding = jnp.broadcast_to(riding[None], (chips,) + riding.shape)
    width = weighted.shape[1]
    sent = jnp.concatenate([weighted.astype(BF16).reshape(chips, own, width), riding], axis=2)
    sent = lax.all_to_all(sent, ("row", "gy"), 0, 0, tiled=True).astype(F32)
    sent = jnp.sum(sent, axis=0)
    weighted = sent[:, :width]
    sums = sent[:, width:].reshape(-1)[: 6 * image_count].reshape(2, 3, image_count).sum(axis=1)
    totals, target = sums[0] * (1.0 / PIECE_SCALE), sums[1]

    factor = LOGIT_SCALE / image_count
    mine = chip * own
    totals_own = lax.dynamic_slice_in_dim(totals, mine, own)
    unit_own = lax.dynamic_slice_in_dim(unit, mine, own)
    inv_own = lax.dynamic_slice_in_dim(inv_embed, mine, own)
    grad_unit = factor * (weighted / totals_own[:, None] - picked)
    grad_embed = inv_own * (grad_unit - unit_own * jnp.sum(grad_unit * unit_own, axis=1, keepdims=True))
    grad_embed = grad_embed.astype(BF16)
    grad_embed = jnp.broadcast_to(grad_embed[None], (chips,) + grad_embed.shape)
    grad_embed = lax.all_to_all(grad_embed, ("row", "gy"), 0, 0, tiled=True).reshape(half, -1)
    grad_embed = jnp.concatenate([grad_embed, core_swap(grad_embed)])

    coeff = (factor * (exp_terms / totals[:, None] - positive)).astype(BF16)
    grad_normed = jnp.dot(coeff.T, unit_half, preferred_element_type=F32)
    grad_cen = inv_cen * (
        grad_normed - normed * jnp.sum(grad_normed * normed, axis=1, keepdims=True)
    )
    loss = jnp.mean(LOGIT_SCALE + jnp.log(totals) - target)

    grad_second = jnp.dot(act_half.T, grad_embed, preferred_element_type=F32)
    grad_act = jnp.dot(grad_embed, second_weight.T, preferred_element_type=F32)
    (grad_hidden,) = gelu_back(grad_act)
    grad_first = jnp.dot(block_rows.T, grad_hidden.astype(BF16), preferred_element_type=F32)
    return (
        loss,
        grad_first.astype(BF16),
        grad_second.astype(BF16),
        grad_cen.astype(BF16),
    )


def solution(mesh):
    gx_count, gy_count = mesh.shape["gx"], mesh.shape["gy"]
    fine = Mesh(mesh.devices.reshape(gx_count // 2, 2, gy_count), ("row", "core", "gy"))
    gx = ("row", "core")
    placed = (
        P(gx, "gy"),
        P(("gy",) + gx, None),
        P(),
        P(gx + ("gy",), None),
        P(gx + ("gy",)),
        P(),
    )
    return jax.shard_map(
        shards,
        mesh=fine,
        in_specs=placed,
        out_specs=(P(), P(("gy",) + gx, None), P(), P(gx + ("gy",), None)),
        check_vma=False,
    )
```

time: 550 us -> 140 us (0.25)
  blocking collectives: 226 us -> 0 us
  waiting for transfers between devices: 209 us -> 34.6 us
  starting transfers between devices: 4.28 us -> 28.5 us
  local copies, waits for them, and re-layouts: 38.7 us -> 23 us
  between operations: 15.9 us -> 2.89 us
  other arithmetic: 24.1 us -> 15.2 us
    reduce_scatter x2 -> x0, waiting for transfers between devices: 209 us -> none  [the longest x1 118 us: shards(): lax.psum_scatter(term, ('gx', 'gy'), scatter_dimension=0, tiled=True)]
    all_gather x2 -> x0, blocking collectives: 132 us -> none  [the longest x1 66.1 us: shards(): unit_all = lax.all_gather(unit_half, ('gx', 'gy'), axis=0, tiled=True)]
    psum x2 -> x0, blocking collectives: 94.1 us -> none  [shards(): totals, target = lax.psum((row_total, row_target), ('gx', 'gy'))]
    all_to_all x1 -> x5, waiting for transfers between devices: 0.01 us -> 21.3 us  [the longest x1 8.64 us: shards(): lax.all_to_all(part.reshape(chips, own, -1), ('row', 'gy'), 0, 0, tiled=T...]
    all_to_all x1 -> x5, starting transfers between devices: 4.24 us -> 25.2 us  [the longest x1 7.08 us: shards(): sent = lax.all_to_all(sent, ('row', 'gy'), 0, 0, tiled=True).astype(F32)]
    ppermute x0 -> x9, waiting for transfers between devices: none -> 13.3 us  [the longest x3 12.3 us: shards(): blocks[dy, dc] = lax.ppermute(part, ('row', 'core'), perm)]
    convert_element_type x1 -> x0, local copies, waits for them, and re-layouts: 7.58 us -> none  [shards(): normed_half = normed.astype(jnp.bfloat16)]
    convert_element_type x5 -> x4, other arithmetic: 15.7 us -> 9.4 us  [the longest x1 9.3 us: shards(): grad_cen.astype(BF16)]
  transfers between devices with their start and end apart: 3 -> 14, of which waited for: 2 -> 7; matrix products, arithmetic and copies ran while one was open for 9% -> 39% of each run, Pallas kernels for 0% -> 0%
where the time goes in v1:
time: 140 us; the launch traced here: 139 us
  waiting for transfers between devices  34.6 us (25%)
  matrix products  34.6 us (25%)
  starting transfers between devices  28.5 us (20%)
  local copies, waits for them, and re-layouts  23 us (16%)
  other arithmetic  15.2 us (11%)
  between operations  2.89 us (2%)
    unnamed x30, local copies, waits for them, and re-layouts  17.9 us
    ppermute x3, waiting for transfers between devices, shards(): blocks[dy, dc] = lax.ppermute(part, ('row', 'core'), perm)  12.3 us
    dot_general x1, matrix products, shards(): grad_normed = jnp.dot(coeff.T, unit_half, preferred_element_type=F32)  10.6 us
    convert_element_type x1, other arithmetic, shards(): grad_cen.astype(BF16)  9.3 us
    all_to_all x1, waiting for transfers between devices, shards(): lax.all_to_all(part.reshape(chips, own, -1), ('row', 'gy'), 0, 0, tiled=T...  8.64 us
    all_to_all x1, waiting for transfers between devices, shards(): sent = lax.all_to_all(sent, ('row', 'gy'), 0, 0, tiled=True).astype(F32)  8.63 us
    all_to_all x1, starting transfers between devices, shards(): sent = lax.all_to_all(sent, ('row', 'gy'), 0, 0, tiled=True).astype(F32)  7.08 us
    all_to_all x1, starting transfers between devices, shards(): lax.all_to_all(part.reshape(chips, own, -1), ('row', 'gy'), 0, 0, tiled=T...  6.98 us
  transfers between devices with their start and end apart: 14, of which 7 were waited for; matrix products, arithmetic and copies ran while one was open for 39% of the time, Pallas kernels for 0%

profile of v1, /device:TPU:0, one launch (start us, length us, event | category | flops | bytes accessed | tf_op | source)
XLA Modules:
  0.0 138.7 jit_solution(14991216449551180780)
XLA Ops:
  0.7 2.4 %dynamic-slice_bitcast_fusion = (bf16[1,64,3456]{2,1,0:T(8,128)(2,1)S(1)}, bf16[64,3456]{1,0:T(8,128)(2,1)S(1)}, bf16[64,3456]{1,0:T(8,128)(2,1)S(1)}, bf16[64,3456]{1,0:T(8,128)(2,1)}) fusion(bf16[64,13824]{1,0:T(8,128)(2,1)} %param.6, s32[]{:T(128)S(6)} %select_n.51, s32[]{:T(128)S(6)} %select_n.53, s32[]{:T(128)S(6)} %select_n.57, s32[]{:T(128)S(6)} %select_n.56), kind=kLoop, calls=%fused_computation.59 | loop fusion | bytes 3538960 | tf_op jit(solution)/shard_map/stack | solution.py:57
  3.5 2.6 %collective-permute-start.2 = (bf16[64,3456]{1,0:T(8,128)(2,1)S(1)}, bf16[64,3456]{1,0:T(8,128)(2,1)S(1)}, u32[]{:S(2)}, u32[]{:S(2)}) collective-permute-start(bf16[64,3456]{1,0:T(8,128)(2,1)S(1)} %get-tuple-element.20), channel_id=1, source_target_pairs={{0,24},{8,16},{16,8},{24,0},{1,25},{9,17},{17,9},{25,1},{2,26},{10... | collective-permute-start | bytes 1327112 | tf_op jit(solution)/shard_map/ppermute | solution.py:53
  6.1 7.6 %copy.14 = bf16[4864,512]{0,1:T(8,128)(2,1)} copy(bf16[4864,512]{1,0:T(8,128)(2,1)} %param.9) | data formatting | bytes 9961472 | tf_op args[3]
  13.9 2.8 %collective-permute-done.2 = bf16[64,3456]{1,0:T(8,128)(2,1)S(1)} collective-permute-done((bf16[64,3456]{1,0:T(8,128)(2,1)S(1)}, bf16[64,3456]{1,0:T(8,128)(2,1)S(1)}, u32[]{:S(2)}, u32[]{:S(2)}) %collective-permute-start.2) | collective-permute-done | bytes 442400 | tf_op jit(solution)/shard_map/ppermute | solution.py:53
  16.8 9.6 %collective-permute-done = bf16[64,3456]{1,0:T(8,128)(2,1)S(1)} collective-permute-done((bf16[64,3456]{1,0:T(8,128)(2,1)S(1)}, bf16[64,3456]{1,0:T(8,128)(2,1)S(1)}, u32[]{:S(2)}, u32[]{:S(2)}) %collective-permute-start) | collective-permute-done | bytes 442400 | tf_op jit(solution)/shard_map/ppermute | solution.py:53
  26.8 4.2 %fusion.38 = f32[256,768]{1,0:T(8,128)S(1)} fusion(bf16[3456,768]{1,0:T(8,128)(2,1)} %param.7, bf16[128,3456]{1,0:T(8,128)(2,1)S(1)} %bitcast.32, bf16[128,3456]{1,0:T(8,128)(2,1)S(1)} %bitcast.34), kind=kOutput, calls=%fused_computation.45 | convolution fusion | flops 1362493440 | bytes 7864320 | tf_op jit(solution)/shard_map/dot_general | solution.py:79
  31.2 1.0 fusion.7
  32.9 0.7 fusion.58
  33.6 7.0 %all-to-all-start = ((bf16[16,8,768]{2,1,0:T(8,128)(2,1)}), bf16[16,8,768]{2,1,0:T(8,128)(2,1)S(1)}, u32[]{:S(2)}, u32[]{:S(2)}) async-start(bf16[16,8,768]{2,1,0:T(8,128)(2,1)} %fusion.58), calls=%async_computation | async-start | bytes 393216 | tf_op jit(solution)/shard_map/all_to_all | solution.py:81
  40.6 8.6 %all-to-all-done = bf16[16,8,768]{2,1,0:T(8,128)(2,1)S(1)} async-done(((bf16[16,8,768]{2,1,0:T(8,128)(2,1)}), bf16[16,8,768]{2,1,0:T(8,128)(2,1)S(1)}, u32[]{:S(2)}, u32[]{:S(2)}) %all-to-all-start) | async-done | bytes 196640 | tf_op jit(solution)/shard_map/all_to_all | solution.py:81
  49.3 0.7 broadcast_in_dim.10
  50.0 3.5 %all-to-all-start.1 = ((bf16[16,8,768]{2,1,0:T(8,128)(2,1)}), bf16[16,8,768]{2,1,0:T(8,128)(2,1)S(1)}, u32[]{:S(2)}, u32[]{:S(2)}) async-start(bf16[16,8,768]{2,1,0:T(8,128)(2,1)} %broadcast_in_dim.10), calls=%async_computation.1 | async-start | bytes 393216 | tf_op jit(solution)/shard_map/all_to_all | solution.py:84
  53.5 3.9 %fusion.33 = bf16[256,512]{1,0:T(8,128)(2,1)S(1)} fusion(bf16[4864,512]{0,1:T(8,128)(2,1)} %copy.14, f32[4864]{0:T(1024)S(1)} %add_rsqrt_fusion, s32[4864]{0:T(1024)S(1)} %broadcast_add_fusion, s32[256]{0:T(256)S(1)} %eq.28), kind=kOutput, calls=%fused_computation.44 | convolution fusion | flops 1286406144 | bytes 5282816 | tf_op jit(solution)/shard_map/dot_general | solution.py:74
  57.5 4.0 %all-to-all-done.1 = bf16[16,8,768]{2,1,0:T(8,128)(2,1)S(1)} async-done(((bf16[16,8,768]{2,1,0:T(8,128)(2,1)}), bf16[16,8,768]{2,1,0:T(8,128)(2,1)S(1)}, u32[]{:S(2)}, u32[]{:S(2)}) %all-to-all-start.1) | async-done | bytes 196640 | tf_op jit(solution)/shard_map/all_to_all | solution.py:84
  61.6 0.7 fusion.61
  62.3 4.1 %all-to-all-start.3 = ((bf16[16,8,512]{2,1,0:T(8,128)(2,1)}), bf16[16,8,512]{2,1,0:T(8,128)(2,1)S(1)}, u32[]{:S(2)}, u32[]{:S(2)}) async-start(bf16[16,8,512]{2,1,0:T(8,128)(2,1)} %fusion.61), calls=%async_computation.3 | async-start | bytes 262144 | tf_op jit(solution)/shard_map/all_to_all | solution.py:76
  66.4 1.5 %multiply_reduce_fusion = (f32[256]{0:T(256)S(1)}, f32[256,512]{1,0:T(8,128)S(1)}) fusion(bf16[768,512]{1,0:T(8,128)(2,1)S(1)} %copy-done, bf16[128,768]{1,0:T(8,128)(2,1)} %collective-permute-done.4, bf16[128,768]{1,0:T(8,128)(2,1)S(1)} %bitcast.40), kind=kOutput, calls=%fused_computation.58 | convolution fusion | flops 204144384 | bytes 1704960 | tf_op jit(solution)/shard_map/dot_general | solution.py:89
  68.0 5.0 %fusion.14 = (f32[256]{0:T(256)S(1)}, f32[256]{0:T(256)S(1)}, f32[256,4864]{1,0:T(8,128)S(1)}) fusion(s32[4864]{0:T(1024)S(1)} %broadcast_add_fusion, s32[256]{0:T(256)S(1)} %eq.28, bf16[4864,512]{0,1:T(8,128)(2,1)} %copy.14, f32[4864]{0:T(1024)S(1)} %add_rsqrt_fusion, f32[256,512]{1,0:T(8,128)S(1)} %broadcast_multiply_fusion), kind=kOutput, calls=%fused_computation.22 | convolution fusion | flops 1292631552 | bytes 10527744 | tf_op jit(solution)/shard_map/dot_general | solution.py:94
  73.2 1.5 %fusion.18 = f32[256,512]{1,0:T(8,128)S(1)} fusion(bf16[4864,512]{0,1:T(8,128)(2,1)S(1)} %bitcast.31, f32[4864]{0:T(1024)S(1)} %add_rsqrt_fusion, f32[256,4864]{1,0:T(8,128)S(1)} %get-tuple-element.36), kind=kOutput, calls=%fused_computation.25 | convolution fusion | flops 1285029888 | bytes 10505216 | tf_op jit(solution)/shard_map/dot_general | solution.py:99
  75.3 0.8 copy-done.1
  76.1 0.7 slice.64
  78.7 1.1 fusion.60
  79.8 0.7 pad_maximum_fusion.8
  80.5 7.1 %all-to-all-start.2 = ((bf16[16,8,768]{2,1,0:T(8,128)(2,1)}), bf16[16,8,768]{2,1,0:T(8,128)(2,1)S(1)}, u32[]{:S(2)}, u32[]{:S(2)}) async-start(bf16[16,8,768]{2,1,0:T(8,128)(2,1)} %pad_maximum_fusion.8), calls=%async_computation.2 | async-start | bytes 393216 | tf_op jit(solution)/shard_map/all_to_all | solution.py:110
  87.7 8.6 %all-to-all-done.2 = bf16[16,8,768]{2,1,0:T(8,128)(2,1)S(1)} async-done(((bf16[16,8,768]{2,1,0:T(8,128)(2,1)}), bf16[16,8,768]{2,1,0:T(8,128)(2,1)S(1)}, u32[]{:S(2)}, u32[]{:S(2)}) %all-to-all-start.2) | async-done | bytes 196640 | tf_op jit(solution)/shard_map/all_to_all | solution.py:110
  96.8 0.7 broadcast_in_dim.14
  97.5 3.5 %all-to-all-start.4 = ((bf16[16,8,512]{2,1,0:T(8,128)(2,1)}), bf16[16,8,512]{2,1,0:T(8,128)(2,1)S(1)}, u32[]{:S(2)}, u32[]{:S(2)}) async-start(bf16[16,8,512]{2,1,0:T(8,128)(2,1)} %broadcast_in_dim.14), calls=%async_computation.4 | async-start | bytes 262144 | tf_op jit(solution)/shard_map/all_to_all | solution.py:125
  101.0 10.6 %fusion.3 = (f32[4864]{0:T(1024)S(1)}, f32[4864,512]{0,1:T(8,128)}) fusion(bf16[4864,512]{0,1:T(8,128)(2,1)} %copy.14, f32[4864]{0:T(1024)S(1)} %add_rsqrt_fusion, f32[256,512]{1,0:T(8,128)S(1)} %broadcast_multiply_fusion, f32[256,4864]{1,0:T(8,128)} %copy-done.6, f32[256]{0:T(256)S(1)} %bitcast.49, s32[4864]{0:T(1024)S(1)} %broadcast_add_fusion, s32[256]{0:T(256)S(1)} %eq.28), kind=kOutput, calls=%fused_computation.5 | convolution fusion | flops 1293872384 | bytes 20507648 | tf_op jit(solution)/shard_map/dot_general | solution.py:129
  111.6 9.3 %fusion.6 = bf16[4864,512]{0,1:T(8,128)(2,1)} fusion(f32[4864,512]{0,1:T(8,128)} %get-tuple-element.38, bf16[4864,512]{0,1:T(8,128)(2,1)} %copy.14, f32[4864]{0:T(1024)S(1)} %get-tuple-element.37, f32[4864]{0:T(1024)S(1)} %add_rsqrt_fusion), kind=kLoop, calls=%fused_computation.8 | loop fusion | flops 14942208 | bytes 19961856 | tf_op jit(solution)/shard_map/convert_element_type | solution.py:143
  120.9 7.6 %copy.16 = bf16[4864,512]{1,0:T(8,128)(2,1)} copy(bf16[4864,512]{0,1:T(8,128)(2,1)} %fusion.6) | data formatting | bytes 9961472
  129.8 2.4 %convolution_convert_fusion.1 = bf16[768,512]{1,0:T(8,128)(2,1)} fusion(bf16[128,512]{1,0:T(8,128)(2,1)S(1)} %collective-permute-done.8, bf16[128,512]{1,0:T(8,128)(2,1)S(1)} %bitcast.44, bf16[128,768]{1,0:T(8,128)(2,1)} %collective-permute-done.4, bf16[128,768]{1,0:T(8,128)(2,1)S(1)} %bitcast.41), kind=kOutput, calls=%fused_computation.41 | convolution fusion | flops 204800000 | bytes 1441792 | tf_op jit(solution)/shard_map/dot_general | solution.py:135
  132.2 5.4 %convolution_convert_fusion = bf16[3456,768]{1,0:T(8,128)(2,1)} fusion(bf16[128,3456]{1,0:T(8,128)(2,1)S(1)} %bitcast.33, bf16[128,3456]{1,0:T(8,128)(2,1)S(1)} %bitcast.35, bf16[128,768]{1,0:T(8,128)(2,1)} %collective-permute-done.4, bf16[128,768]{1,0:T(8,128)(2,1)S(1)} %bitcast.42, bf16[768,512]{1,0:T(8,128)(2,1)S(1)} %copy-done, ...), kind=kOutput, calls=%fused_computation.17 | convolution fusion | flops 1571717120 | bytes 8519680 | tf_op jit(solution)/shard_map/dot_general | solution.py:138
  (84 shorter events, 5.9 us)
Async XLA Ops:
  0.6 65.8 %copy-start = (bf16[768,512]{1,0:T(8,128)(2,1)S(1)}, bf16[768,512]{1,0:T(8,128)(2,1)}, u32[]{:S(2)}) copy-start(bf16[768,512]{1,0:T(8,128)(2,1)} %param.8) | copy-start | bytes 2359300
  3.1 10.9 %collective-permute-start.1 = (bf16[64,3456]{1,0:T(8,128)(2,1)}, bf16[64,3456]{1,0:T(8,128)(2,1)S(1)}, u32[]{:S(2)}, u32[]{:S(2)}) collective-permute-start(bf16[64,3456]{1,0:T(8,128)(2,1)} %get-tuple-element.21), channel_id=1, source_target_pairs={{0,8},{8,0},{16,24},{24,16},{1,9},{9,1},{17,25},{25,17},{2,10},{10... | collective-permute-start | bytes 1327112 | tf_op jit(solution)/shard_map/ppermute | solution.py:53
  3.5 13.2 %collective-permute-start.2 = (bf16[64,3456]{1,0:T(8,128)(2,1)S(1)}, bf16[64,3456]{1,0:T(8,128)(2,1)S(1)}, u32[]{:S(2)}, u32[]{:S(2)}) collective-permute-start(bf16[64,3456]{1,0:T(8,128)(2,1)S(1)} %get-tuple-element.20), channel_id=1, source_target_pairs={{0,24},{8,16},{16,8},{24,0},{1,25},{9,17},{17,9},{25,1},{2,26},{10... | collective-permute-start | bytes 1327112 | tf_op jit(solution)/shard_map/ppermute | solution.py:53
  6.1 20.2 %collective-permute-start = (bf16[64,3456]{1,0:T(8,128)(2,1)S(1)}, bf16[64,3456]{1,0:T(8,128)(2,1)S(1)}, u32[]{:S(2)}, u32[]{:S(2)}) collective-permute-start(bf16[64,3456]{1,0:T(8,128)(2,1)S(1)} %get-tuple-element.19), channel_id=1, source_target_pairs={{0,16},{8,24},{16,0},{24,8},{1,17},{9,25},{17,1},{25,9},{2,18},{10... | collective-permute-start | bytes 1327112 | tf_op jit(solution)/shard_map/ppermute | solution.py:53
  6.1 7.6 %copy-start.5 = (s32[256]{0:T(256)S(1)}, s32[256]{0:T(256)}, u32[]{:S(2)}) copy-start(s32[256]{0:T(256)} %param.11) | copy-start | bytes 3076
  26.4 4.7 %slice-start = ((s8[4980736]{0:T(1024)(128)(4,1)}), s8[4194304]{0:T(1024)(128)(4,1)S(1)}, s32[]{:S(2)}) async-start(s8[4980736]{0:T(1024)(128)(4,1)} %bitcast.28), calls=%async_computation.5 | async-start | bytes 8388608
  26.8 4.4 %slice-start.1 = ((s8[4980736]{0:T(1024)(128)(4,1)}), s8[786432]{0:T(1024)(128)(4,1)S(1)}, s32[]{:S(2)}) async-start(s8[4980736]{0:T(1024)(128)(4,1)} %bitcast.28), calls=%async_computation.6 | async-start | bytes 1572864
  31.0 9.6 %copy-start.4 = (s32[4864]{0:T(1024)S(1)}, s32[4864]{0:T(1024)}, u32[]{:S(2)}) copy-start(s32[4864]{0:T(1024)} %param.10) | copy-start | bytes 58372
  31.1 1.8 %collective-permute-start.3 = (f32[128,768]{1,0:T(8,128)S(1)}, f32[128,768]{1,0:T(8,128)S(1)}, u32[]{:S(2)}, u32[]{:S(2)}) collective-permute-start(f32[128,768]{1,0:T(8,128)S(1)} %slice.62), channel_id=1, source_target_pairs={{0,8},{8,0},{1,9},{9,1},{2,10},{10,2},{3,11},{11,3},{4,12},{12,4},... | collective-permute-start | bytes 1179656 | tf_op jit(solution)/shard_map/ppermute | solution.py:19
  33.6 15.7 %all-to-all-start = ((bf16[16,8,768]{2,1,0:T(8,128)(2,1)}), bf16[16,8,768]{2,1,0:T(8,128)(2,1)S(1)}, u32[]{:S(2)}, u32[]{:S(2)}) async-start(bf16[16,8,768]{2,1,0:T(8,128)(2,1)} %fusion.58), calls=%async_computation | async-start | bytes 393216 | tf_op jit(solution)/shard_map/all_to_all | solution.py:81
  50.0 11.6 %all-to-all-start.1 = ((bf16[16,8,768]{2,1,0:T(8,128)(2,1)}), bf16[16,8,768]{2,1,0:T(8,128)(2,1)S(1)}, u32[]{:S(2)}, u32[]{:S(2)}) async-start(bf16[16,8,768]{2,1,0:T(8,128)(2,1)} %broadcast_in_dim.10), calls=%async_computation.1 | async-start | bytes 393216 | tf_op jit(solution)/shard_map/all_to_all | solution.py:84
  57.4 4.1 %collective-permute-start.7 = (bf16[128,512]{1,0:T(8,128)(2,1)S(1)}, bf16[128,512]{1,0:T(8,128)(2,1)S(1)}, u32[]{:S(2)}, u32[]{:S(2)}) collective-permute-start(bf16[128,512]{1,0:T(8,128)(2,1)S(1)} %slice.74), channel_id=1, source_target_pairs={{0,8},{8,0},{1,9},{9,1},{2,10},{10,2},{3,11},{11,3},{4,12},{12,4},... | collective-permute-start | bytes 393224 | tf_op jit(solution)/shard_map/ppermute | solution.py:19
  61.6 6.3 %copy-start.2 = (bf16[16,8,768]{2,1,0:T(8,128)(2,1)}, bf16[16,8,768]{2,1,0:T(8,128)(2,1)S(1)}, u32[]{:S(2)}) copy-start(bf16[16,8,768]{2,1,0:T(8,128)(2,1)S(1)} %all-to-all-done.1) | copy-start | bytes 589828
  61.6 4.8 %collective-permute-start.4 = (bf16[128,768]{1,0:T(8,128)(2,1)S(1)}, bf16[128,768]{1,0:T(8,128)(2,1)}, u32[]{:S(2)}, u32[]{:S(2)}) collective-permute-start(bf16[128,768]{1,0:T(8,128)(2,1)S(1)} %bitcast.39), channel_id=1, source_target_pairs={{0,8},{8,0},{1,9},{9,1},{2,10},{10,2},{3,11},{11,3},{4,12},{12,4},... | collective-permute-start | bytes 589832 | tf_op jit(solution)/shard_map/ppermute | solution.py:19
  62.3 18.2 %all-to-all-start.3 = ((bf16[16,8,512]{2,1,0:T(8,128)(2,1)}), bf16[16,8,512]{2,1,0:T(8,128)(2,1)S(1)}, u32[]{:S(2)}, u32[]{:S(2)}) async-start(bf16[16,8,512]{2,1,0:T(8,128)(2,1)} %fusion.61), calls=%async_computation.3 | async-start | bytes 262144 | tf_op jit(solution)/shard_map/all_to_all | solution.py:76
  67.9 5.3 %slice-start.2 = ((s8[4980736]{0:T(1024)(128)(4,1)}), s8[4194304]{0:T(1024)(128)(4,1)S(1)}, s32[]{:S(2)}) async-start(s8[4980736]{0:T(1024)(128)(4,1)} %bitcast.30), calls=%async_computation.7 | async-start | bytes 8388608
  68.0 5.2 %slice-start.3 = ((s8[4980736]{0:T(1024)(128)(4,1)}), s8[786432]{0:T(1024)(128)(4,1)S(1)}, s32[]{:S(2)}) async-start(s8[4980736]{0:T(1024)(128)(4,1)} %bitcast.30), calls=%async_computation.8 | async-start | bytes 1572864
  73.1 2.3 %copy-start.6 = (f32[256,4864]{1,0:T(8,128)}, f32[256,4864]{1,0:T(8,128)S(1)}, u32[]{:S(2)}) copy-start(f32[256,4864]{1,0:T(8,128)S(1)} %get-tuple-element.36) | copy-start | bytes 14942212
  73.1 3.8 %collective-permute-start.6 = (f32[2,256]{1,0:T(2,128)S(1)}, f32[2,256]{1,0:T(2,128)S(1)}, u32[]{:S(2)}, u32[]{:S(2)}) collective-permute-start(f32[2,256]{1,0:T(2,128)S(1)} %pad_maximum_fusion.15), channel_id=1, source_target_pairs={{0,8},{8,0},{1,9},{9,1},{2,10},{10,2},{3,11},{11,3},{4,12},{12,4},... | collective-permute-start | bytes 6152 | tf_op jit(solution)/shard_map/ppermute | solution.py:19
  75.3 0.8 copy-start.1
  76.8 1.9 %collective-permute-start.5 = (f32[128,512]{1,0:T(8,128)}, f32[128,512]{1,0:T(8,128)}, u32[]{:S(2)}, u32[]{:S(2)}) collective-permute-start(f32[128,512]{1,0:T(8,128)} %slice.64), channel_id=1, source_target_pairs={{0,8},{8,0},{1,9},{9,1},{2,10},{10,2},{3,11},{11,3},{4,12},{12,4},... | collective-permute-start | bytes 786440 | tf_op jit(solution)/shard_map/ppermute | solution.py:19
  80.5 15.8 %all-to-all-start.2 = ((bf16[16,8,768]{2,1,0:T(8,128)(2,1)}), bf16[16,8,768]{2,1,0:T(8,128)(2,1)S(1)}, u32[]{:S(2)}, u32[]{:S(2)}) async-start(bf16[16,8,768]{2,1,0:T(8,128)(2,1)} %pad_maximum_fusion.8), calls=%async_computation.2 | async-start | bytes 393216 | tf_op jit(solution)/shard_map/all_to_all | solution.py:110
  97.5 14.2 %all-to-all-start.4 = ((bf16[16,8,512]{2,1,0:T(8,128)(2,1)}), bf16[16,8,512]{2,1,0:T(8,128)(2,1)S(1)}, u32[]{:S(2)}, u32[]{:S(2)}) async-start(bf16[16,8,512]{2,1,0:T(8,128)(2,1)} %broadcast_in_dim.14), calls=%async_computation.4 | async-start | bytes 262144 | tf_op jit(solution)/shard_map/all_to_all | solution.py:125
  111.6 18.2 %collective-permute-start.8 = (bf16[128,512]{1,0:T(8,128)(2,1)S(1)}, bf16[128,512]{1,0:T(8,128)(2,1)S(1)}, u32[]{:S(2)}, u32[]{:S(2)}) collective-permute-start(bf16[128,512]{1,0:T(8,128)(2,1)S(1)} %bitcast.43), channel_id=1, source_target_pairs={{0,8},{8,0},{1,9},{9,1},{2,10},{10,2},{3,11},{11,3},{4,12},{12,4},... | collective-permute-start | bytes 393224 | tf_op jit(solution)/shard_map/ppermute | solution.py:19
  120.9 8.9 %copy-start.3 = (bf16[16,8,768]{2,1,0:T(8,128)(2,1)S(1)}, bf16[16,8,768]{2,1,0:T(8,128)(2,1)}, u32[]{:S(2)}) copy-start(bf16[16,8,768]{2,1,0:T(8,128)(2,1)} %copy-done.2) | copy-start | bytes 589828

commit v2 on v1

v2 whole, which is shorter than its diff:
```python
import functools

import jax
import jax.numpy as jnp
from jax import lax
from jax.experimental import pallas as pl
from jax.experimental.pallas import tpu as pltpu
from jax.sharding import Mesh, PartitionSpec as P

CLS_DEV = 16128


LOGIT_SCALE = 64.0
COS_MARGIN = 0.4
NORM_EPSILON = 1e-06

PIECE_SCALE = 2.0**64

F32, BF16 = jnp.float32, jnp.bfloat16
MIB = 2**20
VMEM = pl.BlockSpec(memory_space=pltpu.VMEM)
ANY = pl.BlockSpec(memory_space=pl.ANY)

NN = (((1,), (0,)), ((), ()))
NT = (((1,), (1,)), ((), ()))


def dot(a, b, dims=NN):
    return lax.dot_general(a, b, dims, preferred_element_type=F32)


def tile_of(extent, most, unit=16):
    return max(t for t in range(unit, most + 1, unit) if extent % t == 0)


def gelu_parts(v):
    scale = 0.7978845608028654
    cube = 0.044715
    square = v * v
    bend = jnp.tanh(scale * (v + cube * square * v))
    left = 0.5 * (1.0 + bend)
    slope = left + 0.5 * v * (1.0 - bend * bend) * scale * (1.0 + 3.0 * cube * square)
    return v * left, slope


def prep_kernel(cen_ref, marks_ref, classes_ref, half_ref, picked_ref, total):
    step = pl.program_id(0)
    cen = cen_ref[...].astype(F32)
    inv = lax.rsqrt(jnp.sum(cen * cen, axis=1, keepdims=True) + NORM_EPSILON)
    half = (cen * inv).astype(BF16)
    half_ref[...] = half
    match = (marks_ref[...] == classes_ref[0]).astype(F32).astype(BF16)
    found = dot(match, half)

    @pl.when(step == 0)
    def _():
        total[...] = found

    @pl.when(step > 0)
    def _():
        total[...] += found

    @pl.when(step == pl.num_programs(0) - 1)
    def _():
        picked_ref[...] = total[...].astype(BF16)


def prep(centres, marks, classes):
    count, width = centres.shape
    images = marks.shape[0]
    tile = tile_of(count, 1280)
    steps = count // tile
    return pl.pallas_call(
        prep_kernel,
        grid=(steps,),
        in_specs=[
            pl.BlockSpec((tile, width), lambda i: (i, 0)),
            pl.BlockSpec((images, 1), lambda i: (0, 0)),
            pl.BlockSpec((1, 1, tile), lambda i: (i, 0, 0)),
        ],
        out_specs=[
            pl.BlockSpec((tile, width), lambda i: (i, 0)),
            pl.BlockSpec((images, width), lambda i: (0, 0)),
        ],
        out_shape=[
            jax.ShapeDtypeStruct((count, width), BF16),
            jax.ShapeDtypeStruct((images, width), BF16),
        ],
        scratch_shapes=[pltpu.VMEM((images, width), F32)],
        compiler_params=pltpu.CompilerParams(vmem_limit_bytes=32 * MIB),
        cost_estimate=pl.CostEstimate(
            flops=2 * count * width * images, bytes_accessed=4 * count * width, transcendentals=0
        ),
    )(centres, marks, classes.reshape(steps, 1, tile))


def softmax_kernel(
    tile,
    hid_a,
    hid_b,
    second,
    marks,
    classes,
    half_hbm,
    keep,
    send,
    sums,
    unit_out,
    half,
    unit,
    weighted,
    total,
    target,
    cos_even,
    cos_odd,
    sem,
):
    steps = classes.shape[0]

    def copy(i):
        rows = pl.ds(pl.multiple_of(i * tile, tile), tile)
        return pltpu.make_async_copy(half_hbm.at[rows], half.at[rows], sem.at[i])

    def start(i, carry):
        copy(i).start()
        return carry

    lax.fori_loop(0, steps, start, 0)

    group = hid_a.shape[0]
    for place, hid in enumerate((hid_a, hid_b)):
        act, _ = gelu_parts(hid[...].astype(F32))
        embedding = dot(act.astype(BF16), second[...])
        inv = lax.rsqrt(jnp.sum(embedding * embedding, axis=1, keepdims=True) + NORM_EPSILON)
        unit[pl.ds(place * group, group), :] = (embedding * inv).astype(BF16)
    unit_out[...] = unit[...]
    weighted[...] = jnp.zeros_like(weighted)
    total[...] = jnp.zeros_like(total)
    target[...] = jnp.zeros_like(target)

    def part(i):
        return half[pl.ds(pl.multiple_of(i * tile, tile), tile), :]

    def cosine(i, ref):
        copy(i).wait()
        ref[...] = dot(unit[...], part(i), NT)

    def fold(x):
        return functools.reduce(jnp.add, [x[:, c : c + 128] for c in range(0, tile, 128)])

    def process(i, ref):
        positive = marks[...] == classes[i]
        logits = LOGIT_SCALE * (ref[...] - jnp.where(positive, COS_MARGIN, 0.0))
        exp_terms = jnp.exp(logits - LOGIT_SCALE)
        total[...] += fold(exp_terms)
        target[...] += fold(jnp.where(positive, logits, 0.0))
        weighted[...] += dot(exp_terms.astype(BF16), part(i))

    cosine(0, cos_even)

    def pair(j, carry):
        cosine(2 * j + 1, cos_odd)
        process(2 * j, cos_even)
        cosine(2 * j + 2, cos_even)
        process(2 * j + 1, cos_odd)
        return carry

    lax.fori_loop(0, (steps - 1) // 2, pair, 0)
    if steps % 2:
        process(steps - 1, cos_even)
    else:
        cosine(steps - 1, cos_odd)
        process(steps - 2, cos_even)
        process(steps - 1, cos_odd)

    keep[...] = weighted[:group]
    send[...] = weighted[group:]
    sums[...] = jnp.zeros_like(sums)
    sums[0:1, :] = jnp.sum(total[...].T, axis=0, keepdims=True)
    sums[1:2, :] = jnp.sum(target[...].T, axis=0, keepdims=True)


def softmax_sums(hid_a, hid_b, second, marks, classes, half):
    count, width = half.shape
    group = hid_a.shape[0]
    images = marks.shape[0]
    tile = tile_of(count, 256, 128)
    steps = count // tile
    return pl.pallas_call(
        functools.partial(softmax_kernel, tile),
        in_specs=[VMEM] * 5 + [ANY],
        out_specs=[VMEM] * 4,
        out_shape=[
            jax.ShapeDtypeStruct((group, width), F32),
            jax.ShapeDtypeStruct((group, width), F32),
            jax.ShapeDtypeStruct((8, images), F32),
            jax.ShapeDtypeStruct((images, width), BF16),
        ],
        scratch_shapes=[
            pltpu.VMEM((count, width), BF16),
            pltpu.VMEM((images, width), BF16),
            pltpu.VMEM((images, width), F32),
            pltpu.VMEM((images, 128), F32),
            pltpu.VMEM((images, 128), F32),
            pltpu.VMEM((images, tile), F32),
            pltpu.VMEM((images, tile), F32),
            pltpu.SemaphoreType.DMA((steps,)),
        ],
        compiler_params=pltpu.CompilerParams(vmem_limit_bytes=40 * MIB),
        cost_estimate=pl.CostEstimate(
            flops=4 * count * width * images, bytes_accessed=4 * count * width, transcendentals=0
        ),
    )(hid_a, hid_b, second, marks, classes.reshape(steps, 1, tile), half)


def centres_kernel(factor, cen_ref, classes_ref, marks_ref, unit_ref, inv_total_ref, out_ref):
    cen = cen_ref[...].astype(F32)
    inv = lax.rsqrt(jnp.sum(cen * cen, axis=1, keepdims=True) + NORM_EPSILON)
    normed = cen * inv
    unit = unit_ref[...]
    cosine = dot(normed.astype(BF16), unit, NT)
    positive = classes_ref[...] == marks_ref[...]
    logits = LOGIT_SCALE * (cosine - jnp.where(positive, COS_MARGIN, 0.0))
    exp_terms = jnp.exp(logits - LOGIT_SCALE)
    coeff = factor * (exp_terms * inv_total_ref[...] - jnp.where(positive, 1.0, 0.0))
    grad = dot(coeff.astype(BF16), unit)
    grad = inv * (grad - normed * jnp.sum(grad * normed, axis=1, keepdims=True))
    out_ref[...] = grad.astype(BF16)


def grad_centres(centres, classes, marks, unit, inv_total):
    count, width = centres.shape
    images = unit.shape[0]
    tile = tile_of(count, 1280 if images <= 256 else 256)
    return pl.pallas_call(
        functools.partial(centres_kernel, LOGIT_SCALE / images),
        grid=(count // tile,),
        in_specs=[
            pl.BlockSpec((tile, width), lambda i: (i, 0)),
            pl.BlockSpec((tile, 1), lambda i: (i, 0)),
            pl.BlockSpec((1, images), lambda i: (0, 0)),
            pl.BlockSpec((images, width), lambda i: (0, 0)),
            pl.BlockSpec((1, images), lambda i: (0, 0)),
        ],
        out_specs=pl.BlockSpec((tile, width), lambda i: (i, 0)),
        out_shape=jax.ShapeDtypeStruct((count, width), BF16),
        compiler_params=pltpu.CompilerParams(vmem_limit_bytes=40 * MIB),
        cost_estimate=pl.CostEstimate(
            flops=4 * count * width * images, bytes_accessed=4 * count * width, transcendentals=0
        ),
    )(centres, classes, marks, unit, inv_total)


def turn_kernel(rows, place_ref, *refs):
    blocks, out_ref, stack = refs[:-2], refs[-2], refs[-1]
    group, depth = blocks[0].shape
    y = place_ref[0]
    for i, block in enumerate(blocks):
        dy, dc = divmod(i, 2)
        where = dc * rows + lax.rem(y - dy + rows, rows)
        stack[pl.ds(pl.multiple_of(where * group, group), group), :] = block[...]
    width = tile_of(depth, 128)

    if width == 128:

        def turn(i, carry):
            columns = pl.ds(pl.multiple_of(i * width, width), width)
            out_ref[columns, :] = stack[:, columns].T
            return carry

        lax.fori_loop(0, depth // width, turn, 0)
    else:
        out_ref[...] = stack[...].T


def turned(rows, place, blocks):
    group, depth = blocks[0].shape
    images = group * len(blocks)
    return pl.pallas_call(
        functools.partial(turn_kernel, rows),
        in_specs=[pl.BlockSpec(memory_space=pltpu.SMEM)] + [VMEM] * len(blocks),
        out_specs=VMEM,
        out_shape=jax.ShapeDtypeStruct((depth, images), BF16),
        scratch_shapes=[pltpu.VMEM((images, depth), BF16)],
        compiler_params=pltpu.CompilerParams(vmem_limit_bytes=16 * MIB),
        cost_estimate=pl.CostEstimate(
            flops=0, bytes_accessed=4 * depth * images, transcendentals=0
        ),
    )(place, *blocks)


def tail_kernel(grad_a, grad_b, second, slope, act, turned_ref, first_ref, second_ref, grad_hidden):
    group = grad_a.shape[0]

    @pl.when(pl.program_id(0) == 0)
    def _():
        for place, grad in enumerate((grad_a, grad_b)):
            rows = pl.ds(place * group, group)
            grad_act = dot(grad[...], second[...], NT)
            grad_hidden[rows, :] = (grad_act * slope[rows, :]).astype(BF16)
        second_ref[...] = (dot(act[:, :group], grad_a[...]) + dot(act[:, group:], grad_b[...])).astype(BF16)

    first_ref[...] = dot(turned_ref[...], grad_hidden[...]).astype(BF16)


def tail(grad_a, grad_b, second, slope, act, turned_features):
    depth, images = turned_features.shape
    hidden, width = second.shape
    group = grad_a.shape[0]
    tile = tile_of(depth, 512)

    def whole(*shape):
        return pl.BlockSpec(shape, lambda i: (0,) * len(shape))

    return pl.pallas_call(
        tail_kernel,
        grid=(depth // tile,),
        in_specs=[
            whole(group, width),
            whole(group, width),
            whole(hidden, width),
            whole(images, hidden),
            whole(hidden, images),
            pl.BlockSpec((tile, images), lambda i: (i, 0)),
        ],
        out_specs=[pl.BlockSpec((tile, hidden), lambda i: (i, 0)), whole(hidden, width)],
        out_shape=[
            jax.ShapeDtypeStruct((depth, hidden), BF16),
            jax.ShapeDtypeStruct((hidden, width), BF16),
        ],
        scratch_shapes=[pltpu.VMEM((images, hidden), BF16)],
        compiler_params=pltpu.CompilerParams(vmem_limit_bytes=40 * MIB),
        cost_estimate=pl.CostEstimate(
            flops=2 * depth * hidden * images, bytes_accessed=2 * depth * (hidden + images), transcendentals=0
        ),
    )(grad_a, grad_b, second, slope, act, turned_features)


def core_swap(x):
    return lax.ppermute(x, "core", [(0, 1), (1, 0)])


def to_chips(x):
    return lax.all_to_all(x, ("row", "gy"), 0, 0, tiled=True)


def to_all_chips(x, chips):
    x = to_chips(jnp.broadcast_to(x[None], (chips,) + x.shape))
    return x.reshape(-1, x.shape[-1])


def shards(features, first_weight, second_weight, centres, active, labels):
    rows, gy_count = lax.axis_size("row"), lax.axis_size("gy")
    y, core, gy = lax.axis_index("row"), lax.axis_index("core"), lax.axis_index("gy")
    chips = rows * gy_count
    chip = y * gy_count + gy
    device = (y * 2 + core) * gy_count + gy
    image_count = labels.shape[0]
    half = image_count // 2
    group = features.shape[0]
    own = half // chips
    depth = first_weight.shape[0]

    blocks = {}
    source = features
    for dc in (1, 0):
        for dy in list(range(1, rows)) + [0]:
            target = ((y + dy) % rows) * 2 + (core ^ dc)
            part = lax.dynamic_slice_in_dim(source, target * depth, depth, axis=1)
            if (dy, dc) == (0, 0):
                blocks[dy, dc] = part
                continue
            perm = [
                (a * 2 + b, ((a + dy) % rows) * 2 + (b ^ dc)) for a in range(rows) for b in range(2)
            ]
            blocks[dy, dc] = lax.ppermute(part, ("row", "core"), perm)

    marks = labels.reshape(rows, 2, group).transpose(1, 0, 2)
    marks = jnp.where(core == 0, marks, marks[::-1]).reshape(image_count)
    marks_row, marks_column = marks[None, :], marks[:, None]
    classes = device * CLS_DEV + active

    normed_half, picked = prep(centres, marks_column, classes)
    picked = picked[:half] + core_swap(picked[half:])
    picked = to_chips(picked.reshape(chips, own, -1))
    picked = jnp.sum(picked.astype(F32), axis=0)

    def partial_hidden(*names):
        return jnp.dot(
            jnp.concatenate([blocks[n] for n in names]), first_weight, preferred_element_type=F32
        )

    others = list(range(1, rows))
    near = partial_hidden((0, 1), (0, 0))
    far_send = partial_hidden(*[(dy, 1) for dy in others])
    near_keep = near[group:] + core_swap(near[:group])
    far_got = core_swap(far_send)
    far_keep = partial_hidden(*[(dy, 0) for dy in others]) + far_got
    if rows == 2:
        part = jnp.where(
            y == 0,
            jnp.concatenate([near_keep, far_keep]),
            jnp.concatenate([far_keep, near_keep]),
        )
    else:
        part = jnp.concatenate([near_keep, far_keep]).reshape(rows, group, -1)
        part = part[(y - jnp.arange(rows)) % rows]
    part = to_chips(part.astype(BF16).reshape(chips, own, -1))
    hidden_own = jnp.sum(part.astype(F32), axis=0).astype(BF16)
    hid_a = to_all_chips(hidden_own, chips)
    hid_b = core_swap(hid_a)

    embed_own = jnp.dot(
        gelu_parts(hidden_own.astype(F32))[0].astype(BF16), second_weight, preferred_element_type=F32
    )
    inv_own = lax.rsqrt(jnp.sum(embed_own * embed_own, axis=1, keepdims=True) + NORM_EPSILON)
    unit_own = embed_own * inv_own

    weighted, weighted_send, sums, unit_half = softmax_sums(
        hid_a, hid_b, second_weight, marks_column, classes, normed_half
    )
    act, slope = gelu_parts(jnp.concatenate([hid_a, hid_b]).astype(F32))
    act_turned = act.astype(BF16).T

    weighted = weighted + core_swap(weighted_send)
    sums = sums[:2]
    sums = sums + jnp.roll(core_swap(sums), half, axis=1)
    sums = sums * jnp.array([[PIECE_SCALE], [1.0]], F32)
    high = lax.reduce_precision(sums, 8, 7)
    rest = sums - high
    middle = lax.reduce_precision(rest, 8, 7)
    riding = jnp.concatenate([high, middle, rest - middle, jnp.zeros_like(sums)]).astype(BF16)
    riding = riding.reshape(own, -1)
    riding = jnp.broadcast_to(riding[None], (chips,) + riding.shape)
    width = weighted.shape[1]
    sent = jnp.concatenate([weighted.astype(BF16).reshape(chips, own, width), riding], axis=2)
    sent = jnp.sum(to_chips(sent).astype(F32), axis=0)
    weighted = sent[:, :width]
    sums = sent[:, width:].reshape(4, 2, image_count).sum(axis=0)
    totals, target = sums[0:1] * (1.0 / PIECE_SCALE), sums[1:2]

    factor = LOGIT_SCALE / image_count
    totals_own = lax.dynamic_slice_in_dim(totals, chip * own, own, axis=1).reshape(own, 1)
    grad_unit = factor * (weighted / totals_own - picked)
    grad_embed = inv_own * (grad_unit - unit_own * jnp.sum(grad_unit * unit_own, axis=1, keepdims=True))
    grad_a = to_all_chips(grad_embed.astype(BF16), chips)
    grad_b = core_swap(grad_a)

    grad_cen = grad_centres(centres, classes[:, None], marks_row, unit_half, 1.0 / totals)
    loss = jnp.mean(LOGIT_SCALE + jnp.log(totals) - target)

    place = jnp.reshape(y, (1,)).astype(jnp.int32)
    order = [(dy, dc) for dy in range(rows) for dc in range(2)]
    turned_features = turned(rows, place, [blocks[n] for n in order])
    grad_first, grad_second = tail(
        grad_a, grad_b, second_weight, slope, act_turned, turned_features
    )
    return loss, grad_first, grad_second, grad_cen


def solution(mesh):
    gx_count, gy_count = mesh.shape["gx"], mesh.shape["gy"]
    fine = Mesh(mesh.devices.reshape(gx_count // 2, 2, gy_count), ("row", "core", "gy"))
    gx = ("row", "core")
    placed = (
        P(gx, "gy"),
        P(("gy",) + gx, None),
        P(),
        P(gx + ("gy",), None),
        P(gx + ("gy",)),
        P(),
    )
    return jax.shard_map(
        shards,
        mesh=fine,
        in_specs=placed,
        out_specs=(P(), P(("gy",) + gx, None), P(), P(gx + ("gy",), None)),
        check_vma=False,
    )
```

time: 140 us -> 131 us (0.936)
  matrix products: 34.6 us -> 5.64 us
  Pallas kernels: 0 us -> 28.6 us
  other arithmetic: 15.2 us -> 5.91 us
  starting transfers between devices: 28.5 us -> 33 us
  local copies, waits for them, and re-layouts: 23 us -> 20.4 us
    dot_general x8 -> x4, matrix products: 34.6 us -> 5.64 us  [the longest x3 5.32 us: partial_hidden(): jnp.dot(jnp.concatenate([blocks[n] for n in names]), first_weight, prefer...]
    pallas_call x0 -> x5, Pallas kernels: none -> 28.6 us  [the longest x1 9.05 us: softmax_sums(): pl.pallas_call(functools.partial(softmax_kernel, tile), in_specs=[VMEM] *...]
    convert_element_type x4 -> x2, other arithmetic: 9.4 us -> 0.8 us  [the longest x1 0.71 us: shards(): part = to_chips(part.astype(BF16).reshape(chips, own, -1))]
    all_to_all x5, waiting for transfers between devices: 21.3 us -> 16.5 us  [to_chips(): return lax.all_to_all(x, ('row', 'gy'), 0, 0, tiled=True)]
    unnamed x30 -> x42, local copies, waits for them, and re-layouts: 17.9 us -> 14.4 us
    all_to_all x5, starting transfers between devices: 25.2 us -> 28.1 us  [to_chips(): return lax.all_to_all(x, ('row', 'gy'), 0, 0, tiled=True)]
    ppermute x3, waiting for transfers between devices: 12.3 us -> 15.1 us  [shards(): blocks[dy, dc] = lax.ppermute(part, ('row', 'core'), perm)]
    transpose x0 -> x1, other arithmetic: none -> 2.53 us  [shards(): act_turned = act.astype(BF16).T]
  transfers between devices with their start and end apart: 14 -> 15, of which waited for: 7 -> 7; matrix products, arithmetic and copies ran while one was open for 39% -> 9% of each run, Pallas kernels for 0% -> 17%
where the time goes in v2:
time: 131 us; the launch traced here: 130 us
  waiting for transfers between devices  33.2 us (25%)
  starting transfers between devices  33 us (25%)
  Pallas kernels  28.6 us (22%)
  local copies, waits for them, and re-layouts  20.4 us (16%)
  other arithmetic  5.91 us (5%)
  matrix products  5.64 us (4%)
  between operations  2.94 us (2%)
    all_to_all x5, starting transfers between devices, to_chips(): return lax.all_to_all(x, ('row', 'gy'), 0, 0, tiled=True)  28.1 us
    all_to_all x5, waiting for transfers between devices, to_chips(): return lax.all_to_all(x, ('row', 'gy'), 0, 0, tiled=True)  16.5 us
    ppermute x3, waiting for transfers between devices, shards(): blocks[dy, dc] = lax.ppermute(part, ('row', 'core'), perm)  15.1 us
    unnamed x42, local copies, waits for them, and re-layouts  14.4 us
    pallas_call x1, Pallas kernels, softmax_sums(): pl.pallas_call(functools.partial(softmax_kernel, tile), in_specs=[VMEM] *...  9.05 us
    pallas_call x1, Pallas kernels, grad_centres(): pl.pallas_call(functools.partial(centres_kernel, LOGIT_SCALE / images), g...  7.94 us
    pallas_call x1, Pallas kernels, tail(): pl.pallas_call(tail_kernel, grid=(depth // tile,), in_specs=[whole(group,...  6.26 us
    dot_general x3, matrix products, partial_hidden(): jnp.dot(jnp.concatenate([blocks[n] for n in names]), first_weight, prefer...  5.32 us
  transfers between devices with their start and end apart: 15, of which 7 were waited for; matrix products, arithmetic and copies ran while one was open for 9% of the time, Pallas kernels for 17%

profile of v2, /device:TPU:0, one launch (start us, length us, event | category | flops | bytes accessed | tf_op | source)
XLA Modules:
  0.0 129.7 jit_solution(18190920623922141968)
XLA Ops:
  0.7 1.5 %constant_dynamic-slice_fusion.2 = (bf16[64,3456]{1,0:T(8,128)(2,1)S(1)}, bf16[64,3456]{1,0:T(8,128)(2,1)S(1)}, bf16[64,3456]{1,0:T(8,128)(2,1)S(1)}, bf16[64,3456]{1,0:T(8,128)(2,1)S(1)}) fusion(bf16[64,13824]{1,0:T(8,128)(2,1)} %param.7, s32[]{:T(128)S(6)} %select_n.53, s32[]{:T(128)S(6)} %select_n.51, s32[]{:T(128)S(6)} %select_n.50, s32[]{:T(128)S(6)} %select_n.54), kind=kLoop, calls=%fused_computation.66 | loop fusion | bytes 3538960 | tf_op jit(solution)/shard_map/dynamic_slice | solution.py:369
  2.7 2.6 %collective-permute-start.3 = (bf16[64,3456]{1,0:T(8,128)(2,1)S(1)}, bf16[64,3456]{1,0:T(8,128)(2,1)S(1)}, u32[]{:S(2)}, u32[]{:S(2)}) collective-permute-start(bf16[64,3456]{1,0:T(8,128)(2,1)S(1)} %get-tuple-element.25), channel_id=1, source_target_pairs={{0,24},{8,16},{16,8},{24,0},{1,25},{9,17},{17,9},{25,1},{2,26},{10... | collective-permute-start | bytes 1327112 | tf_op jit(solution)/shard_map/ppermute | solution.py:376
  5.4 3.5 %fusion.2 = f32[128,768]{1,0:T(8,128)S(1)} fusion(bf16[3456,768]{1,0:T(8,128)(2,1)} %param.8, bf16[64,3456]{1,0:T(8,128)(2,1)S(1)} %get-tuple-element.23.refs_0_, bf16[64,3456]{1,0:T(8,128)(2,1)S(1)} %collective-permute-done.refs_1_), kind=kOutput, calls=%fused_computation.8 | convolution fusion | flops 681246720 | bytes 6586368 | tf_op jit(solution)/shard_map/dot_general | solution.py:389
  9.2 6.7 %collective-permute-done.3.refs_3_ = bf16[64,3456]{1,0:T(8,128)(2,1)S(1)} collective-permute-done((bf16[64,3456]{1,0:T(8,128)(2,1)S(1)}, bf16[64,3456]{1,0:T(8,128)(2,1)S(1)}, u32[]{:S(2)}, u32[]{:S(2)}) %collective-permute-start.3) | collective-permute-done | bytes 442400 | tf_op jit(solution)/shard_map/ppermute | solution.py:376
  15.9 0.9 fusion.43
  17.2 8.4 %collective-permute-done.2.refs_2_ = bf16[64,3456]{1,0:T(8,128)(2,1)S(1)} collective-permute-done((bf16[64,3456]{1,0:T(8,128)(2,1)S(1)}, bf16[64,3456]{1,0:T(8,128)(2,1)S(1)}, u32[]{:S(2)}, u32[]{:S(2)}) %collective-permute-start.2) | collective-permute-done | bytes 442400 | tf_op jit(solution)/shard_map/ppermute | solution.py:376
  25.6 0.9 convolution_add_fusion
  26.5 0.7 fusion.16
  27.2 7.1 %all-to-all-start = ((bf16[16,8,768]{2,1,0:T(8,128)(2,1)}), bf16[16,8,768]{2,1,0:T(8,128)(2,1)S(1)}, u32[]{:S(2)}, u32[]{:S(2)}) async-start(bf16[16,8,768]{2,1,0:T(8,128)(2,1)} %fusion.16), calls=%async_computation | async-start | bytes 393216 | tf_op jit(solution)/shard_map/all_to_all | solution.py:344
  34.6 7.9 %all-to-all-done = bf16[16,8,768]{2,1,0:T(8,128)(2,1)S(1)} async-done(((bf16[16,8,768]{2,1,0:T(8,128)(2,1)}), bf16[16,8,768]{2,1,0:T(8,128)(2,1)S(1)}, u32[]{:S(2)}, u32[]{:S(2)}) %all-to-all-start) | async-done | bytes 196640 | tf_op jit(solution)/shard_map/all_to_all | solution.py:344
  42.5 0.7 broadcast_in_dim.10
  43.2 3.5 %all-to-all-start.1 = ((bf16[16,8,768]{2,1,0:T(8,128)(2,1)}), bf16[16,8,768]{2,1,0:T(8,128)(2,1)S(1)}, u32[]{:S(2)}, u32[]{:S(2)}) async-start(bf16[16,8,768]{2,1,0:T(8,128)(2,1)} %broadcast_in_dim.10), calls=%async_computation.1 | async-start | bytes 393216 | tf_op jit(solution)/shard_map/all_to_all | solution.py:344
  46.9 2.4 %copy-done = bf16[4864,512]{1,0:T(8,128)(2,1)S(1)} copy-done((bf16[4864,512]{1,0:T(8,128)(2,1)S(1)}, bf16[4864,512]{1,0:T(8,128)(2,1)}, u32[]{:S(2)}) %copy-start) | copy-done | bytes 4980760
  49.3 3.3 %shard_map.102 = (bf16[4864,512]{1,0:T(8,128)(2,1)S(1)}, bf16[256,512]{1,0:T(8,128)(2,1)S(1)}) custom-call(bf16[4864,512]{1,0:T(8,128)(2,1)S(1)} %copy-done, s32[256,1]{1,0:T(8,128)S(1)} %broadcast_in_dim_reshape.8.marks_ref.marks, s32[4,1,1216]{2,1,0:T(1,128)S(1)} %reshape.81.classes_ref), custom_call_target="tpu_custom_call" | custom-call | flops 1275068416 | bytes 9961472 | tf_op jit(solution)/shard_map/pallas_call | solution.py:73
  52.7 2.3 %copy-done.13 = bf16[4864,512]{1,0:T(8,128)(2,1)} copy-done((bf16[4864,512]{1,0:T(8,128)(2,1)}, bf16[4864,512]{1,0:T(8,128)(2,1)S(1)}, u32[]{:S(2)}) %copy-start.13) | copy-done | bytes 4980760
  57.0 6.9 %all-to-all-start.3 = ((bf16[16,8,512]{2,1,0:T(8,128)(2,1)}), bf16[16,8,512]{2,1,0:T(8,128)(2,1)S(1)}, u32[]{:S(2)}, u32[]{:S(2)}) async-start(bf16[16,8,512]{2,1,0:T(8,128)(2,1)} %add_bitcast_fusion), calls=%async_computation.3 | async-start | bytes 262144 | tf_op jit(solution)/shard_map/all_to_all | solution.py:344
  64.2 2.4 %copy-done.14 = bf16[4864,512]{1,0:T(8,128)(2,1)S(1)} copy-done((bf16[4864,512]{1,0:T(8,128)(2,1)S(1)}, bf16[4864,512]{1,0:T(8,128)(2,1)}, u32[]{:S(2)}) %copy-start.14) | copy-done | bytes 4980760
  66.6 9.0 %shard_map.103 = (f32[128,512]{1,0:T(8,128)S(1)}, f32[128,512]{1,0:T(8,128)S(1)}, f32[8,256]{1,0:T(8,128)S(1)}, bf16[256,512]{1,0:T(8,128)(2,1)S(1)}) custom-call(bf16[128,768]{1,0:T(8,128)(2,1)S(1)} %bitcast.22, bf16[128,768]{1,0:T(8,128)(2,1)S(1)} %copy.17.hid_b, bf16[768,512]{1,0:T(8,128)(2,1)S(1)} %copy-done.8, ...), custom_call_target="tpu_custom_call" | custom-call | flops 2550136832 | bytes 9961472 | tf_op jit(solution)/shard_map/pallas_call | solution.py:189
  78.2 0.7 pad_maximum_fusion.1
  78.9 6.9 %all-to-all-start.2 = ((bf16[16,8,768]{2,1,0:T(8,128)(2,1)}), bf16[16,8,768]{2,1,0:T(8,128)(2,1)S(1)}, u32[]{:S(2)}, u32[]{:S(2)}) async-start(bf16[16,8,768]{2,1,0:T(8,128)(2,1)} %pad_maximum_fusion.1), calls=%async_computation.2 | async-start | bytes 393216 | tf_op jit(solution)/shard_map/all_to_all | solution.py:344
  86.2 8.6 %all-to-all-done.2 = bf16[16,8,768]{2,1,0:T(8,128)(2,1)S(1)} async-done(((bf16[16,8,768]{2,1,0:T(8,128)(2,1)}), bf16[16,8,768]{2,1,0:T(8,128)(2,1)S(1)}, u32[]{:S(2)}, u32[]{:S(2)}) %all-to-all-start.2) | async-done | bytes 196640 | tf_op jit(solution)/shard_map/all_to_all | solution.py:344
  96.5 3.7 %all-to-all-start.4 = ((bf16[16,8,512]{2,1,0:T(8,128)(2,1)}), bf16[16,8,512]{2,1,0:T(8,128)(2,1)S(1)}, u32[]{:S(2)}, u32[]{:S(2)}) async-start(bf16[16,8,512]{2,1,0:T(8,128)(2,1)} %broadcast_in_dim.13), calls=%async_computation.4 | async-start | bytes 262144 | tf_op jit(solution)/shard_map/all_to_all | solution.py:344
  101.0 1.0 copy-done.5
  102.0 1.0 copy-done.7
  103.0 2.0 %shard_map.104.turned_ref = bf16[3456,256]{1,0:T(8,128)(2,1)S(1)} custom-call(s32[1]{0:T(128)} %bitcast.8.place_ref, bf16[64,3456]{1,0:T(8,128)(2,1)S(1)} %get-tuple-element.23.refs_0_, bf16[64,3456]{1,0:T(8,128)(2,1)S(1)} %collective-permute-done.refs_1_, bf16[64,3456]{1,0:T(8,128)(2,1)S(1)} %copy-done.7, bf16[64,3456]{1,0:T(8,128)(2,1)S(1)} %copy-done.5), custom_call_target="tpu_custom_call" | custom-call | bytes 3538944 | tf_op jit(solution)/shard_map/pallas_call | solution.py:279
  105.1 1.2 copy-done.2
  106.3 2.5 %fusion.14 = (bf16[768,256]{1,0:T(8,128)(2,1)}, f32[256,768]{0,1:T(8,128)}) fusion(bf16[128,768]{0,1:T(8,128)(2,1)} %copy-done.17, bf16[128,768]{0,1:T(8,128)(2,1)} %copy-done.16), kind=kLoop, calls=%fused_computation.21 | loop fusion | flops 4325376 | bytes 1572864 | tf_op jit(solution)/shard_map/transpose | solution.py:423
  108.8 1.4 %copy.20.slope = f32[256,768]{1,0:T(8,128)S(1)} copy(f32[256,768]{0,1:T(8,128)} %get-tuple-element.27) | data formatting | bytes 1572864 | tf_op jit(solution)/shard_map/add | solution.py:42
  111.0 2.4 %copy-done.1 = bf16[4864,512]{1,0:T(8,128)(2,1)S(1)} copy-done((bf16[4864,512]{1,0:T(8,128)(2,1)S(1)}, bf16[4864,512]{1,0:T(8,128)(2,1)}, u32[]{:S(2)}) %copy-start.1) | copy-done | bytes 4980760
  113.4 0.9 copy-done.12
  114.4 7.9 %shard_map.106 = bf16[4864,512]{1,0:T(8,128)(2,1)} custom-call(bf16[4864,512]{1,0:T(8,128)(2,1)S(1)} %copy-done.1, s32[4864,1]{1,0:T(8,128)S(1)} %broadcast_in_dim.15.classes_ref, s32[1,256]{1,0:T(1,128)S(1)} %broadcast_in_dim_reshape.7.marks_ref, bf16[256,512]{1,0:T(8,128)(2,1)S(1)} %copy-done.12, f32[1,256]{1,0:T(1,128)S(1)} %get-tuple-element.28.inv_total_ref), custom_call_target="tpu_custom_call" | custom-call | flops 2550136832 | bytes 9961472 | tf_op jit(solution)/shard_map/pallas_call | solution.py:235
  122.3 6.3 %shard_map.105 = (bf16[3456,768]{1,0:T(8,128)(2,1)}, bf16[768,512]{1,0:T(8,128)(2,1)}) custom-call(bf16[128,512]{1,0:T(8,128)(2,1)S(1)} %bitcast.24, bf16[128,512]{1,0:T(8,128)(2,1)S(1)} %collective-permute-done.9.grad_b, bf16[768,512]{1,0:T(8,128)(2,1)S(1)} %copy-done.9, f32[256,768]{1,0:T(8,128)S(1)} %copy.20.slope, bf16[768,256]{1,0:T(8,128)(2,1)S(1)} %copy-done.10, ...), custom_call_target="tpu_custom_call" | custom-call | flops 1358954496 | bytes 7077888 | tf_op jit(solution)/shard_map/pallas_call | solution.py:315
  (92 shorter events, 9.3 us)
Async XLA Ops:
  2.2 3.2 %collective-permute-start = (bf16[64,3456]{1,0:T(8,128)(2,1)S(1)}, bf16[64,3456]{1,0:T(8,128)(2,1)S(1)}, u32[]{:S(2)}, u32[]{:S(2)}) collective-permute-start(bf16[64,3456]{1,0:T(8,128)(2,1)S(1)} %get-tuple-element.24), channel_id=1, source_target_pairs={{0,8},{8,0},{16,24},{24,16},{1,9},{9,1},{17,25},{25,17},{2,10},{10... | collective-permute-start | bytes 1327112 | tf_op jit(solution)/shard_map/ppermute | solution.py:376
  2.7 13.1 %collective-permute-start.3 = (bf16[64,3456]{1,0:T(8,128)(2,1)S(1)}, bf16[64,3456]{1,0:T(8,128)(2,1)S(1)}, u32[]{:S(2)}, u32[]{:S(2)}) collective-permute-start(bf16[64,3456]{1,0:T(8,128)(2,1)S(1)} %get-tuple-element.25), channel_id=1, source_target_pairs={{0,24},{8,16},{16,8},{24,0},{1,25},{9,17},{17,9},{25,1},{2,26},{10... | collective-permute-start | bytes 1327112 | tf_op jit(solution)/shard_map/ppermute | solution.py:376
  5.4 20.2 %collective-permute-start.2 = (bf16[64,3456]{1,0:T(8,128)(2,1)S(1)}, bf16[64,3456]{1,0:T(8,128)(2,1)S(1)}, u32[]{:S(2)}, u32[]{:S(2)}) collective-permute-start(bf16[64,3456]{1,0:T(8,128)(2,1)S(1)} %get-tuple-element.22), channel_id=1, source_target_pairs={{0,16},{8,24},{16,0},{24,8},{1,17},{9,25},{17,1},{25,9},{2,18},{10... | collective-permute-start | bytes 1327112 | tf_op jit(solution)/shard_map/ppermute | solution.py:376
  5.4 10.5 %copy-start.15 = (bf16[3456,768]{1,0:T(8,128)(2,1)S(1)}, bf16[3456,768]{1,0:T(8,128)(2,1)}, u32[]{:S(2)}) copy-start(bf16[3456,768]{1,0:T(8,128)(2,1)} %param.8) | copy-start | bytes 15925252
  9.0 25.3 %copy-start.19 = (s32[256]{0:T(256)S(1)}, s32[256]{0:T(256)}, u32[]{:S(2)}) copy-start(s32[256]{0:T(256)} %param.12) | copy-start | bytes 3076
  9.0 8.1 %collective-permute-start.1 = (f32[64,768]{1,0:T(8,128)S(1)}, f32[64,768]{1,0:T(8,128)S(1)}, u32[]{:S(2)}, u32[]{:S(2)}) collective-permute-start(f32[64,768]{1,0:T(8,128)S(1)} %slice.47), channel_id=1, source_target_pairs={{0,8},{8,0},{1,9},{9,1},{2,10},{10,2},{3,11},{11,3},{4,12},{12,4},... | collective-permute-start | bytes 589832 | tf_op jit(solution)/shard_map/ppermute | solution.py:340
  15.9 10.6 %copy-start.4 = (bf16[64,3456]{1,0:T(8,128)(2,1)}, bf16[64,3456]{1,0:T(8,128)(2,1)S(1)}, u32[]{:S(2)}) copy-start(bf16[64,3456]{1,0:T(8,128)(2,1)S(1)} %collective-permute-done.3.refs_3_) | copy-start | bytes 1327108
  16.8 30.0 %copy-start.18 = (s32[4864]{0:T(1024)S(1)}, s32[4864]{0:T(1024)}, u32[]{:S(2)}) copy-start(s32[4864]{0:T(1024)} %param.11) | copy-start | bytes 58372
  16.8 8.8 %collective-permute-start.4 = (f32[64,768]{1,0:T(8,128)S(1)}, f32[64,768]{1,0:T(8,128)S(1)}, u32[]{:S(2)}, u32[]{:S(2)}) collective-permute-start(f32[64,768]{1,0:T(8,128)S(1)} %fusion.43), channel_id=1, source_target_pairs={{0,8},{8,0},{1,9},{9,1},{2,10},{10,2},{3,11},{11,3},{4,12},{12,4},... | collective-permute-start | bytes 589832 | tf_op jit(solution)/shard_map/ppermute | solution.py:340
  25.6 27.1 %copy-start.6 = (bf16[64,3456]{1,0:T(8,128)(2,1)}, bf16[64,3456]{1,0:T(8,128)(2,1)S(1)}, u32[]{:S(2)}) copy-start(bf16[64,3456]{1,0:T(8,128)(2,1)S(1)} %collective-permute-done.2.refs_2_) | copy-start | bytes 1327108
  26.5 37.7 %copy-start.8 = (bf16[768,512]{1,0:T(8,128)(2,1)S(1)}, bf16[768,512]{1,0:T(8,128)(2,1)}, u32[]{:S(2)}) copy-start(bf16[768,512]{1,0:T(8,128)(2,1)} %second.3) | copy-start | bytes 2359300
  27.2 15.3 %all-to-all-start = ((bf16[16,8,768]{2,1,0:T(8,128)(2,1)}), bf16[16,8,768]{2,1,0:T(8,128)(2,1)S(1)}, u32[]{:S(2)}, u32[]{:S(2)}) async-start(bf16[16,8,768]{2,1,0:T(8,128)(2,1)} %fusion.16), calls=%async_computation | async-start | bytes 393216 | tf_op jit(solution)/shard_map/all_to_all | solution.py:344
  43.2 11.8 %all-to-all-start.1 = ((bf16[16,8,768]{2,1,0:T(8,128)(2,1)}), bf16[16,8,768]{2,1,0:T(8,128)(2,1)S(1)}, u32[]{:S(2)}, u32[]{:S(2)}) async-start(bf16[16,8,768]{2,1,0:T(8,128)(2,1)} %broadcast_in_dim.10), calls=%async_computation.1 | async-start | bytes 393216 | tf_op jit(solution)/shard_map/all_to_all | solution.py:344
  46.9 2.4 %copy-start = (bf16[4864,512]{1,0:T(8,128)(2,1)S(1)}, bf16[4864,512]{1,0:T(8,128)(2,1)}, u32[]{:S(2)}) copy-start(bf16[4864,512]{1,0:T(8,128)(2,1)} %cen_ref.3) | copy-start | bytes 14942212
  52.6 2.3 %copy-start.13 = (bf16[4864,512]{1,0:T(8,128)(2,1)}, bf16[4864,512]{1,0:T(8,128)(2,1)S(1)}, u32[]{:S(2)}) copy-start(bf16[4864,512]{1,0:T(8,128)(2,1)S(1)} %get-tuple-element.12.half_hbm) | copy-start | bytes 14942212
  54.9 1.4 %collective-permute-start.8 = (bf16[128,512]{1,0:T(8,128)(2,1)S(1)}, bf16[128,512]{1,0:T(8,128)(2,1)S(1)}, u32[]{:S(2)}, u32[]{:S(2)}) collective-permute-start(bf16[128,512]{1,0:T(8,128)(2,1)S(1)} %slice.45), channel_id=1, source_target_pairs={{0,8},{8,0},{1,9},{9,1},{2,10},{10,2},{3,11},{11,3},{4,12},{12,4},... | collective-permute-start | bytes 393224 | tf_op jit(solution)/shard_map/ppermute | solution.py:340
  55.2 9.0 %copy-start.16 = (bf16[128,768]{0,1:T(8,128)(2,1)}, bf16[128,768]{0,1:T(8,128)(2,1)S(1)}, u32[]{:S(2)}) copy-start(bf16[128,768]{0,1:T(8,128)(2,1)S(1)} %copy.14) | copy-start | bytes 589828
  55.2 22.3 %copy-start.20 = (f32[2]{0:T(128)S(1)}, f32[2]{0:T(128)}, u32[]{:S(2)}) copy-start(f32[2]{0:T(128)} %constant.81) | copy-start | bytes 28
  55.2 8.8 %collective-permute-start.5 = (bf16[128,768]{0,1:T(8,128)(2,1)S(1)}, bf16[128,768]{0,1:T(8,128)(2,1)S(1)}, u32[]{:S(2)}, u32[]{:S(2)}) collective-permute-start(bf16[128,768]{0,1:T(8,128)(2,1)S(1)} %copy.14), channel_id=1, source_target_pairs={{0,8},{8,0},{1,9},{9,1},{2,10},{10,2},{3,11},{11,3},{4,12},{12,4},... | collective-permute-start | bytes 589832 | tf_op jit(solution)/shard_map/ppermute | solution.py:340
  57.0 19.4 %all-to-all-start.3 = ((bf16[16,8,512]{2,1,0:T(8,128)(2,1)}), bf16[16,8,512]{2,1,0:T(8,128)(2,1)S(1)}, u32[]{:S(2)}, u32[]{:S(2)}) async-start(bf16[16,8,512]{2,1,0:T(8,128)(2,1)} %add_bitcast_fusion), calls=%async_computation.3 | async-start | bytes 262144 | tf_op jit(solution)/shard_map/all_to_all | solution.py:344
  64.0 14.2 %copy-start.17 = (bf16[128,768]{0,1:T(8,128)(2,1)}, bf16[128,768]{0,1:T(8,128)(2,1)S(1)}, u32[]{:S(2)}) copy-start(bf16[128,768]{0,1:T(8,128)(2,1)S(1)} %collective-permute-done.5) | copy-start | bytes 589828
  64.2 2.4 %copy-start.14 = (bf16[4864,512]{1,0:T(8,128)(2,1)S(1)}, bf16[4864,512]{1,0:T(8,128)(2,1)}, u32[]{:S(2)}) copy-start(bf16[4864,512]{1,0:T(8,128)(2,1)} %copy-done.13) | copy-start | bytes 14942212
  76.4 1.2 collective-permute-start.7
  76.4 1.7 %collective-permute-start.6 = (f32[128,512]{1,0:T(8,128)S(1)}, f32[128,512]{1,0:T(8,128)S(1)}, u32[]{:S(2)}, u32[]{:S(2)}) collective-permute-start(f32[128,512]{1,0:T(8,128)S(1)} %get-tuple-element.14), channel_id=1, source_target_pairs={{0,8},{8,0},{1,9},{9,1},{2,10},{10,2},{3,11},{11,3},{4,12},{12,4},... | collective-permute-start | bytes 786440 | tf_op jit(solution)/shard_map/ppermute | solution.py:340
  78.9 15.8 %all-to-all-start.2 = ((bf16[16,8,768]{2,1,0:T(8,128)(2,1)}), bf16[16,8,768]{2,1,0:T(8,128)(2,1)S(1)}, u32[]{:S(2)}, u32[]{:S(2)}) async-start(bf16[16,8,768]{2,1,0:T(8,128)(2,1)} %pad_maximum_fusion.1), calls=%async_computation.2 | async-start | bytes 393216 | tf_op jit(solution)/shard_map/all_to_all | solution.py:344
  96.5 14.4 %all-to-all-start.4 = ((bf16[16,8,512]{2,1,0:T(8,128)(2,1)}), bf16[16,8,512]{2,1,0:T(8,128)(2,1)S(1)}, u32[]{:S(2)}, u32[]{:S(2)}) async-start(bf16[16,8,512]{2,1,0:T(8,128)(2,1)} %broadcast_in_dim.13), calls=%async_computation.4 | async-start | bytes 262144 | tf_op jit(solution)/shard_map/all_to_all | solution.py:344
  105.1 1.2 copy-start.2
  110.9 11.4 %collective-permute-start.9 = (bf16[128,512]{1,0:T(8,128)(2,1)S(1)}, bf16[128,512]{1,0:T(8,128)(2,1)S(1)}, u32[]{:S(2)}, u32[]{:S(2)}) collective-permute-start(bf16[128,512]{1,0:T(8,128)(2,1)S(1)} %bitcast.23), channel_id=1, source_target_pairs={{0,8},{8,0},{1,9},{9,1},{2,10},{10,2},{3,11},{11,3},{4,12},{12,4},... | collective-permute-start | bytes 393224 | tf_op jit(solution)/shard_map/ppermute | solution.py:340
  111.0 2.4 %copy-start.1 = (bf16[4864,512]{1,0:T(8,128)(2,1)S(1)}, bf16[4864,512]{1,0:T(8,128)(2,1)}, u32[]{:S(2)}) copy-start(bf16[4864,512]{1,0:T(8,128)(2,1)} %cen_ref.3) | copy-start | bytes 14942212
  114.4 8.0 %copy-start.3 = (bf16[3456,256]{1,0:T(8,128)(2,1)S(1)}, bf16[3456,256]{1,0:T(8,128)(2,1)}, u32[]{:S(2)}) copy-start(bf16[3456,256]{1,0:T(8,128)(2,1)} %copy-done.2) | copy-start | bytes 5308420
  114.4 8.0 %copy-start.9 = (bf16[768,512]{1,0:T(8,128)(2,1)S(1)}, bf16[768,512]{1,0:T(8,128)(2,1)}, u32[]{:S(2)}) copy-start(bf16[768,512]{1,0:T(8,128)(2,1)} %second.3) | copy-start | bytes 2359300
  114.4 8.0 %copy-start.10 = (bf16[768,256]{1,0:T(8,128)(2,1)S(1)}, bf16[768,256]{1,0:T(8,128)(2,1)}, u32[]{:S(2)}) copy-start(bf16[768,256]{1,0:T(8,128)(2,1)} %get-tuple-element.26.act) | copy-start | bytes 1179652
  (4 other events, 3.7 us)

commit v3 on v2

v3 whole, which is shorter than its diff:
```python
import functools

import jax
import jax.numpy as jnp
from jax import lax
from jax.experimental import pallas as pl
from jax.experimental.pallas import tpu as pltpu
from jax.sharding import Mesh, PartitionSpec as P

CLS_DEV = 16128


LOGIT_SCALE = 64.0
COS_MARGIN = 0.4
NORM_EPSILON = 1e-06

PIECE_SCALE = 2.0**64

F32, BF16 = jnp.float32, jnp.bfloat16
MIB = 2**20
VMEM = pl.BlockSpec(memory_space=pltpu.VMEM)
HBM = pl.BlockSpec(memory_space=pltpu.HBM)

NN = (((1,), (0,)), ((), ()))
NT = (((1,), (1,)), ((), ()))


def dot(a, b, dims=NN):
    return lax.dot_general(a, b, dims, preferred_element_type=F32)


def tile_of(extent, most, unit=16):
    return max(t for t in range(unit, most + 1, unit) if extent % t == 0)


def gelu_parts(v):
    scale = 0.7978845608028654
    cube = 0.044715
    square = v * v
    bend = jnp.tanh(scale * (v + cube * square * v))
    left = 0.5 * (1.0 + bend)
    slope = left + 0.5 * v * (1.0 - bend * bend) * scale * (1.0 + 3.0 * cube * square)
    return v * left, slope


def row_to_column(row):
    return jnp.broadcast_to(row, (8, row.shape[1])).T[:, :1]


def each(count, plain, step):
    if plain:
        for i in range(count):
            step(i)
    else:

        def run(i, carry):
            step(i)
            return carry

        lax.fori_loop(0, count, run, 0)


def rows_at(i, tile):
    return pl.ds(i * tile if isinstance(i, int) else pl.multiple_of(i * tile, tile), tile)


def params(mib):
    return pltpu.CompilerParams(vmem_limit_bytes=mib * MIB)


def cost(flops, moved):
    return pl.CostEstimate(flops=flops, bytes_accessed=moved, transcendentals=0)


def prep_kernel(plain, marks, classes, cen_hbm, half_hbm, picked, cen, half, total, in_sem, out_sem):
    steps, tile = classes.shape
    column = row_to_column(marks[...])

    def load(i):
        rows = rows_at(i, tile)
        return pltpu.make_async_copy(cen_hbm.at[rows], cen.at[rows], in_sem.at[i])

    def store(i):
        rows = rows_at(i, tile)
        return pltpu.make_async_copy(half.at[rows], half_hbm.at[rows], out_sem.at[i])

    each(steps, plain, lambda i: load(i).start())
    total[...] = jnp.zeros_like(total)

    def step(i):
        load(i).wait()
        rows = rows_at(i, tile)
        block = cen[rows, :].astype(F32)
        inv = lax.rsqrt(jnp.sum(block * block, axis=1, keepdims=True) + NORM_EPSILON)
        block = (block * inv).astype(BF16)
        half[rows, :] = block
        store(i).start()
        match = jnp.where(column == classes[pl.ds(i, 1), :], 1.0, 0.0).astype(BF16)
        total[...] += dot(match, block)

    each(steps, plain, step)
    picked[...] = total[...].astype(BF16)
    each(steps, plain, lambda i: store(i).wait())


def prep(centres, marks, classes):
    count, width = centres.shape
    images = marks.shape[1]
    steps = classes.shape[0]
    return pl.pallas_call(
        functools.partial(prep_kernel, images <= 256),
        in_specs=[VMEM, VMEM, HBM],
        out_specs=[HBM, VMEM],
        out_shape=[
            jax.ShapeDtypeStruct((count, width), BF16),
            jax.ShapeDtypeStruct((images, width), BF16),
        ],
        scratch_shapes=[
            pltpu.VMEM((count, width), BF16),
            pltpu.VMEM((count, width), BF16),
            pltpu.VMEM((images, width), F32),
            pltpu.SemaphoreType.DMA((steps,)),
            pltpu.SemaphoreType.DMA((steps,)),
        ],
        compiler_params=params(28),
        cost_estimate=cost(2 * count * width * images, 8 * count * width),
    )(marks, classes, centres)


def softmax_kernel(
    plain,
    hid_a_hbm,
    hid_b_hbm,
    second_hbm,
    marks,
    classes,
    half_hbm,
    keep,
    send,
    sums,
    unit_hbm,
    hid_a,
    hid_b,
    second,
    half,
    unit,
    weighted,
    first_sem,
    in_sem,
    out_sem,
):
    steps, tile = classes.shape
    firsts = [
        pltpu.make_async_copy(source, place, first_sem.at[i])
        for i, (source, place) in enumerate(
            ((hid_a_hbm, hid_a), (second_hbm, second), (hid_b_hbm, hid_b))
        )
    ]
    for copy in firsts:
        copy.start()

    def load(i):
        rows = rows_at(i, tile)
        return pltpu.make_async_copy(half_hbm.at[rows], half.at[rows], in_sem.at[i])

    each(steps, plain, lambda i: load(i).start())

    group = hid_a.shape[0]
    images = 2 * group
    column = row_to_column(marks[...])
    firsts[0].wait()
    firsts[1].wait()
    for place, hid in enumerate((hid_a, hid_b)):
        if place == 1:
            firsts[2].wait()
        act, _ = gelu_parts(hid[...].astype(F32))
        embedding = dot(act.astype(BF16), second[...])
        inv = lax.rsqrt(jnp.sum(embedding * embedding, axis=1, keepdims=True) + NORM_EPSILON)
        unit[pl.ds(place * group, group), :] = (embedding * inv).astype(BF16)
    store = pltpu.make_async_copy(unit, unit_hbm, out_sem)
    store.start()
    weighted[...] = jnp.zeros_like(weighted)

    def step(i, sums):
        load(i).wait()
        block = half[rows_at(i, tile), :]
        cosine = dot(unit[...], block, NT)
        positive = column == classes[pl.ds(i, 1), :]
        logits = LOGIT_SCALE * (cosine - jnp.where(positive, COS_MARGIN, 0.0))
        exp_terms = jnp.exp(logits - LOGIT_SCALE)
        weighted[...] += dot(exp_terms.astype(BF16), block)
        total = jnp.sum(exp_terms, axis=1, keepdims=True)
        target = jnp.sum(jnp.where(positive, logits, 0.0), axis=1, keepdims=True)
        return sums[0] + total, sums[1] + target

    total = target = jnp.zeros((images, 1), F32)
    if plain:
        for i in range(steps):
            total, target = step(i, (total, target))
    else:
        total, target = lax.fori_loop(0, steps, step, (total, target))
    keep[...] = weighted[:group]
    send[...] = weighted[group:]
    for i, column in enumerate((total, target)):
        sums[i : i + 1, :] = jnp.broadcast_to(column, (images, 128)).T[:1]
    store.wait()


def softmax_sums(hid_a, hid_b, second, marks, classes, half):
    count, width = half.shape
    group = hid_a.shape[0]
    images = marks.shape[1]
    steps = classes.shape[0]
    return pl.pallas_call(
        functools.partial(softmax_kernel, images <= 256),
        in_specs=[HBM] * 3 + [VMEM] * 2 + [HBM],
        out_specs=[VMEM] * 3 + [HBM],
        out_shape=[
            jax.ShapeDtypeStruct((group, width), F32),
            jax.ShapeDtypeStruct((group, width), F32),
            jax.ShapeDtypeStruct((2, images), F32),
            jax.ShapeDtypeStruct((images, width), BF16),
        ],
        scratch_shapes=[
            pltpu.VMEM(hid_a.shape, BF16),
            pltpu.VMEM(hid_b.shape, BF16),
            pltpu.VMEM(second.shape, BF16),
            pltpu.VMEM((count, width), BF16),
            pltpu.VMEM((images, width), BF16),
            pltpu.VMEM((images, width), F32),
            pltpu.SemaphoreType.DMA((3,)),
            pltpu.SemaphoreType.DMA((steps,)),
            pltpu.SemaphoreType.DMA,
        ],
        compiler_params=params(57),
        cost_estimate=cost(4 * count * width * images, 4 * count * width),
    )(hid_a, hid_b, second, marks, classes, half)


def centres_kernel(
    plain, factor, marks, classes, inv_total, unit_ref, cen_hbm, out_hbm, cen, out, in_sem, out_sem
):
    steps, tile = classes.shape
    columns = jnp.concatenate([classes[...], jnp.zeros((-steps % 8, tile), jnp.int32)]).T

    def load(i):
        rows = rows_at(i, tile)
        return pltpu.make_async_copy(cen_hbm.at[rows], cen.at[rows], in_sem.at[i])

    def store(i):
        rows = rows_at(i, tile)
        return pltpu.make_async_copy(out.at[rows], out_hbm.at[rows], out_sem.at[i])

    each(steps, True, lambda i: load(i).start())
    unit = unit_ref[...]

    def step(i):
        load(i).wait()
        rows = rows_at(i, tile)
        block = cen[rows, :].astype(F32)
        inv = lax.rsqrt(jnp.sum(block * block, axis=1, keepdims=True) + NORM_EPSILON)
        normed = block * inv
        cosine = dot(normed.astype(BF16), unit, NT)
        positive = columns[:, i : i + 1] == marks[...]
        logits = LOGIT_SCALE * (cosine - jnp.where(positive, COS_MARGIN, 0.0))
        exp_terms = jnp.exp(logits - LOGIT_SCALE)
        coeff = factor * (exp_terms * inv_total[...] - jnp.where(positive, 1.0, 0.0))
        grad = dot(coeff.astype(BF16), unit)
        grad = inv * (grad - normed * jnp.sum(grad * normed, axis=1, keepdims=True))
        out[rows, :] = grad.astype(BF16)
        store(i).start()

    each(steps, True, step)
    each(steps, True, lambda i: store(i).wait())


def grad_centres(centres, classes, marks, unit, inv_total):
    count, width = centres.shape
    images = unit.shape[0]
    steps = classes.shape[0]
    return pl.pallas_call(
        functools.partial(centres_kernel, images <= 256, LOGIT_SCALE / images),
        in_specs=[VMEM] * 4 + [HBM],
        out_specs=HBM,
        out_shape=jax.ShapeDtypeStruct((count, width), BF16),
        scratch_shapes=[
            pltpu.VMEM((count, width), BF16),
            pltpu.VMEM((count, width), BF16),
            pltpu.SemaphoreType.DMA((steps,)),
            pltpu.SemaphoreType.DMA((steps,)),
        ],
        compiler_params=params(57),
        cost_estimate=cost(4 * count * width * images, 8 * count * width),
    )(marks, classes, inv_total, unit, centres)


def turn_kernel(rows, place_ref, *refs):
    blocks, out_ref, stack = refs[:-2], refs[-2], refs[-1]
    group, depth = blocks[0].shape
    y = place_ref[0]
    for i, block in enumerate(blocks):
        dy, dc = divmod(i, 2)
        where = dc * rows + lax.rem(y - dy + rows, rows)
        stack[pl.ds(pl.multiple_of(where * group, group), group), :] = block[...]
    width = tile_of(depth, 128)

    if width == 128:

        def turn(i, carry):
            columns = pl.ds(pl.multiple_of(i * width, width), width)
            out_ref[columns, :] = stack[:, columns].T
            return carry

        lax.fori_loop(0, depth // width, turn, 0)
    else:
        out_ref[...] = stack[...].T


def turned(rows, place, blocks):
    group, depth = blocks[0].shape
    images = group * len(blocks)
    return pl.pallas_call(
        functools.partial(turn_kernel, rows),
        in_specs=[pl.BlockSpec(memory_space=pltpu.SMEM)] + [VMEM] * len(blocks),
        out_specs=VMEM,
        out_shape=jax.ShapeDtypeStruct((depth, images), BF16),
        scratch_shapes=[pltpu.VMEM((images, depth), BF16)],
        compiler_params=params(16),
        cost_estimate=cost(0, 4 * depth * images),
    )(place, *blocks)


def tail_kernel(
    grad_a,
    grad_b,
    hid_a,
    hid_b,
    second,
    turned_hbm,
    first_hbm,
    second_out,
    features,
    out,
    grad_hidden,
    in_sem,
    out_sem,
):
    group = grad_a.shape[0]
    steps = in_sem.shape[0]
    tile = out.shape[0] // steps

    def load(i):
        rows = rows_at(i, tile)
        return pltpu.make_async_copy(turned_hbm.at[rows], features.at[rows], in_sem.at[i])

    def store(i):
        rows = rows_at(i, tile)
        return pltpu.make_async_copy(out.at[rows], first_hbm.at[rows], out_sem.at[i])

    each(steps, True, lambda i: load(i).start())
    acts = []
    for place, (grad, hid) in enumerate(((grad_a, hid_a), (grad_b, hid_b))):
        act, slope = gelu_parts(hid[...].astype(F32))
        acts.append(act.astype(BF16))
        grad_act = dot(grad[...], second[...], NT)
        grad_hidden[pl.ds(place * group, group), :] = (grad_act * slope).astype(BF16)

    def step(i):
        load(i).wait()
        rows = rows_at(i, tile)
        out[rows, :] = dot(features[rows, :], grad_hidden[...]).astype(BF16)
        store(i).start()

    each(steps, True, step)
    act = jnp.concatenate(acts)
    grad = jnp.concatenate([grad_a[...], grad_b[...]])
    second_out[...] = dot(act.T, grad).astype(BF16)
    each(steps, True, lambda i: store(i).wait())


def tail(grad_a, grad_b, hid_a, hid_b, second, turned_features):
    depth, images = turned_features.shape
    hidden, width = second.shape
    steps = depth // tile_of(depth, 1200)
    return pl.pallas_call(
        tail_kernel,
        in_specs=[VMEM] * 5 + [HBM],
        out_specs=[HBM, VMEM],
        out_shape=[
            jax.ShapeDtypeStruct((depth, hidden), BF16),
            jax.ShapeDtypeStruct((hidden, width), BF16),
        ],
        scratch_shapes=[
            pltpu.VMEM((depth, images), BF16),
            pltpu.VMEM((depth, hidden), BF16),
            pltpu.VMEM((images, hidden), BF16),
            pltpu.SemaphoreType.DMA((steps,)),
            pltpu.SemaphoreType.DMA((steps,)),
        ],
        compiler_params=params(57),
        cost_estimate=cost(2 * depth * hidden * images, 2 * depth * (hidden + images)),
    )(grad_a, grad_b, hid_a, hid_b, second, turned_features)


def core_swap(x):
    return lax.ppermute(x, "core", [(0, 1), (1, 0)])


def to_chips(x):
    return lax.all_to_all(x, ("row", "gy"), 0, 0, tiled=True)


def to_all_chips(x, chips):
    x = to_chips(jnp.broadcast_to(x[None], (chips,) + x.shape))
    return x.reshape(-1, x.shape[-1])


def shards(features, first_weight, second_weight, centres, active, labels):
    rows, gy_count = lax.axis_size("row"), lax.axis_size("gy")
    y, core, gy = lax.axis_index("row"), lax.axis_index("core"), lax.axis_index("gy")
    chips = rows * gy_count
    chip = y * gy_count + gy
    device = (y * 2 + core) * gy_count + gy
    image_count = labels.shape[0]
    half = image_count // 2
    group = features.shape[0]
    own = half // chips
    depth = first_weight.shape[0]

    blocks = {}
    source = features
    for dc in (1, 0):
        for dy in list(range(1, rows)) + [0]:
            target = ((y + dy) % rows) * 2 + (core ^ dc)
            part = lax.dynamic_slice_in_dim(source, target * depth, depth, axis=1)
            if (dy, dc) == (0, 0):
                blocks[dy, dc] = part
                continue
            perm = [
                (a * 2 + b, ((a + dy) % rows) * 2 + (b ^ dc)) for a in range(rows) for b in range(2)
            ]
            blocks[dy, dc] = lax.ppermute(part, ("row", "core"), perm)

    marks = labels.reshape(rows, 2, group).transpose(1, 0, 2)
    marks = jnp.where(core == 0, marks, marks[::-1]).reshape(image_count)
    marks = marks[None, :]
    count = active.shape[0]
    tile = tile_of(count, 1280 if image_count <= 256 else 256)
    classes = (device * CLS_DEV + active).reshape(count // tile, tile)

    first_arrived, marks, classes = lax.optimization_barrier((blocks[0, 1], marks, classes))
    blocks[0, 1] = first_arrived
    normed_half, picked = prep(centres, marks, classes)
    picked = picked[:half] + core_swap(picked[half:])

    def partial_hidden(*names):
        return jnp.dot(
            jnp.concatenate([blocks[n] for n in names]), first_weight, preferred_element_type=F32
        )

    others = list(range(1, rows))
    near = partial_hidden((0, 1), (0, 0))
    far_send = partial_hidden(*[(dy, 1) for dy in others])
    near_keep = near[group:] + core_swap(near[:group])
    far_got = core_swap(far_send)
    last = [blocks[dy, 0] for dy in others]
    last, normed_half, picked = lax.optimization_barrier((last, normed_half, picked))
    for dy, block in zip(others, last):
        blocks[dy, 0] = block
    far_keep = partial_hidden(*[(dy, 0) for dy in others]) + far_got
    if rows == 2:
        part = jnp.where(
            y == 0,
            jnp.concatenate([near_keep, far_keep]),
            jnp.concatenate([far_keep, near_keep]),
        )
    else:
        part = jnp.concatenate([near_keep, far_keep]).reshape(rows, group, -1)
        part = part[(y - jnp.arange(rows)) % rows].reshape(half, -1)
    wide = part.shape[1]
    part = jnp.concatenate([part.astype(BF16), picked], axis=1)
    part = to_chips(part.reshape(chips, own, -1))
    place = jnp.reshape(y, (1,)).astype(jnp.int32)
    order = [(dy, dc) for dy in range(rows) for dc in range(2)]
    turned_features = turned(rows, place, [blocks[n] for n in order])
    part, turned_features = lax.optimization_barrier((part, turned_features))
    part = jnp.sum(part.astype(F32), axis=0)
    hidden_own, picked = part[:, :wide].astype(BF16), part[:, wide:]
    hid_a = to_all_chips(hidden_own, chips)
    hid_b = core_swap(hid_a)

    embed_own = jnp.dot(
        gelu_parts(hidden_own.astype(F32))[0].astype(BF16), second_weight, preferred_element_type=F32
    )
    inv_own = lax.rsqrt(jnp.sum(embed_own * embed_own, axis=1, keepdims=True) + NORM_EPSILON)
    unit_own = embed_own * inv_own

    weighted, weighted_send, sums, unit_half = softmax_sums(
        hid_a, hid_b, second_weight, marks, classes, normed_half
    )
    weighted = weighted + core_swap(weighted_send)
    sums = sums + jnp.roll(core_swap(sums), half, axis=1)
    sums = sums * jnp.array([[PIECE_SCALE], [1.0]], F32)
    high = lax.reduce_precision(sums, 8, 7)
    rest = sums - high
    middle = lax.reduce_precision(rest, 8, 7)
    riding = jnp.concatenate([high, middle, rest - middle, jnp.zeros_like(sums)]).astype(BF16)
    riding = riding.reshape(own, -1)
    riding = jnp.broadcast_to(riding[None], (chips,) + riding.shape)
    width = weighted.shape[1]
    sent = jnp.concatenate([weighted.astype(BF16).reshape(chips, own, width), riding], axis=2)
    sent = jnp.sum(to_chips(sent).astype(F32), axis=0)
    weighted = sent[:, :width]
    sums = sent[:, width:].reshape(4, 2, image_count).sum(axis=0)
    totals, target = sums[0:1] * (1.0 / PIECE_SCALE), sums[1:2]

    factor = LOGIT_SCALE / image_count
    totals_own = lax.dynamic_slice_in_dim(totals, chip * own, own, axis=1).reshape(own, 1)
    grad_unit = factor * (weighted / totals_own - picked)
    grad_embed = inv_own * (grad_unit - unit_own * jnp.sum(grad_unit * unit_own, axis=1, keepdims=True))
    grad_cen = grad_centres(centres, classes, marks, unit_half, 1.0 / totals)
    grad_a = to_all_chips(grad_embed.astype(BF16), chips)
    grad_a, grad_cen = lax.optimization_barrier((grad_a, grad_cen))
    grad_b = core_swap(grad_a)
    loss = jnp.mean(LOGIT_SCALE + jnp.log(totals) - target)
    grad_first, grad_second = tail(grad_a, grad_b, hid_a, hid_b, second_weight, turned_features)
    return loss, grad_first, grad_second, grad_cen


def solution(mesh):
    gx_count, gy_count = mesh.shape["gx"], mesh.shape["gy"]
    fine = Mesh(mesh.devices.reshape(gx_count // 2, 2, gy_count), ("row", "core", "gy"))
    gx = ("row", "core")
    placed = (
        P(gx, "gy"),
        P(("gy",) + gx, None),
        P(),
        P(gx + ("gy",), None),
        P(gx + ("gy",)),
        P(),
    )
    return jax.shard_map(
        shards,
        mesh=fine,
        in_specs=placed,
        out_specs=(P(), P(("gy",) + gx, None), P(), P(gx + ("gy",), None)),
        check_vma=False,
    )
```

time: 131 us -> 110 us (0.84)
  local copies, waits for them, and re-layouts: 20.4 us -> 6.24 us
  starting transfers between devices: 33 us -> 18.9 us
  blocking collectives: 0 us -> 11.2 us
  waiting for transfers between devices: 33.2 us -> 25.4 us
  Pallas kernels: 28.6 us -> 33.8 us
    all_to_all x5 -> x3, starting transfers between devices: 28.1 us -> 14.3 us  [to_chips(): return lax.all_to_all(x, ('row', 'gy'), 0, 0, tiled=True)]
    unnamed x42 -> x24, local copies, waits for them, and re-layouts: 14.4 us -> 2.84 us
    all_to_all x0 -> x1, blocking collectives: none -> 11.2 us  [to_chips(): return lax.all_to_all(x, ('row', 'gy'), 0, 0, tiled=True)]
    ppermute x3, waiting for transfers between devices: 15.1 us -> 6.36 us  [shards(): blocks[dy, dc] = lax.ppermute(part, ('row', 'core'), perm)]
    pallas_call x4, Pallas kernels: 26.6 us -> 31.8 us  [the longest x1 10.2 us: grad_centres(): pl.pallas_call(functools.partial(centres_kernel, images <= 256, LOGIT_SCA...]
    transpose x1 -> x0, other arithmetic: 2.53 us -> none  [shards(): act_turned = act.astype(BF16).T]
    add x1 -> x0, local copies, waits for them, and re-layouts: 1.39 us -> none  [gelu_parts(): left + 0.5 * v * (1.0 - bend * bend) * scale * (1.0 + 3.0 * cube * square)]
    ppermute x7, waiting for transfers between devices: 1.59 us -> 2.91 us  [core_swap(): return lax.ppermute(x, 'core', [(0, 1), (1, 0)])]
  transfers between devices with their start and end apart: 15 -> 13, of which waited for: 7 -> 6; matrix products, arithmetic and copies ran while one was open for 9% -> 7% of each run, Pallas kernels for 17% -> 17%
where the time goes in v3:
time: 110 us
  Pallas kernels  33.8 us (31%)
  waiting for transfers between devices  25.4 us (23%)
  starting transfers between devices  18.9 us (17%)
  blocking collectives  11.2 us (10%)
  local copies, waits for them, and re-layouts  6.24 us (6%)
  other arithmetic  5.63 us (5%)
  matrix products  5.63 us (5%)
  between operations  2.77 us (3%)
    all_to_all x3, waiting for transfers between devices, to_chips(): return lax.all_to_all(x, ('row', 'gy'), 0, 0, tiled=True)  16.1 us
    all_to_all x3, starting transfers between devices, to_chips(): return lax.all_to_all(x, ('row', 'gy'), 0, 0, tiled=True)  14.3 us
    all_to_all x1, blocking collectives, to_chips(): return lax.all_to_all(x, ('row', 'gy'), 0, 0, tiled=True)  11.2 us
    pallas_call x1, Pallas kernels, grad_centres(): pl.pallas_call(functools.partial(centres_kernel, images <= 256, LOGIT_SCA...  10.2 us
    pallas_call x1, Pallas kernels, softmax_sums(): pl.pallas_call(functools.partial(softmax_kernel, images <= 256), in_specs...  7.99 us
    pallas_call x1, Pallas kernels, tail(): pl.pallas_call(tail_kernel, in_specs=[VMEM] * 5 + [HBM], out_specs=[HBM,...  7.06 us
    pallas_call x1, Pallas kernels, prep(): pl.pallas_call(functools.partial(prep_kernel, images <= 256), in_specs=[V...  6.47 us
    ppermute x3, waiting for transfers between devices, shards(): blocks[dy, dc] = lax.ppermute(part, ('row', 'core'), perm)  6.36 us
  transfers between devices with their start and end apart: 13, of which 6 were waited for; matrix products, arithmetic and copies ran while one was open for 7% of the time, Pallas kernels for 17%

profile of v3, /device:TPU:0, one launch (start us, length us, event | category | flops | bytes accessed | tf_op | source)
XLA Modules:
  0.0 109.6 jit_solution(13241327933875496809)
XLA Ops:
  0.7 1.5 %constant_dynamic-slice_fusion.3 = (bf16[64,3456]{1,0:T(8,128)(2,1)S(1)}, bf16[64,3456]{1,0:T(8,128)(2,1)S(1)}, bf16[64,3456]{1,0:T(8,128)(2,1)S(1)}, bf16[64,3456]{1,0:T(8,128)(2,1)S(1)}) fusion(bf16[64,13824]{1,0:T(8,128)(2,1)} %param.7, s32[]{:T(128)S(6)} %select_n.51, s32[]{:T(128)S(6)} %select_n.48, s32[]{:T(128)S(6)} %select_n.54, s32[]{:T(128)S(6)} %select_n.53), kind=kLoop, calls=%fused_computation.50 | loop fusion | bytes 3538960 | tf_op jit(solution)/shard_map/dynamic_slice | solution.py:435
  2.2 0.5 collective-permute-start
  2.7 2.6 %collective-permute-start.4 = (bf16[64,3456]{1,0:T(8,128)(2,1)S(1)}, bf16[64,3456]{1,0:T(8,128)(2,1)S(1)}, u32[]{:S(2)}, u32[]{:S(2)}) collective-permute-start(bf16[64,3456]{1,0:T(8,128)(2,1)S(1)} %get-tuple-element.44), channel_id=1, source_target_pairs={{0,24},{8,16},{16,8},{24,0},{1,25},{9,17},{17,9},{25,1},{2,26},{10... | collective-permute-start | bytes 1327112 | tf_op jit(solution)/shard_map/ppermute | solution.py:442
  5.4 0.8 reshape.69
  6.3 0.7 broadcast_add_fusion
  7.2 3.5 %fusion = f32[128,768]{1,0:T(8,128)S(1)} fusion(bf16[3456,768]{1,0:T(8,128)(2,1)} %param.8, bf16[64,3456]{1,0:T(8,128)(2,1)S(1)} %get-tuple-element.42.refs_0_, bf16[64,3456]{1,0:T(8,128)(2,1)S(1)} %collective-permute-done.refs_1_), kind=kOutput, calls=%fused_computation.1 | convolution fusion | flops 681246720 | bytes 6586368 | tf_op jit(solution)/shard_map/dot_general | solution.py:457
  11.1 6.5 %shard_map.102 = (bf16[4864,512]{1,0:T(8,128)(2,1)S(1)}, bf16[256,512]{1,0:T(8,128)(2,1)S(1)}) custom-call(s32[1,256]{1,0:T(1,128)S(1)} %broadcast_in_dim_reshape.3.marks, s32[4,1216]{1,0:T(4,128)S(1)} %reshape.70.classes, bf16[4864,512]{1,0:T(8,128)(2,1)S(1)} %copy-done), custom_call_target="tpu_custom_call" | custom-call | flops 1275068416 | bytes 19922944 | tf_op jit(solution)/shard_map/pallas_call | solution.py:110
  17.9 0.9 fusion.31
  19.2 6.4 %collective-permute-done.2.refs_2_ = bf16[64,3456]{1,0:T(8,128)(2,1)S(1)} collective-permute-done((bf16[64,3456]{1,0:T(8,128)(2,1)S(1)}, bf16[64,3456]{1,0:T(8,128)(2,1)S(1)}, u32[]{:S(2)}, u32[]{:S(2)}) %collective-permute-start.2) | collective-permute-done | bytes 442400 | tf_op jit(solution)/shard_map/ppermute | solution.py:442
  25.6 0.9 convolution_add_fusion
  26.6 0.7 maximum_bitcast_fusion
  27.3 7.1 %all-to-all-start = ((bf16[16,8,1280]{2,1,0:T(8,128)(2,1)}), bf16[16,8,1280]{2,1,0:T(8,128)(2,1)S(1)}, u32[]{:S(2)}, u32[]{:S(2)}) async-start(bf16[16,8,1280]{2,1,0:T(8,128)(2,1)} %maximum_bitcast_fusion), calls=%async_computation | async-start | bytes 655360 | tf_op jit(solution)/shard_map/all_to_all | solution.py:410
  34.4 2.0 %shard_map.103.turned_hbm = bf16[3456,256]{1,0:T(8,128)(2,1)S(1)} custom-call(s32[1]{0:T(128)} %bitcast.2.place_ref, bf16[64,3456]{1,0:T(8,128)(2,1)S(1)} %get-tuple-element.42.refs_0_, bf16[64,3456]{1,0:T(8,128)(2,1)S(1)} %collective-permute-done.refs_1_, bf16[64,3456]{1,0:T(8,128)(2,1)S(1)} %collective-permute-done.2.refs_2_, ...), custom_call_target="tpu_custom_call" | custom-call | bytes 3538944 | tf_op jit(solution)/shard_map/pallas_call | solution.py:322
  36.4 1.2 %copy-done.1 = bf16[3456,256]{1,0:T(8,128)(2,1)} copy-done((bf16[3456,256]{1,0:T(8,128)(2,1)}, bf16[3456,256]{1,0:T(8,128)(2,1)S(1)}, u32[]{:S(2)}) %copy-start.1) | copy-done | bytes 1769496
  37.7 7.7 %all-to-all-done = bf16[16,8,1280]{2,1,0:T(8,128)(2,1)S(1)} async-done(((bf16[16,8,1280]{2,1,0:T(8,128)(2,1)}), bf16[16,8,1280]{2,1,0:T(8,128)(2,1)S(1)}, u32[]{:S(2)}, u32[]{:S(2)}) %all-to-all-start) | async-done | bytes 327712 | tf_op jit(solution)/shard_map/all_to_all | solution.py:410
  45.5 11.2 %all_to_all.20 = bf16[16,8,768]{2,1,0:T(8,128)(2,1)S(1)} all-to-all(bf16[16,8,768]{2,1,0:T(8,128)(2,1)S(1)} %broadcast_in_dim.8), channel_id=1, replica_groups=mesh['row'=2,'core'=2,'gy'=8] {'row','gy'}, dimensions={0} | all-to-all | bytes 393216 | tf_op jit(solution)/shard_map/all_to_all | solution.py:410
  56.7 1.4 %collective-permute-done.6.hid_b_hbm.hid_b = bf16[128,768]{1,0:T(8,128)(2,1)S(1)} collective-permute-done((bf16[128,768]{1,0:T(8,128)(2,1)S(1)}, bf16[128,768]{1,0:T(8,128)(2,1)S(1)}, u32[]{:S(2)}, u32[]{:S(2)}) %collective-permute-start.6) | collective-permute-done | bytes 196640 | tf_op jit(solution)/shard_map/ppermute | solution.py:406
  58.1 0.7 copy-done.10
  58.8 8.0 %shard_map.104 = (f32[128,512]{1,0:T(8,128)}, f32[128,512]{1,0:T(8,128)}, f32[2,256]{1,0:T(2,128)}, bf16[256,512]{1,0:T(8,128)(2,1)}) custom-call(bf16[128,768]{1,0:T(8,128)(2,1)} %bitcast.18, bf16[128,768]{1,0:T(8,128)(2,1)} %copy-done.10, bf16[768,512]{1,0:T(8,128)(2,1)} %second.1, s32[1,256]{1,0:T(1,128)} %copy-done.3, s32[4,1216]{1,0:T(4,128)} %copy-done.2, ...), custom_call_target="tpu_custom_call" | custom-call | flops 2550136832 | bytes 9961472 | tf_op jit(solution)/shard_map/pallas_call | solution.py:214
  67.4 0.8 collective-permute-done.8
  68.2 0.8 reduce-precision_convert_fusion.1
  69.1 1.0 fusion.5
  70.1 0.7 pad_maximum_fusion
  70.8 3.7 %all-to-all-start.2 = ((bf16[16,8,768]{2,1,0:T(8,128)(2,1)}), bf16[16,8,768]{2,1,0:T(8,128)(2,1)S(1)}, u32[]{:S(2)}, u32[]{:S(2)}) async-start(bf16[16,8,768]{2,1,0:T(8,128)(2,1)} %pad_maximum_fusion), calls=%async_computation.2 | async-start | bytes 393216 | tf_op jit(solution)/shard_map/all_to_all | solution.py:410
  74.8 8.4 %all-to-all-done.2 = bf16[16,8,768]{2,1,0:T(8,128)(2,1)S(1)} async-done(((bf16[16,8,768]{2,1,0:T(8,128)(2,1)}), bf16[16,8,768]{2,1,0:T(8,128)(2,1)S(1)}, u32[]{:S(2)}, u32[]{:S(2)}) %all-to-all-start.2) | async-done | bytes 196640 | tf_op jit(solution)/shard_map/all_to_all | solution.py:410
  83.3 1.2 %broadcast_divide_fusion = (f32[1,256]{1,0:T(1,128)}, f32[]{:T(128)}, f32[1,256]{1,0:T(1,128)S(1)}) fusion(f32[2,256]{1,0:T(2,128)S(1)} %reduce_sum.56), kind=kLoop, calls=%fused_computation.56 | loop fusion | flops 1279 | bytes 4100 | tf_op jit(solution)/shard_map/div | solution.py:521
  84.8 0.7 broadcast_in_dim.11
  85.5 3.5 %all-to-all-start.3 = ((bf16[16,8,512]{2,1,0:T(8,128)(2,1)}), bf16[16,8,512]{2,1,0:T(8,128)(2,1)S(1)}, u32[]{:S(2)}, u32[]{:S(2)}) async-start(bf16[16,8,512]{2,1,0:T(8,128)(2,1)} %broadcast_in_dim.11), calls=%async_computation.3 | async-start | bytes 262144 | tf_op jit(solution)/shard_map/all_to_all | solution.py:410
  89.0 10.2 %shard_map.105 = bf16[4864,512]{1,0:T(8,128)(2,1)} custom-call(s32[1,256]{1,0:T(1,128)} %copy-done.3, s32[4,1216]{1,0:T(4,128)} %copy-done.2, f32[1,256]{1,0:T(1,128)} %get-tuple-element.46.inv_total, bf16[256,512]{1,0:T(8,128)(2,1)} %get-tuple-element.34.unit_ref, bf16[4864,512]{1,0:T(8,128)(2,1)} %cen_hbm.3), custom_call_target="tpu_custom_call" | custom-call | flops 2550136832 | bytes 19922944 | tf_op jit(solution)/shard_map/pallas_call | solution.py:281
  100.0 0.7 collective-permute-done.9.grad_b
  100.7 0.6 copy-done.11
  101.4 7.1 %shard_map.106 = (bf16[3456,768]{1,0:T(8,128)(2,1)}, bf16[768,512]{1,0:T(8,128)(2,1)}) custom-call(bf16[128,512]{1,0:T(8,128)(2,1)} %bitcast.21, bf16[128,512]{1,0:T(8,128)(2,1)} %copy-done.11, bf16[128,768]{1,0:T(8,128)(2,1)} %bitcast.19, bf16[128,768]{1,0:T(8,128)(2,1)} %copy-done.10, bf16[768,512]{1,0:T(8,128)(2,1)} %second.1, bf16[3456,256]{1,0:T(8,128)(2,1)} %copy-done.1), custom_call_target="tpu_custom_call" | custom-call | flops 1358954496 | bytes 7077888 | tf_op jit(solution)/shard_map/pallas_call | solution.py:385
  (64 shorter events, 3.1 us)
Async XLA Ops:
  2.2 4.9 %collective-permute-start = (bf16[64,3456]{1,0:T(8,128)(2,1)S(1)}, bf16[64,3456]{1,0:T(8,128)(2,1)S(1)}, u32[]{:S(2)}, u32[]{:S(2)}) collective-permute-start(bf16[64,3456]{1,0:T(8,128)(2,1)S(1)} %get-tuple-element.43), channel_id=1, source_target_pairs={{0,8},{8,0},{16,24},{24,16},{1,9},{9,1},{17,25},{25,17},{2,10},{10... | collective-permute-start | bytes 1327112 | tf_op jit(solution)/shard_map/ppermute | solution.py:442
  2.7 15.2 %collective-permute-start.4 = (bf16[64,3456]{1,0:T(8,128)(2,1)S(1)}, bf16[64,3456]{1,0:T(8,128)(2,1)S(1)}, u32[]{:S(2)}, u32[]{:S(2)}) collective-permute-start(bf16[64,3456]{1,0:T(8,128)(2,1)S(1)} %get-tuple-element.44), channel_id=1, source_target_pairs={{0,24},{8,16},{16,8},{24,0},{1,25},{9,17},{17,9},{25,1},{2,26},{10... | collective-permute-start | bytes 1327112 | tf_op jit(solution)/shard_map/ppermute | solution.py:442
  5.4 20.2 %collective-permute-start.2 = (bf16[64,3456]{1,0:T(8,128)(2,1)S(1)}, bf16[64,3456]{1,0:T(8,128)(2,1)S(1)}, u32[]{:S(2)}, u32[]{:S(2)}) collective-permute-start(bf16[64,3456]{1,0:T(8,128)(2,1)S(1)} %get-tuple-element.45), channel_id=1, source_target_pairs={{0,16},{8,24},{16,0},{24,8},{1,17},{9,25},{17,1},{25,9},{2,18},{10... | collective-permute-start | bytes 1327112 | tf_op jit(solution)/shard_map/ppermute | solution.py:442
  6.3 11.3 %copy-start.3 = (s32[1,256]{1,0:T(1,128)}, s32[1,256]{1,0:T(1,128)S(1)}, u32[]{:S(2)}) copy-start(s32[1,256]{1,0:T(1,128)S(1)} %broadcast_in_dim_reshape.3.marks) | copy-start | bytes 3076
  7.1 10.5 %copy-start.2 = (s32[4,1216]{1,0:T(4,128)}, s32[4,1216]{1,0:T(4,128)S(1)}, u32[]{:S(2)}) copy-start(s32[4,1216]{1,0:T(4,128)S(1)} %reshape.70.classes) | copy-start | bytes 58372
  7.2 4.0 %copy-start = (bf16[4864,512]{1,0:T(8,128)(2,1)S(1)}, bf16[4864,512]{1,0:T(8,128)(2,1)}, u32[]{:S(2)}) copy-start(bf16[4864,512]{1,0:T(8,128)(2,1)} %cen_hbm.3) | copy-start | bytes 14942212
  7.2 10.8 %copy-start.5 = (bf16[3456,768]{1,0:T(8,128)(2,1)S(1)}, bf16[3456,768]{1,0:T(8,128)(2,1)}, u32[]{:S(2)}) copy-start(bf16[3456,768]{1,0:T(8,128)(2,1)} %param.8) | copy-start | bytes 15925252
  10.8 14.8 %collective-permute-start.1 = (f32[64,768]{1,0:T(8,128)S(1)}, f32[64,768]{1,0:T(8,128)S(1)}, u32[]{:S(2)}, u32[]{:S(2)}) collective-permute-start(f32[64,768]{1,0:T(8,128)S(1)} %slice.52), channel_id=1, source_target_pairs={{0,8},{8,0},{1,9},{9,1},{2,10},{10,2},{3,11},{11,3},{4,12},{12,4},... | collective-permute-start | bytes 589832 | tf_op jit(solution)/shard_map/ppermute | solution.py:406
  17.6 8.9 %copy-start.4 = (bf16[4864,512]{1,0:T(8,128)(2,1)}, bf16[4864,512]{1,0:T(8,128)(2,1)S(1)}, u32[]{:S(2)}) copy-start(bf16[4864,512]{1,0:T(8,128)(2,1)S(1)} %get-tuple-element.30.half_hbm) | copy-start | bytes 14942212
  17.7 1.5 %collective-permute-start.3 = (bf16[128,512]{1,0:T(8,128)(2,1)S(1)}, bf16[128,512]{1,0:T(8,128)(2,1)S(1)}, u32[]{:S(2)}, u32[]{:S(2)}) collective-permute-start(bf16[128,512]{1,0:T(8,128)(2,1)S(1)} %slice.42), channel_id=1, source_target_pairs={{0,8},{8,0},{1,9},{9,1},{2,10},{10,2},{3,11},{11,3},{4,12},{12,4},... | collective-permute-start | bytes 393224 | tf_op jit(solution)/shard_map/ppermute | solution.py:406
  18.8 6.8 %collective-permute-start.5 = (f32[64,768]{1,0:T(8,128)S(1)}, f32[64,768]{1,0:T(8,128)S(1)}, u32[]{:S(2)}, u32[]{:S(2)}) collective-permute-start(f32[64,768]{1,0:T(8,128)S(1)} %fusion.31), channel_id=1, source_target_pairs={{0,8},{8,0},{1,9},{9,1},{2,10},{10,2},{3,11},{11,3},{4,12},{12,4},... | collective-permute-start | bytes 589832 | tf_op jit(solution)/shard_map/ppermute | solution.py:406
  27.3 18.1 %all-to-all-start = ((bf16[16,8,1280]{2,1,0:T(8,128)(2,1)}), bf16[16,8,1280]{2,1,0:T(8,128)(2,1)S(1)}, u32[]{:S(2)}, u32[]{:S(2)}) async-start(bf16[16,8,1280]{2,1,0:T(8,128)(2,1)} %maximum_bitcast_fusion), calls=%async_computation | async-start | bytes 655360 | tf_op jit(solution)/shard_map/all_to_all | solution.py:410
  36.4 1.3 %copy-start.1 = (bf16[3456,256]{1,0:T(8,128)(2,1)}, bf16[3456,256]{1,0:T(8,128)(2,1)S(1)}, u32[]{:S(2)}) copy-start(bf16[3456,256]{1,0:T(8,128)(2,1)S(1)} %shard_map.103.turned_hbm) | copy-start | bytes 5308420
  37.7 30.5 %copy-start.9 = (f32[2]{0:T(128)S(1)}, f32[2]{0:T(128)}, u32[]{:S(2)}) copy-start(f32[2]{0:T(128)} %constant.74) | copy-start | bytes 28
  56.7 1.4 %copy-start.7 = (bf16[16,8,768]{2,1,0:T(8,128)(2,1)}, bf16[16,8,768]{2,1,0:T(8,128)(2,1)S(1)}, u32[]{:S(2)}) copy-start(bf16[16,8,768]{2,1,0:T(8,128)(2,1)S(1)} %all_to_all.20) | copy-start | bytes 589828
  56.7 17.8 %copy-start.6 = (bf16[768,512]{1,0:T(8,128)(2,1)S(1)}, bf16[768,512]{1,0:T(8,128)(2,1)}, u32[]{:S(2)}) copy-start(bf16[768,512]{1,0:T(8,128)(2,1)} %second.1) | copy-start | bytes 2359300
  56.7 1.4 %collective-permute-start.6 = (bf16[128,768]{1,0:T(8,128)(2,1)S(1)}, bf16[128,768]{1,0:T(8,128)(2,1)S(1)}, u32[]{:S(2)}, u32[]{:S(2)}) collective-permute-start(bf16[128,768]{1,0:T(8,128)(2,1)S(1)} %bitcast.17), channel_id=1, source_target_pairs={{0,8},{8,0},{1,9},{9,1},{2,10},{10,2},{3,11},{11,3},{4,12},{12,4},... | collective-permute-start | bytes 589832 | tf_op jit(solution)/shard_map/ppermute | solution.py:406
  58.1 0.7 copy-start.10
  66.8 1.4 %collective-permute-start.8 = (f32[2,256]{1,0:T(2,128)}, f32[2,256]{1,0:T(2,128)S(1)}, u32[]{:S(2)}, u32[]{:S(2)}) collective-permute-start(f32[2,256]{1,0:T(2,128)} %get-tuple-element.33), channel_id=1, source_target_pairs={{0,8},{8,0},{1,9},{9,1},{2,10},{10,2},{3,11},{11,3},{4,12},{12,4},... | collective-permute-start | bytes 6152 | tf_op jit(solution)/shard_map/ppermute | solution.py:406
  67.1 2.0 %collective-permute-start.7 = (f32[128,512]{1,0:T(8,128)}, f32[128,512]{1,0:T(8,128)S(1)}, u32[]{:S(2)}, u32[]{:S(2)}) collective-permute-start(f32[128,512]{1,0:T(8,128)} %get-tuple-element.32), channel_id=1, source_target_pairs={{0,8},{8,0},{1,9},{9,1},{2,10},{10,2},{3,11},{11,3},{4,12},{12,4},... | collective-permute-start | bytes 786440 | tf_op jit(solution)/shard_map/ppermute | solution.py:406
  70.8 12.5 %all-to-all-start.2 = ((bf16[16,8,768]{2,1,0:T(8,128)(2,1)}), bf16[16,8,768]{2,1,0:T(8,128)(2,1)S(1)}, u32[]{:S(2)}, u32[]{:S(2)}) async-start(bf16[16,8,768]{2,1,0:T(8,128)(2,1)} %pad_maximum_fusion), calls=%async_computation.2 | async-start | bytes 393216 | tf_op jit(solution)/shard_map/all_to_all | solution.py:410
  85.5 13.8 %all-to-all-start.3 = ((bf16[16,8,512]{2,1,0:T(8,128)(2,1)}), bf16[16,8,512]{2,1,0:T(8,128)(2,1)S(1)}, u32[]{:S(2)}, u32[]{:S(2)}) async-start(bf16[16,8,512]{2,1,0:T(8,128)(2,1)} %broadcast_in_dim.11), calls=%async_computation.3 | async-start | bytes 262144 | tf_op jit(solution)/shard_map/all_to_all | solution.py:410
  99.3 1.4 %copy-start.8 = (bf16[16,8,512]{2,1,0:T(8,128)(2,1)}, bf16[16,8,512]{2,1,0:T(8,128)(2,1)S(1)}, u32[]{:S(2)}) copy-start(bf16[16,8,512]{2,1,0:T(8,128)(2,1)S(1)} %all-to-all-done.3) | copy-start | bytes 393220
  99.3 1.4 %collective-permute-start.9 = (bf16[128,512]{1,0:T(8,128)(2,1)S(1)}, bf16[128,512]{1,0:T(8,128)(2,1)S(1)}, u32[]{:S(2)}, u32[]{:S(2)}) collective-permute-start(bf16[128,512]{1,0:T(8,128)(2,1)S(1)} %bitcast.20), channel_id=1, source_target_pairs={{0,8},{8,0},{1,9},{9,1},{2,10},{10,2},{3,11},{11,3},{4,12},{12,4},... | collective-permute-start | bytes 393224 | tf_op jit(solution)/shard_map/ppermute | solution.py:406
  100.7 0.6 copy-start.11

commit v4 on v3

--- a/solution.py
+++ b/solution.py
@@ -14,7 +14,13 @@
 COS_MARGIN = 0.4
 NORM_EPSILON = 1e-06
 
+POWER = LOGIT_SCALE * 1.4426950408889634
+
 PIECE_SCALE = 2.0**64
+
+SMALLEST = 1.1754944e-38
+
+AHEAD = 2
 
 F32, BF16 = jnp.float32, jnp.bfloat16
 MIB = 2**20
@@ -70,6 +76,12 @@
 
 def cost(flops, moved):
     return pl.CostEstimate(flops=flops, bytes_accessed=moved, transcendentals=0)
+
+
+def exp_terms_of(cosine, positive):
+    return jnp.exp2(
+        cosine * POWER - jnp.where(positive, POWER * (1.0 + COS_MARGIN), POWER)
+    )
 
 
 def prep_kernel(plain, marks, classes, cen_hbm, half_hbm, picked, cen, half, total, in_sem, out_sem):
@@ -112,7 +124,7 @@
         in_specs=[VMEM, VMEM, HBM],
         out_specs=[HBM, VMEM],
         out_shape=[
-            jax.ShapeDtypeStruct((count, width), BF16),
+            jax.ShapeDtypeStruct((5 * count, width), BF16),
             jax.ShapeDtypeStruct((images, width), BF16),
         ],
         scratch_shapes=[
@@ -137,8 +149,7 @@
     half_hbm,
     keep,
     send,
-    sums,
-    unit_hbm,
+    shared,
     hid_a,
     hid_b,
     second,
@@ -163,13 +174,13 @@
         rows = rows_at(i, tile)
         return pltpu.make_async_copy(half_hbm.at[rows], half.at[rows], in_sem.at[i])
 
-    each(steps, plain, lambda i: load(i).start())
-
+    load(0).start()
     group = hid_a.shape[0]
     images = 2 * group
     column = row_to_column(marks[...])
     firsts[0].wait()
     firsts[1].wait()
+    each(steps - 1, plain, lambda i: load(i + 1).start())
     for place, hid in enumerate((hid_a, hid_b)):
         if place == 1:
             firsts[2].wait()
@@ -177,7 +188,7 @@
         embedding = dot(act.astype(BF16), second[...])
         inv = lax.rsqrt(jnp.sum(embedding * embedding, axis=1, keepdims=True) + NORM_EPSILON)
         unit[pl.ds(place * group, group), :] = (embedding * inv).astype(BF16)
-    store = pltpu.make_async_copy(unit, unit_hbm, out_sem)
+    store = pltpu.make_async_copy(unit, shared.at[pl.ds(steps * tile, images)], out_sem)
     store.start()
     weighted[...] = jnp.zeros_like(weighted)
 
@@ -186,11 +197,10 @@
         block = half[rows_at(i, tile), :]
         cosine = dot(unit[...], block, NT)
         positive = column == classes[pl.ds(i, 1), :]
-        logits = LOGIT_SCALE * (cosine - jnp.where(positive, COS_MARGIN, 0.0))
-        exp_terms = jnp.exp(logits - LOGIT_SCALE)
+        exp_terms = exp_terms_of(cosine, positive)
         weighted[...] += dot(exp_terms.astype(BF16), block)
         total = jnp.sum(exp_terms, axis=1, keepdims=True)
-        target = jnp.sum(jnp.where(positive, logits, 0.0), axis=1, keepdims=True)
+        target = jnp.sum(jnp.where(positive, cosine - COS_MARGIN, 0.0), axis=1, keepdims=True)
         return sums[0] + total, sums[1] + target
 
     total = target = jnp.zeros((images, 1), F32)
@@ -199,27 +209,32 @@
             total, target = step(i, (total, target))
     else:
         total, target = lax.fori_loop(0, steps, step, (total, target))
-    keep[...] = weighted[:group]
-    send[...] = weighted[group:]
-    for i, column in enumerate((total, target)):
-        sums[i : i + 1, :] = jnp.broadcast_to(column, (images, 128)).T[:1]
+    sums = [jnp.broadcast_to(x, (images, 128)).T[:1] for x in (total, LOGIT_SCALE * target)]
+    width = keep.shape[1]
+    rows = [x[:, c : c + width] for x in sums for c in range(0, images, width)]
+    rows = [jnp.pad(x, ((0, 0), (0, width - x.shape[1]))) for x in rows]
+    rows = jnp.concatenate(rows + [jnp.zeros((8 - len(rows), width), F32)])
+    for ref, part in ((keep, weighted[:group]), (send, weighted[group:])):
+        ref[:group, :] = part
+        ref[group:, :] = rows
     store.wait()
 
 
 def softmax_sums(hid_a, hid_b, second, marks, classes, half):
-    count, width = half.shape
+    width = half.shape[1]
     group = hid_a.shape[0]
     images = marks.shape[1]
     steps = classes.shape[0]
+    count = classes.size
     return pl.pallas_call(
         functools.partial(softmax_kernel, images <= 256),
         in_specs=[HBM] * 3 + [VMEM] * 2 + [HBM],
-        out_specs=[VMEM] * 3 + [HBM],
+        out_specs=[VMEM] * 2 + [HBM],
+        input_output_aliases={5: 2},
         out_shape=[
-            jax.ShapeDtypeStruct((group, width), F32),
-            jax.ShapeDtypeStruct((group, width), F32),
-            jax.ShapeDtypeStruct((2, images), F32),
-            jax.ShapeDtypeStruct((images, width), BF16),
+            jax.ShapeDtypeStruct((group + 8, width), F32),
+            jax.ShapeDtypeStruct((group + 8, width), F32),
+            jax.ShapeDtypeStruct(half.shape, BF16),
         ],
         scratch_shapes=[
             pltpu.VMEM(hid_a.shape, BF16),
@@ -232,66 +247,158 @@
             pltpu.SemaphoreType.DMA((steps,)),
             pltpu.SemaphoreType.DMA,
         ],
-        compiler_params=params(57),
+        compiler_params=params(40),
         cost_estimate=cost(4 * count * width * images, 4 * count * width),
     )(hid_a, hid_b, second, marks, classes, half)
 
 
-def centres_kernel(
-    plain, factor, marks, classes, inv_total, unit_ref, cen_hbm, out_hbm, cen, out, in_sem, out_sem
-):
+def chunked(steps, tile, pairs, sem):
+    def copies(i):
+        rows = rows_at(i, tile)
+        return [
+            pltpu.make_async_copy(source.at[rows], target.at[rows], sem.at[p, i])
+            for p, (source, target) in enumerate(pairs)
+        ]
+
+    def start(i):
+        for copy in copies(i):
+            copy.start()
+
+    def wait(i):
+        for copy in copies(i):
+            copy.wait()
+
+    return start, wait
+
+
+def columns_of(classes):
+    pad = jnp.zeros((-classes.shape[0] % 8, classes.shape[1]), jnp.int32)
+    return jnp.concatenate([classes[...], pad]).T
+
+
+def inverse_norm(block):
+    return lax.rsqrt(jnp.sum(block * block, axis=1, keepdims=True) + NORM_EPSILON)
+
+
+def terms_kernel(marks, classes, cen_hbm, shared_hbm, out_hbm, cen, unit, out, unit_sem, in_sem, out_sem):
     steps, tile = classes.shape
-    columns = jnp.concatenate([classes[...], jnp.zeros((-steps % 8, tile), jnp.int32)]).T
-
-    def load(i):
-        rows = rows_at(i, tile)
-        return pltpu.make_async_copy(cen_hbm.at[rows], cen.at[rows], in_sem.at[i])
-
-    def store(i):
-        rows = rows_at(i, tile)
-        return pltpu.make_async_copy(out.at[rows], out_hbm.at[rows], out_sem.at[i])
-
-    each(steps, True, lambda i: load(i).start())
-    unit = unit_ref[...]
-
-    def step(i):
-        load(i).wait()
+    count = steps * tile
+    unit_copy = pltpu.make_async_copy(shared_hbm.at[pl.ds(count, unit.shape[0])], unit, unit_sem)
+    unit_copy.start()
+    load, loaded = chunked(steps, tile, [(cen_hbm, cen)], in_sem)
+    store, stored = chunked(steps, tile, [(out, out_hbm)], out_sem)
+    for i in range(min(AHEAD, steps)):
+        load(i)
+    columns = columns_of(classes)
+    unit_copy.wait()
+    for i in range(steps):
+        loaded(i)
+        if i + AHEAD < steps:
+            load(i + AHEAD)
         rows = rows_at(i, tile)
         block = cen[rows, :].astype(F32)
-        inv = lax.rsqrt(jnp.sum(block * block, axis=1, keepdims=True) + NORM_EPSILON)
-        normed = block * inv
-        cosine = dot(normed.astype(BF16), unit, NT)
+        cosine = dot((block * inverse_norm(block)).astype(BF16), unit[...], NT)
         positive = columns[:, i : i + 1] == marks[...]
-        logits = LOGIT_SCALE * (cosine - jnp.where(positive, COS_MARGIN, 0.0))
-        exp_terms = jnp.exp(logits - LOGIT_SCALE)
-        coeff = factor * (exp_terms * inv_total[...] - jnp.where(positive, 1.0, 0.0))
-        grad = dot(coeff.astype(BF16), unit)
-        grad = inv * (grad - normed * jnp.sum(grad * normed, axis=1, keepdims=True))
-        out[rows, :] = grad.astype(BF16)
-        store(i).start()
-
-    each(steps, True, step)
-    each(steps, True, lambda i: store(i).wait())
-
-
-def grad_centres(centres, classes, marks, unit, inv_total):
+        terms = exp_terms_of(cosine, positive)
+        out[rows, :] = jnp.where(positive, -jnp.maximum(terms, SMALLEST), terms)
+        store(i)
+    for i in range(steps):
+        stored(i)
+
+
+def turned_terms(centres, classes, marks, shared):
     count, width = centres.shape
-    images = unit.shape[0]
+    images = marks.shape[1]
     steps = classes.shape[0]
     return pl.pallas_call(
-        functools.partial(centres_kernel, images <= 256, LOGIT_SCALE / images),
-        in_specs=[VMEM] * 4 + [HBM],
+        terms_kernel,
+        in_specs=[VMEM] * 2 + [HBM] * 2,
+        out_specs=HBM,
+        out_shape=jax.ShapeDtypeStruct((count, images), F32),
+        scratch_shapes=[
+            pltpu.VMEM((count, width), BF16),
+            pltpu.VMEM((images, width), BF16),
+            pltpu.VMEM((count, images), F32),
+            pltpu.SemaphoreType.DMA,
+            pltpu.SemaphoreType.DMA((1, steps)),
+            pltpu.SemaphoreType.DMA((1, steps)),
+        ],
+        compiler_params=params(57),
+        cost_estimate=cost(2 * count * width * images, 8 * count * width),
+    )(marks, classes, centres, shared)
+
+
+def centres_kernel(
+    factor,
+    totals_hbm,
+    cen_hbm,
+    shared_hbm,
+    terms_hbm,
+    out_hbm,
+    totals,
+    unit,
+    cen,
+    terms,
+    out,
+    first_sem,
+    in_sem,
+    out_sem,
+):
+    steps = in_sem.shape[1]
+    count = cen.shape[0]
+    tile = count // steps
+    firsts = [
+        pltpu.make_async_copy(totals_hbm, totals, first_sem.at[0]),
+        pltpu.make_async_copy(shared_hbm.at[pl.ds(count, unit.shape[0])], unit, first_sem.at[1]),
+    ]
+    load, loaded = chunked(steps, tile, [(cen_hbm, cen), (terms_hbm, terms)], in_sem)
+    store, stored = chunked(steps, tile, [(out, out_hbm)], out_sem)
+    for copy in firsts:
+        copy.start()
+    for i in range(min(AHEAD + 1, steps)):
+        load(i)
+    for copy in firsts:
+        copy.wait()
+    share = factor / totals[...]
+    for i in range(steps):
+        loaded(i)
+        if i + AHEAD + 1 < steps:
+            load(i + AHEAD + 1)
+        rows = rows_at(i, tile)
+        block = cen[rows, :].astype(F32)
+        inv = inverse_norm(block)
+        signed = terms[rows, :]
+        coeff = jnp.abs(signed) * share - jnp.where(signed < 0.0, factor, 0.0)
+        grad = dot(coeff.astype(BF16), unit[...])
+        along = jnp.sum(grad * block, axis=1, keepdims=True) * (inv * inv)
+        out[rows, :] = (inv * (grad - block * along)).astype(BF16)
+        store(i)
+    for i in range(steps):
+        stored(i)
+
+
+def grad_centres(centres, terms, shared, totals):
+    count, width = centres.shape
+    images = terms.shape[1]
+    steps = count // tile_of(count, 640)
+    return pl.pallas_call(
+        functools.partial(centres_kernel, LOGIT_SCALE / images),
+        in_specs=[HBM] * 4,
         out_specs=HBM,
         out_shape=jax.ShapeDtypeStruct((count, width), BF16),
         scratch_shapes=[
+            pltpu.VMEM((1, images), F32),
+            pltpu.VMEM((images, width), BF16),
             pltpu.VMEM((count, width), BF16),
+            pltpu.VMEM((count, images), F32),
             pltpu.VMEM((count, width), BF16),
-            pltpu.SemaphoreType.DMA((steps,)),
-            pltpu.SemaphoreType.DMA((steps,)),
+            pltpu.SemaphoreType.DMA((2,)),
+            pltpu.SemaphoreType.DMA((2, steps)),
+            pltpu.SemaphoreType.DMA((1, steps)),
         ],
         compiler_params=params(57),
         cost_estimate=cost(4 * count * width * images, 8 * count * width),
-    )(marks, classes, inv_total, unit, centres)
+    )(totals, centres, shared, terms)
 
 
 def turn_kernel(rows, place_ref, *refs):
@@ -325,7 +432,7 @@
         out_specs=VMEM,
         out_shape=jax.ShapeDtypeStruct((depth, images), BF16),
         scratch_shapes=[pltpu.VMEM((images, depth), BF16)],
-        compiler_params=params(16),
+        compiler_params=params(57),
         cost_estimate=cost(0, 4 * depth * images),
     )(place, *blocks)
 
@@ -397,9 +504,47 @@
             pltpu.SemaphoreType.DMA((steps,)),
             pltpu.SemaphoreType.DMA((steps,)),
         ],
-        compiler_params=params(57),
+        compiler_params=params(40),
         cost_estimate=cost(2 * depth * hidden * images, 2 * depth * (hidden + images)),
     )(grad_a, grad_b, hid_a, hid_b, second, turned_features)
+
+
+def assemble_kernel(images, keep, got, out):
+    width = keep.shape[1]
+    half = keep.shape[0] - 8
+    each = -(-images // width)
+
+    def sums(ref):
+        lines = [
+            jnp.concatenate([ref[half + each * q + r : half + each * q + r + 1, :] for r in range(each)], axis=1)
+            for q in range(2)
+        ]
+        return jnp.concatenate(lines)[:, :images]
+
+    other = sums(got)
+    both = sums(keep) + jnp.concatenate([other[:, images // 2 :], other[:, : images // 2]], axis=1)
+    scale = jnp.where(lax.broadcasted_iota(jnp.int32, both.shape, 0) == 0, PIECE_SCALE, 1.0)
+    both = both * scale
+    parts = []
+    for _ in range(3):
+        part = both.astype(BF16).astype(F32)
+        parts.append(part)
+        both = both - part
+    riding = jnp.concatenate(parts + [jnp.zeros_like(both)])
+    out[:, :width] = (keep[:half, :] + got[:half, :]).astype(BF16)
+    out[:, width:] = jnp.concatenate([riding] * (half // 8)).astype(BF16)
+
+
+def assemble(images, keep, got):
+    half, width = keep.shape[0] - 8, keep.shape[1]
+    return pl.pallas_call(
+        functools.partial(assemble_kernel, images),
+        in_specs=[VMEM] * 2,
+        out_specs=VMEM,
+        out_shape=jax.ShapeDtypeStruct((half, width + images), BF16),
+        compiler_params=params(16),
+        cost_estimate=cost(0, 8 * half * (width + images)),
+    )(keep, got)
 
 
 def core_swap(x):
@@ -428,18 +573,18 @@
     depth = first_weight.shape[0]
 
     blocks = {}
-    source = features
-    for dc in (1, 0):
-        for dy in list(range(1, rows)) + [0]:
-            target = ((y + dy) % rows) * 2 + (core ^ dc)
-            part = lax.dynamic_slice_in_dim(source, target * depth, depth, axis=1)
-            if (dy, dc) == (0, 0):
-                blocks[dy, dc] = part
-                continue
-            perm = [
-                (a * 2 + b, ((a + dy) % rows) * 2 + (b ^ dc)) for a in range(rows) for b in range(2)
-            ]
-            blocks[dy, dc] = lax.ppermute(part, ("row", "core"), perm)
+    others = list(range(1, rows))
+    for dy, dc in [(dy, 1) for dy in others] + [(0, 1)] + [(dy, 0) for dy in others] + [(0, 0)]:
+        target = ((y + dy) % rows) * 2 + (core ^ dc)
+        if (dy, dc) == (0, 0):
+            source, labels = lax.optimization_barrier((features, labels))
+            blocks[dy, dc] = lax.dynamic_slice_in_dim(source, target * depth, depth, axis=1)
+            continue
+        part = lax.dynamic_slice_in_dim(features, target * depth, depth, axis=1)
+        perm = [
+            (a * 2 + b, ((a + dy) % rows) * 2 + (b ^ dc)) for a in range(rows) for b in range(2)
+        ]
+        blocks[dy, dc] = lax.ppermute(part, ("row", "core"), perm)
 
     marks = labels.reshape(rows, 2, group).transpose(1, 0, 2)
     marks = jnp.where(core == 0, marks, marks[::-1]).reshape(image_count)
@@ -458,13 +603,16 @@
             jnp.concatenate([blocks[n] for n in names]), first_weight, preferred_element_type=F32
         )
 
-    others = list(range(1, rows))
     near = partial_hidden((0, 1), (0, 0))
+    early = [blocks[dy, 1] for dy in others]
+    early, near, normed_half, picked = lax.optimization_barrier((early, near, normed_half, picked))
+    for dy, block in zip(others, early):
+        blocks[dy, 1] = block
     far_send = partial_hidden(*[(dy, 1) for dy in others])
     near_keep = near[group:] + core_swap(near[:group])
     far_got = core_swap(far_send)
     last = [blocks[dy, 0] for dy in others]
-    last, normed_half, picked = lax.optimization_barrier((last, normed_half, picked))
+    last, far_got, near_keep, picked = lax.optimization_barrier((last, far_got, near_keep, picked))
     for dy, block in zip(others, last):
         blocks[dy, 0] = block
     far_keep = partial_hidden(*[(dy, 0) for dy in others]) + far_got
@@ -495,21 +643,15 @@
     inv_own = lax.rsqrt(jnp.sum(embed_own * embed_own, axis=1, keepdims=True) + NORM_EPSILON)
     unit_own = embed_own * inv_own
 
-    weighted, weighted_send, sums, unit_half = softmax_sums(
+    weighted, weighted_send, shared = softmax_sums(
         hid_a, hid_b, second_weight, marks, classes, normed_half
     )
-    weighted = weighted + core_swap(weighted_send)
-    sums = sums + jnp.roll(core_swap(sums), half, axis=1)
-    sums = sums * jnp.array([[PIECE_SCALE], [1.0]], F32)
-    high = lax.reduce_precision(sums, 8, 7)
-    rest = sums - high
-    middle = lax.reduce_precision(rest, 8, 7)
-    riding = jnp.concatenate([high, middle, rest - middle, jnp.zeros_like(sums)]).astype(BF16)
-    riding = riding.reshape(own, -1)
-    riding = jnp.broadcast_to(riding[None], (chips,) + riding.shape)
     width = weighted.shape[1]
-    sent = jnp.concatenate([weighted.astype(BF16).reshape(chips, own, width), riding], axis=2)
-    sent = jnp.sum(to_chips(sent).astype(F32), axis=0)
+    sent = assemble(image_count, weighted, core_swap(weighted_send))
+    sent, shared = lax.optimization_barrier((sent, shared))
+    terms = turned_terms(centres, classes, marks, shared)
+    sent, terms = lax.optimization_barrier((to_chips(sent.reshape(chips, own, -1)), terms))
+    sent = jnp.sum(sent.astype(F32), axis=0)
     weighted = sent[:, :width]
     sums = sent[:, width:].reshape(4, 2, image_count).sum(axis=0)
     totals, target = sums[0:1] * (1.0 / PIECE_SCALE), sums[1:2]
@@ -518,8 +660,11 @@
     totals_own = lax.dynamic_slice_in_dim(totals, chip * own, own, axis=1).reshape(own, 1)
     grad_unit = factor * (weighted / totals_own - picked)
     grad_embed = inv_own * (grad_unit - unit_own * jnp.sum(grad_unit * unit_own, axis=1, keepdims=True))
-    grad_cen = grad_centres(centres, classes, marks, unit_half, 1.0 / totals)
-    grad_a = to_all_chips(grad_embed.astype(BF16), chips)
+    grad_embed = grad_embed.astype(BF16)
+    grad_embed = jnp.broadcast_to(grad_embed[None], (chips,) + grad_embed.shape)
+    grad_embed, totals, target = lax.optimization_barrier((grad_embed, totals, target))
+    grad_cen = grad_centres(centres, terms, shared, totals)
+    grad_a = to_chips(grad_embed).reshape(half, -1)
     grad_a, grad_cen = lax.optimization_barrier((grad_a, grad_cen))
     grad_b = core_swap(grad_a)
     loss = jnp.mean(LOGIT_SCALE + jnp.log(totals) - target)

time: 110 us -> 103 us (0.936)
  waiting for transfers between devices: 25.4 us -> 15.1 us
  Pallas kernels: 33.8 us -> 36.4 us
  other arithmetic: 5.63 us -> 3.2 us
  local copies, waits for them, and re-layouts: 6.24 us -> 7.58 us
  starting transfers between devices: 18.9 us -> 20.1 us
    all_to_all x3, waiting for transfers between devices: 16.1 us -> 7.66 us  [to_chips(): return lax.all_to_all(x, ('row', 'gy'), 0, 0, tiled=True)]
    pallas_call x1 -> x3, Pallas kernels: 10.2 us -> 15.5 us  [the longest x1 7.81 us: grad_centres(): pl.pallas_call(functools.partial(centres_kernel, LOGIT_SCALE / images), i...]
    pallas_call x1, Pallas kernels: 2.04 us -> 4.73 us  [turned(): pl.pallas_call(functools.partial(turn_kernel, rows), in_specs=[pl.BlockSp...]
    pallas_call x1, Pallas kernels: 7.99 us -> 5.63 us  [softmax_sums(): pl.pallas_call(functools.partial(softmax_kernel, images <= 256), in_specs...]
    ppermute x3, waiting for transfers between devices: 6.36 us -> 4.57 us  [shards(): blocks[dy, dc] = lax.ppermute(part, ('row', 'core'), perm)]
    all_to_all x3, starting transfers between devices: 14.3 us -> 15.9 us  [to_chips(): return lax.all_to_all(x, ('row', 'gy'), 0, 0, tiled=True)]
    dynamic_slice x1 -> x2, local copies, waits for them, and re-layouts: 1.55 us -> 3.19 us  [the longest x1 2.14 us: shards(): part = lax.dynamic_slice_in_dim(features, target * depth, depth, axis=1)]
    pallas_call x1, Pallas kernels: 6.47 us -> 4.9 us  [prep(): pl.pallas_call(functools.partial(prep_kernel, images <= 256), in_specs=[V...]
  transfers between devices with their start and end apart: 13 -> 12, of which waited for: 6 -> 5; matrix products, arithmetic and copies ran while one was open for 7% -> 9% of each run, Pallas kernels for 17% -> 24%
where the time goes in v4:
time: 103 us; the launch traced here: 102 us
  Pallas kernels  36.4 us (35%)
  starting transfers between devices  20.1 us (20%)
  waiting for transfers between devices  15.1 us (15%)
  blocking collectives  11.2 us (11%)
  local copies, waits for them, and re-layouts  7.58 us (7%)
  matrix products  5.54 us (5%)
  other arithmetic  3.2 us (3%)
  between operations  2.79 us (3%)
    all_to_all x3, starting transfers between devices, to_chips(): return lax.all_to_all(x, ('row', 'gy'), 0, 0, tiled=True)  15.9 us
    all_to_all x1, blocking collectives, to_chips(): return lax.all_to_all(x, ('row', 'gy'), 0, 0, tiled=True)  11.2 us
    pallas_call x1, Pallas kernels, grad_centres(): pl.pallas_call(functools.partial(centres_kernel, LOGIT_SCALE / images), i...  7.81 us
    all_to_all x3, waiting for transfers between devices, to_chips(): return lax.all_to_all(x, ('row', 'gy'), 0, 0, tiled=True)  7.66 us
    pallas_call x1, Pallas kernels, turned_terms(): pl.pallas_call(terms_kernel, in_specs=[VMEM] * 2 + [HBM] * 2, out_specs=H...  6.94 us
    pallas_call x1, Pallas kernels, tail(): pl.pallas_call(tail_kernel, in_specs=[VMEM] * 5 + [HBM], out_specs=[HBM,...  5.69 us
    pallas_call x1, Pallas kernels, softmax_sums(): pl.pallas_call(functools.partial(softmax_kernel, images <= 256), in_specs...  5.63 us
    dot_general x3, matrix products, partial_hidden(): jnp.dot(jnp.concatenate([blocks[n] for n in names]), first_weight, prefer...  5.22 us
  transfers between devices with their start and end apart: 12, of which 5 were waited for; matrix products, arithmetic and copies ran while one was open for 9% of the time, Pallas kernels for 24%

profile of v4, /device:TPU:0, one launch (start us, length us, event | category | flops | bytes accessed | tf_op | source)
XLA Modules:
  0.0 101.9 jit_solution(32989281616179473)
XLA Ops:
  0.7 2.1 %constant_dynamic-slice_fusion.2 = (bf16[64,3456]{1,0:T(8,128)(2,1)}, bf16[64,3456]{1,0:T(8,128)(2,1)S(1)}, bf16[64,3456]{1,0:T(8,128)(2,1)S(1)}) fusion(bf16[64,13824]{1,0:T(8,128)(2,1)} %param.6, s32[]{:T(128)S(6)} %select_n.51, s32[]{:T(128)S(6)} %select_n.49, s32[]{:T(128)S(6)} %select_n.48), kind=kLoop, calls=%fused_computation.38 | loop fusion | bytes 2654220 | tf_op jit(solution)/shard_map/dynamic_slice | solution.py:583
  2.8 0.5 collective-permute-start.2
  3.3 2.6 %collective-permute-start.1 = (bf16[64,3456]{1,0:T(8,128)(2,1)S(1)}, bf16[64,3456]{1,0:T(8,128)(2,1)S(1)}, u32[]{:S(2)}, u32[]{:S(2)}) collective-permute-start(bf16[64,3456]{1,0:T(8,128)(2,1)S(1)} %get-tuple-element.67), channel_id=1, source_target_pairs={{0,24},{8,16},{16,8},{24,0},{1,25},{9,17},{17,9},{25,1},{2,26},{10... | collective-permute-start | bytes 1327112 | tf_op jit(solution)/shard_map/ppermute | solution.py:587
  5.9 0.7 broadcast_add_fusion
  6.7 0.8 reshape.43
  7.6 1.0 %constant_dynamic-slice_fusion.1.refs_0_ = bf16[64,3456]{1,0:T(8,128)(2,1)S(1)} fusion(bf16[64,13824]{1,0:T(8,128)(2,1)} %param.6, s32[]{:T(128)S(6)} %select_n.54), kind=kLoop, calls=%fused_computation.37 | loop fusion | bytes 884740 | tf_op jit(solution)/shard_map/dynamic_slice | solution.py:581
  8.7 2.6 %copy-done = bf16[4864,512]{1,0:T(8,128)(2,1)S(1)} copy-done((bf16[4864,512]{1,0:T(8,128)(2,1)S(1)}, bf16[4864,512]{1,0:T(8,128)(2,1)}, u32[]{:S(2)}) %copy-start) | copy-done | bytes 4980760
  11.3 4.9 %shard_map.93 = (bf16[24320,512]{1,0:T(8,128)(2,1)}, bf16[256,512]{1,0:T(8,128)(2,1)S(1)}) custom-call(s32[1,256]{1,0:T(1,128)S(1)} %broadcast_in_dim_reshape.3.marks, s32[4,1216]{1,0:T(4,128)S(1)} %reshape.44.classes, bf16[4864,512]{1,0:T(8,128)(2,1)S(1)} %copy-done), custom_call_target="tpu_custom_call" | custom-call | flops 1275068416 | bytes 19922944 | tf_op jit(solution)/shard_map/pallas_call | solution.py:122
  16.4 3.4 %fusion = f32[128,768]{1,0:T(8,128)S(1)} fusion(bf16[3456,768]{1,0:T(8,128)(2,1)} %param.7, bf16[64,3456]{1,0:T(8,128)(2,1)S(1)} %constant_dynamic-slice_fusion.1.refs_0_, bf16[64,3456]{1,0:T(8,128)(2,1)S(1)} %collective-permute-done.2.refs_1_), kind=kOutput, calls=%fused_computation.1 | convolution fusion | flops 681246720 | bytes 6586368 | tf_op jit(solution)/shard_map/dot_general | solution.py:602
  20.0 0.4 collective-permute-start.5
  20.4 0.9 fusion.26
  21.3 0.2 collective-permute-start.4
  21.5 4.6 %collective-permute-done.refs_2_ = bf16[64,3456]{1,0:T(8,128)(2,1)S(1)} collective-permute-done((bf16[64,3456]{1,0:T(8,128)(2,1)S(1)}, bf16[64,3456]{1,0:T(8,128)(2,1)S(1)}, u32[]{:S(2)}, u32[]{:S(2)}) %collective-permute-start) | collective-permute-done | bytes 442400 | tf_op jit(solution)/shard_map/ppermute | solution.py:587
  26.1 0.9 convolution_add_fusion
  27.1 0.8 maximum_bitcast_fusion
  27.8 7.0 %all-to-all-start = ((bf16[16,8,1280]{2,1,0:T(8,128)(2,1)}), bf16[16,8,1280]{2,1,0:T(8,128)(2,1)S(1)}, u32[]{:S(2)}, u32[]{:S(2)}) async-start(bf16[16,8,1280]{2,1,0:T(8,128)(2,1)} %maximum_bitcast_fusion), calls=%async_computation | async-start | bytes 655360 | tf_op jit(solution)/shard_map/all_to_all | solution.py:555
  34.8 4.7 %shard_map.94.turned_hbm = bf16[3456,256]{1,0:T(8,128)(2,1)} custom-call(s32[1]{0:T(128)} %bitcast.2.place_ref, bf16[64,3456]{1,0:T(8,128)(2,1)} %copy-done.6, bf16[64,3456]{1,0:T(8,128)(2,1)} %copy-done.7, bf16[64,3456]{1,0:T(8,128)(2,1)} %copy-done.9, bf16[64,3456]{1,0:T(8,128)(2,1)} %copy-done.8), custom_call_target="tpu_custom_call" | custom-call | bytes 3538944 | tf_op jit(solution)/shard_map/pallas_call | solution.py:429
  39.5 6.2 %all-to-all-done = bf16[16,8,1280]{2,1,0:T(8,128)(2,1)S(1)} async-done(((bf16[16,8,1280]{2,1,0:T(8,128)(2,1)}), bf16[16,8,1280]{2,1,0:T(8,128)(2,1)S(1)}, u32[]{:S(2)}, u32[]{:S(2)}) %all-to-all-start) | async-done | bytes 327712 | tf_op jit(solution)/shard_map/all_to_all | solution.py:555
  45.8 11.2 %all_to_all.20 = bf16[16,8,768]{2,1,0:T(8,128)(2,1)S(1)} all-to-all(bf16[16,8,768]{2,1,0:T(8,128)(2,1)S(1)} %broadcast_in_dim.4), channel_id=1, replica_groups=mesh['row'=2,'core'=2,'gy'=8] {'row','gy'}, dimensions={0} | all-to-all | bytes 393216 | tf_op jit(solution)/shard_map/all_to_all | solution.py:555
  57.0 1.4 %collective-permute-done.6.hid_b_hbm.hid_b = bf16[128,768]{1,0:T(8,128)(2,1)S(1)} collective-permute-done((bf16[128,768]{1,0:T(8,128)(2,1)S(1)}, bf16[128,768]{1,0:T(8,128)(2,1)S(1)}, u32[]{:S(2)}, u32[]{:S(2)}) %collective-permute-start.6) | collective-permute-done | bytes 196640 | tf_op jit(solution)/shard_map/ppermute | solution.py:551
  58.4 5.6 %shard_map.95 = (f32[136,512]{1,0:T(8,128)S(1)}, f32[136,512]{1,0:T(8,128)S(1)}, bf16[24320,512]{1,0:T(8,128)(2,1)}) custom-call(bf16[128,768]{1,0:T(8,128)(2,1)S(1)} %bitcast.17, bf16[128,768]{1,0:T(8,128)(2,1)S(1)} %collective-permute-done.6.hid_b_hbm.hid_b, bf16[768,512]{1,0:T(8,128)(2,1)S(1)} %copy-done.1, ...), custom_call_target="tpu_custom_call", output_to_operand_aliasing={{2}: (5, {})} | custom-call | flops 2550136832 | bytes 9961472 | tf_op jit(solution)/shard_map/pallas_call | solution.py:229
  64.3 1.4 %collective-permute-done.7.got = f32[136,512]{1,0:T(8,128)S(1)} collective-permute-done((f32[136,512]{1,0:T(8,128)S(1)}, f32[136,512]{1,0:T(8,128)S(1)}, u32[]{:S(2)}, u32[]{:S(2)}) %collective-permute-start.7) | collective-permute-done | bytes 278560 | tf_op jit(solution)/shard_map/ppermute | solution.py:551
  65.7 0.7 shard_map.96
  66.4 3.7 %all-to-all-start.2 = ((bf16[16,8,768]{2,1,0:T(8,128)(2,1)}), bf16[16,8,768]{2,1,0:T(8,128)(2,1)S(1)}, u32[]{:S(2)}, u32[]{:S(2)}) async-start(bf16[16,8,768]{2,1,0:T(8,128)(2,1)} %bitcast.4), calls=%async_computation.2 | async-start | bytes 393216 | tf_op jit(solution)/shard_map/all_to_all | solution.py:555
  70.1 0.3 multiply_reduce_fusion.1
  70.5 6.9 %shard_map.97.terms_hbm = f32[4864,256]{1,0:T(8,128)} custom-call(s32[1,256]{1,0:T(1,128)} %copy-done.4, s32[4,1216]{1,0:T(4,128)} %copy-done.3, bf16[4864,512]{1,0:T(8,128)(2,1)} %cen_hbm.5, bf16[24320,512]{1,0:T(8,128)(2,1)} %get-tuple-element.55.shared_hbm), custom_call_target="tpu_custom_call" | custom-call | flops 1275068416 | bytes 19922944 | tf_op jit(solution)/shard_map/pallas_call | solution.py:313
  77.4 1.4 %all-to-all-done.2 = bf16[16,8,768]{2,1,0:T(8,128)(2,1)S(1)} async-done(((bf16[16,8,768]{2,1,0:T(8,128)(2,1)}), bf16[16,8,768]{2,1,0:T(8,128)(2,1)S(1)}, u32[]{:S(2)}, u32[]{:S(2)}) %all-to-all-start.2) | async-done | bytes 196640 | tf_op jit(solution)/shard_map/all_to_all | solution.py:555
  79.3 0.7 broadcast_in_dim.5
  80.0 5.3 %all-to-all-start.3 = ((bf16[16,8,512]{2,1,0:T(8,128)(2,1)}), bf16[16,8,512]{2,1,0:T(8,128)(2,1)S(1)}, u32[]{:S(2)}, u32[]{:S(2)}) async-start(bf16[16,8,512]{2,1,0:T(8,128)(2,1)} %broadcast_in_dim.5), calls=%async_computation.3 | async-start | bytes 262144 | tf_op jit(solution)/shard_map/all_to_all | solution.py:555
  85.3 7.8 %shard_map.98 = bf16[4864,512]{1,0:T(8,128)(2,1)} custom-call(f32[1,256]{1,0:T(1,128)} %copy-done.10, bf16[4864,512]{1,0:T(8,128)(2,1)} %cen_hbm.5, bf16[24320,512]{1,0:T(8,128)(2,1)} %get-tuple-element.55.shared_hbm, f32[4864,256]{1,0:T(8,128)} %shard_map.97.terms_hbm), custom_call_target="tpu_custom_call" | custom-call | flops 2550136832 | bytes 19922944 | tf_op jit(solution)/shard_map/pallas_call | solution.py:384
  93.2 1.2 %subtract_reduce_fusion = f32[]{:T(128)} fusion(f32[1,256]{1,0:T(1,128)S(1)} %get-tuple-element.58, f32[1,256]{1,0:T(1,128)} %copy-done.10), kind=kLoop, calls=%fused_computation.42 | loop fusion | flops 767 | bytes 2052 | tf_op jit(solution)/shard_map/reduce_sum | solution.py:670
  95.1 5.7 %shard_map.99 = (bf16[3456,768]{1,0:T(8,128)(2,1)}, bf16[768,512]{1,0:T(8,128)(2,1)}) custom-call(bf16[128,512]{1,0:T(8,128)(2,1)S(1)} %bitcast.20, bf16[128,512]{1,0:T(8,128)(2,1)S(1)} %collective-permute-done.8.grad_b, bf16[128,768]{1,0:T(8,128)(2,1)S(1)} %bitcast.18, bf16[128,768]{1,0:T(8,128)(2,1)S(1)} %collective-permute-done.6.hid_b_hbm.hid_b, ...), custom_call_target="tpu_custom_call" | custom-call | flops 1358954496 | bytes 7077888 | tf_op jit(solution)/shard_map/pallas_call | solution.py:492
  (55 shorter events, 1.4 us)
Async XLA Ops:
  2.8 5.9 %collective-permute-start.2 = (bf16[64,3456]{1,0:T(8,128)(2,1)}, bf16[64,3456]{1,0:T(8,128)(2,1)S(1)}, u32[]{:S(2)}, u32[]{:S(2)}) collective-permute-start(bf16[64,3456]{1,0:T(8,128)(2,1)} %get-tuple-element.66), channel_id=1, source_target_pairs={{0,8},{8,0},{16,24},{24,16},{1,9},{9,1},{17,25},{25,17},{2,10},{10... | collective-permute-start | bytes 1327112 | tf_op jit(solution)/shard_map/ppermute | solution.py:587
  3.3 16.7 %collective-permute-start.1 = (bf16[64,3456]{1,0:T(8,128)(2,1)S(1)}, bf16[64,3456]{1,0:T(8,128)(2,1)S(1)}, u32[]{:S(2)}, u32[]{:S(2)}) collective-permute-start(bf16[64,3456]{1,0:T(8,128)(2,1)S(1)} %get-tuple-element.67), channel_id=1, source_target_pairs={{0,24},{8,16},{16,8},{24,0},{1,25},{9,17},{17,9},{25,1},{2,26},{10... | collective-permute-start | bytes 1327112 | tf_op jit(solution)/shard_map/ppermute | solution.py:587
  5.9 20.2 %collective-permute-start = (bf16[64,3456]{1,0:T(8,128)(2,1)S(1)}, bf16[64,3456]{1,0:T(8,128)(2,1)S(1)}, u32[]{:S(2)}, u32[]{:S(2)}) collective-permute-start(bf16[64,3456]{1,0:T(8,128)(2,1)S(1)} %get-tuple-element.68), channel_id=1, source_target_pairs={{0,16},{8,24},{16,0},{24,8},{1,17},{9,25},{17,1},{25,9},{2,18},{10... | collective-permute-start | bytes 1327112 | tf_op jit(solution)/shard_map/ppermute | solution.py:587
  6.7 51.7 %copy-start.3 = (s32[4,1216]{1,0:T(4,128)}, s32[4,1216]{1,0:T(4,128)S(1)}, u32[]{:S(2)}) copy-start(s32[4,1216]{1,0:T(4,128)S(1)} %reshape.44.classes) | copy-start | bytes 58372
  7.6 50.8 %copy-start.4 = (s32[1,256]{1,0:T(1,128)}, s32[1,256]{1,0:T(1,128)S(1)}, u32[]{:S(2)}) copy-start(s32[1,256]{1,0:T(1,128)S(1)} %broadcast_in_dim_reshape.3.marks) | copy-start | bytes 3076
  8.7 11.2 %copy-start.6 = (bf16[64,3456]{1,0:T(8,128)(2,1)}, bf16[64,3456]{1,0:T(8,128)(2,1)S(1)}, u32[]{:S(2)}) copy-start(bf16[64,3456]{1,0:T(8,128)(2,1)S(1)} %constant_dynamic-slice_fusion.1.refs_0_) | copy-start | bytes 1327108
  8.7 2.6 %copy-start = (bf16[4864,512]{1,0:T(8,128)(2,1)S(1)}, bf16[4864,512]{1,0:T(8,128)(2,1)}, u32[]{:S(2)}) copy-start(bf16[4864,512]{1,0:T(8,128)(2,1)} %cen_hbm.5) | copy-start | bytes 14942212
  11.3 8.6 %copy-start.7 = (bf16[64,3456]{1,0:T(8,128)(2,1)}, bf16[64,3456]{1,0:T(8,128)(2,1)S(1)}, u32[]{:S(2)}) copy-start(bf16[64,3456]{1,0:T(8,128)(2,1)S(1)} %collective-permute-done.2.refs_1_) | copy-start | bytes 1327108
  11.3 9.1 %copy-start.5 = (bf16[3456,768]{1,0:T(8,128)(2,1)S(1)}, bf16[3456,768]{1,0:T(8,128)(2,1)}, u32[]{:S(2)}) copy-start(bf16[3456,768]{1,0:T(8,128)(2,1)} %param.7) | copy-start | bytes 15925252
  16.2 3.7 %collective-permute-start.3 = (bf16[128,512]{1,0:T(8,128)(2,1)S(1)}, bf16[128,512]{1,0:T(8,128)(2,1)S(1)}, u32[]{:S(2)}, u32[]{:S(2)}) collective-permute-start(bf16[128,512]{1,0:T(8,128)(2,1)S(1)} %slice.32), channel_id=1, source_target_pairs={{0,8},{8,0},{1,9},{9,1},{2,10},{10,2},{3,11},{11,3},{4,12},{12,4},... | collective-permute-start | bytes 393224 | tf_op jit(solution)/shard_map/ppermute | solution.py:551
  19.9 7.1 %copy-start.8 = (bf16[64,3456]{1,0:T(8,128)(2,1)}, bf16[64,3456]{1,0:T(8,128)(2,1)S(1)}, u32[]{:S(2)}) copy-start(bf16[64,3456]{1,0:T(8,128)(2,1)S(1)} %collective-permute-done.1.refs_3_) | copy-start | bytes 1327108
  20.0 1.5 %collective-permute-start.5 = (f32[64,768]{1,0:T(8,128)S(1)}, f32[64,768]{1,0:T(8,128)S(1)}, u32[]{:S(2)}, u32[]{:S(2)}) collective-permute-start(f32[64,768]{1,0:T(8,128)S(1)} %slice.34), channel_id=1, source_target_pairs={{0,8},{8,0},{1,9},{9,1},{2,10},{10,2},{3,11},{11,3},{4,12},{12,4},... | collective-permute-start | bytes 589832 | tf_op jit(solution)/shard_map/ppermute | solution.py:551
  21.3 4.8 %collective-permute-start.4 = (f32[64,768]{1,0:T(8,128)S(1)}, f32[64,768]{1,0:T(8,128)S(1)}, u32[]{:S(2)}, u32[]{:S(2)}) collective-permute-start(f32[64,768]{1,0:T(8,128)S(1)} %fusion.26), channel_id=1, source_target_pairs={{0,8},{8,0},{1,9},{9,1},{2,10},{10,2},{3,11},{11,3},{4,12},{12,4},... | collective-permute-start | bytes 589832 | tf_op jit(solution)/shard_map/ppermute | solution.py:551
  21.5 36.9 %copy-start.1 = (bf16[768,512]{1,0:T(8,128)(2,1)S(1)}, bf16[768,512]{1,0:T(8,128)(2,1)}, u32[]{:S(2)}) copy-start(bf16[768,512]{1,0:T(8,128)(2,1)} %second.1) | copy-start | bytes 2359300
  26.1 8.7 %copy-start.9 = (bf16[64,3456]{1,0:T(8,128)(2,1)}, bf16[64,3456]{1,0:T(8,128)(2,1)S(1)}, u32[]{:S(2)}) copy-start(bf16[64,3456]{1,0:T(8,128)(2,1)S(1)} %collective-permute-done.refs_2_) | copy-start | bytes 1327108
  27.8 17.9 %all-to-all-start = ((bf16[16,8,1280]{2,1,0:T(8,128)(2,1)}), bf16[16,8,1280]{2,1,0:T(8,128)(2,1)S(1)}, u32[]{:S(2)}, u32[]{:S(2)}) async-start(bf16[16,8,1280]{2,1,0:T(8,128)(2,1)} %maximum_bitcast_fusion), calls=%async_computation | async-start | bytes 655360 | tf_op jit(solution)/shard_map/all_to_all | solution.py:555
  57.0 1.4 %collective-permute-start.6 = (bf16[128,768]{1,0:T(8,128)(2,1)S(1)}, bf16[128,768]{1,0:T(8,128)(2,1)S(1)}, u32[]{:S(2)}, u32[]{:S(2)}) collective-permute-start(bf16[128,768]{1,0:T(8,128)(2,1)S(1)} %bitcast.16), channel_id=1, source_target_pairs={{0,8},{8,0},{1,9},{9,1},{2,10},{10,2},{3,11},{11,3},{4,12},{12,4},... | collective-permute-start | bytes 589832 | tf_op jit(solution)/shard_map/ppermute | solution.py:551
  64.1 1.6 %collective-permute-start.7 = (f32[136,512]{1,0:T(8,128)S(1)}, f32[136,512]{1,0:T(8,128)S(1)}, u32[]{:S(2)}, u32[]{:S(2)}) collective-permute-start(f32[136,512]{1,0:T(8,128)S(1)} %get-tuple-element.52), channel_id=1, source_target_pairs={{0,8},{8,0},{1,9},{9,1},{2,10},{10,2},{3,11},{11,3},{4,12},{12,4},... | collective-permute-start | bytes 835592 | tf_op jit(solution)/shard_map/ppermute | solution.py:551
  66.4 12.4 %all-to-all-start.2 = ((bf16[16,8,768]{2,1,0:T(8,128)(2,1)}), bf16[16,8,768]{2,1,0:T(8,128)(2,1)S(1)}, u32[]{:S(2)}, u32[]{:S(2)}) async-start(bf16[16,8,768]{2,1,0:T(8,128)(2,1)} %bitcast.4), calls=%async_computation.2 | async-start | bytes 393216 | tf_op jit(solution)/shard_map/all_to_all | solution.py:555
  79.0 6.3 %copy-start.10 = (f32[1,256]{1,0:T(1,128)}, f32[1,256]{1,0:T(1,128)S(1)}, u32[]{:S(2)}) copy-start(f32[1,256]{1,0:T(1,128)S(1)} %get-tuple-element.57.totals_hbm) | copy-start | bytes 3076
  80.0 13.1 %all-to-all-start.3 = ((bf16[16,8,512]{2,1,0:T(8,128)(2,1)}), bf16[16,8,512]{2,1,0:T(8,128)(2,1)S(1)}, u32[]{:S(2)}, u32[]{:S(2)}) async-start(bf16[16,8,512]{2,1,0:T(8,128)(2,1)} %broadcast_in_dim.5), calls=%async_computation.3 | async-start | bytes 262144 | tf_op jit(solution)/shard_map/all_to_all | solution.py:555
  85.3 9.8 %copy-start.2 = (bf16[3456,256]{1,0:T(8,128)(2,1)S(1)}, bf16[3456,256]{1,0:T(8,128)(2,1)}, u32[]{:S(2)}) copy-start(bf16[3456,256]{1,0:T(8,128)(2,1)} %shard_map.94.turned_hbm) | copy-start | bytes 5308420
  93.1 2.0 %collective-permute-start.8 = (bf16[128,512]{1,0:T(8,128)(2,1)S(1)}, bf16[128,512]{1,0:T(8,128)(2,1)S(1)}, u32[]{:S(2)}, u32[]{:S(2)}) collective-permute-start(bf16[128,512]{1,0:T(8,128)(2,1)S(1)} %bitcast.19), channel_id=1, source_target_pairs={{0,8},{8,0},{1,9},{9,1},{2,10},{10,2},{3,11},{11,3},{4,12},{12,4},... | collective-permute-start | bytes 393224 | tf_op jit(solution)/shard_map/ppermute | solution.py:551

commit v5 on v4

--- a/solution.py
+++ b/solution.py
@@ -280,52 +280,61 @@
     return lax.rsqrt(jnp.sum(block * block, axis=1, keepdims=True) + NORM_EPSILON)
 
 
-def terms_kernel(marks, classes, cen_hbm, shared_hbm, out_hbm, cen, unit, out, unit_sem, in_sem, out_sem):
+def terms_kernel(
+    marks_hbm, classes_hbm, shared_hbm, out_hbm, marks, classes, half, unit, out, first_sem, in_sem, out_sem
+):
     steps, tile = classes.shape
     count = steps * tile
-    unit_copy = pltpu.make_async_copy(shared_hbm.at[pl.ds(count, unit.shape[0])], unit, unit_sem)
-    unit_copy.start()
-    load, loaded = chunked(steps, tile, [(cen_hbm, cen)], in_sem)
+    units = shared_hbm.at[pl.ds(count, unit.shape[0])]
+    firsts = [
+        pltpu.make_async_copy(source, place, first_sem.at[i])
+        for i, (source, place) in enumerate(((marks_hbm, marks), (classes_hbm, classes), (units, unit)))
+    ]
+    for copy in firsts:
+        copy.start()
+    load, loaded = chunked(steps, tile, [(shared_hbm, half)], in_sem)
     store, stored = chunked(steps, tile, [(out, out_hbm)], out_sem)
     for i in range(min(AHEAD, steps)):
         load(i)
+    for copy in firsts:
+        copy.wait()
     columns = columns_of(classes)
-    unit_copy.wait()
     for i in range(steps):
         loaded(i)
         if i + AHEAD < steps:
             load(i + AHEAD)
         rows = rows_at(i, tile)
-        block = cen[rows, :].astype(F32)
-        cosine = dot((block * inverse_norm(block)).astype(BF16), unit[...], NT)
+        cosine = dot(half[rows, :], unit[...], NT)
         positive = columns[:, i : i + 1] == marks[...]
         terms = exp_terms_of(cosine, positive)
-        out[rows, :] = jnp.where(positive, -jnp.maximum(terms, SMALLEST), terms)
+        out[rows, :] = jnp.where(positive, -jnp.maximum(terms, SMALLEST), terms).astype(BF16)
         store(i)
     for i in range(steps):
         stored(i)
 
 
-def turned_terms(centres, classes, marks, shared):
-    count, width = centres.shape
+def turned_terms(classes, marks, shared):
+    count, width = classes.size, shared.shape[1]
     images = marks.shape[1]
     steps = classes.shape[0]
     return pl.pallas_call(
         terms_kernel,
-        in_specs=[VMEM] * 2 + [HBM] * 2,
+        in_specs=[HBM] * 3,
         out_specs=HBM,
-        out_shape=jax.ShapeDtypeStruct((count, images), F32),
+        out_shape=jax.ShapeDtypeStruct((count, images), BF16),
         scratch_shapes=[
+            pltpu.VMEM(marks.shape, jnp.int32),
+            pltpu.VMEM(classes.shape, jnp.int32),
             pltpu.VMEM((count, width), BF16),
             pltpu.VMEM((images, width), BF16),
-            pltpu.VMEM((count, images), F32),
-            pltpu.SemaphoreType.DMA,
+            pltpu.VMEM((count, images), BF16),
+            pltpu.SemaphoreType.DMA((3,)),
             pltpu.SemaphoreType.DMA((1, steps)),
             pltpu.SemaphoreType.DMA((1, steps)),
         ],
         compiler_params=params(57),
         cost_estimate=cost(2 * count * width * images, 8 * count * width),
-    )(marks, classes, centres, shared)
+    )(marks, classes, shared)
 
 
 def centres_kernel(
@@ -367,7 +376,7 @@
         rows = rows_at(i, tile)
         block = cen[rows, :].astype(F32)
         inv = inverse_norm(block)
-        signed = terms[rows, :]
+        signed = terms[rows, :].astype(F32)
         coeff = jnp.abs(signed) * share - jnp.where(signed < 0.0, factor, 0.0)
         grad = dot(coeff.astype(BF16), unit[...])
         along = jnp.sum(grad * block, axis=1, keepdims=True) * (inv * inv)
@@ -390,7 +399,7 @@
             pltpu.VMEM((1, images), F32),
             pltpu.VMEM((images, width), BF16),
             pltpu.VMEM((count, width), BF16),
-            pltpu.VMEM((count, images), F32),
+            pltpu.VMEM((count, images), BF16),
             pltpu.VMEM((count, width), BF16),
             pltpu.SemaphoreType.DMA((2,)),
             pltpu.SemaphoreType.DMA((2, steps)),
@@ -443,28 +452,21 @@
     hid_a,
     hid_b,
     second,
-    turned_hbm,
+    features,
     first_hbm,
     second_out,
-    features,
     out,
     grad_hidden,
-    in_sem,
     out_sem,
 ):
     group = grad_a.shape[0]
-    steps = in_sem.shape[0]
+    steps = out_sem.shape[0]
     tile = out.shape[0] // steps
 
-    def load(i):
-        rows = rows_at(i, tile)
-        return pltpu.make_async_copy(turned_hbm.at[rows], features.at[rows], in_sem.at[i])
-
     def store(i):
         rows = rows_at(i, tile)
         return pltpu.make_async_copy(out.at[rows], first_hbm.at[rows], out_sem.at[i])
 
-    each(steps, True, lambda i: load(i).start())
     acts = []
     for place, (grad, hid) in enumerate(((grad_a, hid_a), (grad_b, hid_b))):
         act, slope = gelu_parts(hid[...].astype(F32))
@@ -473,7 +475,6 @@
         grad_hidden[pl.ds(place * group, group), :] = (grad_act * slope).astype(BF16)
 
     def step(i):
-        load(i).wait()
         rows = rows_at(i, tile)
         out[rows, :] = dot(features[rows, :], grad_hidden[...]).astype(BF16)
         store(i).start()
@@ -488,20 +489,18 @@
 def tail(grad_a, grad_b, hid_a, hid_b, second, turned_features):
     depth, images = turned_features.shape
     hidden, width = second.shape
-    steps = depth // tile_of(depth, 1200)
+    steps = depth // tile_of(depth, 600)
     return pl.pallas_call(
         tail_kernel,
-        in_specs=[VMEM] * 5 + [HBM],
+        in_specs=[VMEM] * 6,
         out_specs=[HBM, VMEM],
         out_shape=[
             jax.ShapeDtypeStruct((depth, hidden), BF16),
             jax.ShapeDtypeStruct((hidden, width), BF16),
         ],
         scratch_shapes=[
-            pltpu.VMEM((depth, images), BF16),
             pltpu.VMEM((depth, hidden), BF16),
             pltpu.VMEM((images, hidden), BF16),
-            pltpu.SemaphoreType.DMA((steps,)),
             pltpu.SemaphoreType.DMA((steps,)),
         ],
         compiler_params=params(40),
@@ -649,7 +648,7 @@
     width = weighted.shape[1]
     sent = assemble(image_count, weighted, core_swap(weighted_send))
     sent, shared = lax.optimization_barrier((sent, shared))
-    terms = turned_terms(centres, classes, marks, shared)
+    terms = turned_terms(classes, marks, shared)
     sent, terms = lax.optimization_barrier((to_chips(sent.reshape(chips, own, -1)), terms))
     sent = jnp.sum(sent.astype(F32), axis=0)
     weighted = sent[:, :width]

time: 103 us -> 101 us (0.981)
  Pallas kernels: 36.4 us -> 34.1 us
    pallas_call x2, Pallas kernels: 12.6 us -> 10.7 us  [the longest x1 6.33 us: turned_terms(): pl.pallas_call(terms_kernel, in_specs=[HBM] * 3, out_specs=HBM, out_shape...]
  transfers between devices with their start and end apart: 12 -> 12, of which waited for: 5 -> 6; matrix products, arithmetic and copies ran while one was open for 9% -> 9% of each run, Pallas kernels for 24% -> 23%
where the time goes in v5:
time: 101 us; the launch traced here: 99.9 us
  Pallas kernels  34.1 us (34%)
  starting transfers between devices  19.5 us (19%)
  waiting for transfers between devices  16.1 us (16%)
  blocking collectives  11.2 us (11%)
  local copies, waits for them, and re-layouts  7.58 us (8%)
  matrix products  5.54 us (5%)
  other arithmetic  3.2 us (3%)
  between operations  2.78 us (3%)
    all_to_all x3, starting transfers between devices, to_chips(): return lax.all_to_all(x, ('row', 'gy'), 0, 0, tiled=True)  15.3 us
    all_to_all x1, blocking collectives, to_chips(): return lax.all_to_all(x, ('row', 'gy'), 0, 0, tiled=True)  11.2 us
    all_to_all x3, waiting for transfers between devices, to_chips(): return lax.all_to_all(x, ('row', 'gy'), 0, 0, tiled=True)  8.65 us
    pallas_call x1, Pallas kernels, grad_centres(): pl.pallas_call(functools.partial(centres_kernel, LOGIT_SCALE / images), i...  7.39 us
    pallas_call x1, Pallas kernels, turned_terms(): pl.pallas_call(terms_kernel, in_specs=[HBM] * 3, out_specs=HBM, out_shape...  6.33 us
    pallas_call x1, Pallas kernels, softmax_sums(): pl.pallas_call(functools.partial(softmax_kernel, images <= 256), in_specs...  5.63 us
    dot_general x3, matrix products, partial_hidden(): jnp.dot(jnp.concatenate([blocks[n] for n in names]), first_weight, prefer...  5.22 us
    pallas_call x1, Pallas kernels, prep(): pl.pallas_call(functools.partial(prep_kernel, images <= 256), in_specs=[V...  4.9 us
  transfers between devices with their start and end apart: 12, of which 6 were waited for; matrix products, arithmetic and copies ran while one was open for 9% of the time, Pallas kernels for 23%

profile of v5, /device:TPU:0, one launch (start us, length us, event | category | flops | bytes accessed | tf_op | source)
XLA Modules:
  0.0 99.9 jit_solution(7038502183221881247)
XLA Ops:
  0.7 2.1 %constant_dynamic-slice_fusion.2 = (bf16[64,3456]{1,0:T(8,128)(2,1)}, bf16[64,3456]{1,0:T(8,128)(2,1)S(1)}, bf16[64,3456]{1,0:T(8,128)(2,1)S(1)}) fusion(bf16[64,13824]{1,0:T(8,128)(2,1)} %param.6, s32[]{:T(128)S(6)} %select_n.51, s32[]{:T(128)S(6)} %select_n.49, s32[]{:T(128)S(6)} %select_n.48), kind=kLoop, calls=%fused_computation.38 | loop fusion | bytes 2654220 | tf_op jit(solution)/shard_map/dynamic_slice | solution.py:582
  2.8 0.5 collective-permute-start.2
  3.3 2.6 %collective-permute-start.1 = (bf16[64,3456]{1,0:T(8,128)(2,1)S(1)}, bf16[64,3456]{1,0:T(8,128)(2,1)S(1)}, u32[]{:S(2)}, u32[]{:S(2)}) collective-permute-start(bf16[64,3456]{1,0:T(8,128)(2,1)S(1)} %get-tuple-element.67), channel_id=1, source_target_pairs={{0,24},{8,16},{16,8},{24,0},{1,25},{9,17},{17,9},{25,1},{2,26},{10... | collective-permute-start | bytes 1327112 | tf_op jit(solution)/shard_map/ppermute | solution.py:586
  5.9 0.7 broadcast_add_fusion
  6.7 0.8 reshape.43
  7.6 1.0 %constant_dynamic-slice_fusion.1.refs_0_ = bf16[64,3456]{1,0:T(8,128)(2,1)S(1)} fusion(bf16[64,13824]{1,0:T(8,128)(2,1)} %param.6, s32[]{:T(128)S(6)} %select_n.54), kind=kLoop, calls=%fused_computation.37 | loop fusion | bytes 884740 | tf_op jit(solution)/shard_map/dynamic_slice | solution.py:580
  8.7 2.6 %copy-done = bf16[4864,512]{1,0:T(8,128)(2,1)S(1)} copy-done((bf16[4864,512]{1,0:T(8,128)(2,1)S(1)}, bf16[4864,512]{1,0:T(8,128)(2,1)}, u32[]{:S(2)}) %copy-start) | copy-done | bytes 4980760
  11.3 4.9 %shard_map.93 = (bf16[24320,512]{1,0:T(8,128)(2,1)}, bf16[256,512]{1,0:T(8,128)(2,1)S(1)}) custom-call(s32[1,256]{1,0:T(1,128)S(1)} %broadcast_in_dim_reshape.3.marks.marks_hbm, s32[4,1216]{1,0:T(4,128)S(1)} %reshape.44.classes.classes_hbm, bf16[4864,512]{1,0:T(8,128)(2,1)S(1)} %copy-done), custom_call_target="tpu_custom_call" | custom-call | flops 1275068416 | bytes 19922944 | tf_op jit(solution)/shard_map/pallas_call | solution.py:122
  16.4 3.4 %fusion = f32[128,768]{1,0:T(8,128)S(1)} fusion(bf16[3456,768]{1,0:T(8,128)(2,1)} %param.7, bf16[64,3456]{1,0:T(8,128)(2,1)S(1)} %constant_dynamic-slice_fusion.1.refs_0_, bf16[64,3456]{1,0:T(8,128)(2,1)S(1)} %collective-permute-done.2.refs_1_), kind=kOutput, calls=%fused_computation.1 | convolution fusion | flops 681246720 | bytes 6586368 | tf_op jit(solution)/shard_map/dot_general | solution.py:601
  20.0 0.4 collective-permute-start.5
  20.4 0.9 fusion.26
  21.5 4.6 %collective-permute-done.refs_2_ = bf16[64,3456]{1,0:T(8,128)(2,1)S(1)} collective-permute-done((bf16[64,3456]{1,0:T(8,128)(2,1)S(1)}, bf16[64,3456]{1,0:T(8,128)(2,1)S(1)}, u32[]{:S(2)}, u32[]{:S(2)}) %collective-permute-start) | collective-permute-done | bytes 442400 | tf_op jit(solution)/shard_map/ppermute | solution.py:586
  26.1 0.9 convolution_add_fusion
  27.1 0.8 maximum_bitcast_fusion
  27.8 7.0 %all-to-all-start = ((bf16[16,8,1280]{2,1,0:T(8,128)(2,1)}), bf16[16,8,1280]{2,1,0:T(8,128)(2,1)S(1)}, u32[]{:S(2)}, u32[]{:S(2)}) async-start(bf16[16,8,1280]{2,1,0:T(8,128)(2,1)} %maximum_bitcast_fusion), calls=%async_computation | async-start | bytes 655360 | tf_op jit(solution)/shard_map/all_to_all | solution.py:554
  34.8 4.7 %shard_map.94.features = bf16[3456,256]{1,0:T(8,128)(2,1)} custom-call(s32[1]{0:T(128)} %bitcast.2.place_ref, bf16[64,3456]{1,0:T(8,128)(2,1)} %copy-done.6, bf16[64,3456]{1,0:T(8,128)(2,1)} %copy-done.7, bf16[64,3456]{1,0:T(8,128)(2,1)} %copy-done.9, bf16[64,3456]{1,0:T(8,128)(2,1)} %copy-done.8), custom_call_target="tpu_custom_call" | custom-call | bytes 3538944 | tf_op jit(solution)/shard_map/pallas_call | solution.py:438
  39.5 6.2 %all-to-all-done = bf16[16,8,1280]{2,1,0:T(8,128)(2,1)S(1)} async-done(((bf16[16,8,1280]{2,1,0:T(8,128)(2,1)}), bf16[16,8,1280]{2,1,0:T(8,128)(2,1)S(1)}, u32[]{:S(2)}, u32[]{:S(2)}) %all-to-all-start) | async-done | bytes 327712 | tf_op jit(solution)/shard_map/all_to_all | solution.py:554
  45.8 11.2 %all_to_all.20 = bf16[16,8,768]{2,1,0:T(8,128)(2,1)S(1)} all-to-all(bf16[16,8,768]{2,1,0:T(8,128)(2,1)S(1)} %broadcast_in_dim.4), channel_id=1, replica_groups=mesh['row'=2,'core'=2,'gy'=8] {'row','gy'}, dimensions={0} | all-to-all | bytes 393216 | tf_op jit(solution)/shard_map/all_to_all | solution.py:554
  57.0 1.4 %collective-permute-done.6.hid_b_hbm.hid_b = bf16[128,768]{1,0:T(8,128)(2,1)S(1)} collective-permute-done((bf16[128,768]{1,0:T(8,128)(2,1)S(1)}, bf16[128,768]{1,0:T(8,128)(2,1)S(1)}, u32[]{:S(2)}, u32[]{:S(2)}) %collective-permute-start.6) | collective-permute-done | bytes 196640 | tf_op jit(solution)/shard_map/ppermute | solution.py:550
  58.4 5.6 %shard_map.95 = (f32[136,512]{1,0:T(8,128)S(1)}, f32[136,512]{1,0:T(8,128)S(1)}, bf16[24320,512]{1,0:T(8,128)(2,1)}) custom-call(bf16[128,768]{1,0:T(8,128)(2,1)S(1)} %bitcast.17, bf16[128,768]{1,0:T(8,128)(2,1)S(1)} %collective-permute-done.6.hid_b_hbm.hid_b, bf16[768,512]{1,0:T(8,128)(2,1)S(1)} %copy-done.1, ...), custom_call_target="tpu_custom_call", output_to_operand_aliasing={{2}: (5, {})} | custom-call | flops 2550136832 | bytes 9961472 | tf_op jit(solution)/shard_map/pallas_call | solution.py:229
  64.3 1.4 %collective-permute-done.7.got = f32[136,512]{1,0:T(8,128)S(1)} collective-permute-done((f32[136,512]{1,0:T(8,128)S(1)}, f32[136,512]{1,0:T(8,128)S(1)}, u32[]{:S(2)}, u32[]{:S(2)}) %collective-permute-start.7) | collective-permute-done | bytes 278560 | tf_op jit(solution)/shard_map/ppermute | solution.py:550
  65.7 0.7 shard_map.96
  66.4 3.7 %all-to-all-start.2 = ((bf16[16,8,768]{2,1,0:T(8,128)(2,1)}), bf16[16,8,768]{2,1,0:T(8,128)(2,1)S(1)}, u32[]{:S(2)}, u32[]{:S(2)}) async-start(bf16[16,8,768]{2,1,0:T(8,128)(2,1)} %bitcast.4), calls=%async_computation.2 | async-start | bytes 393216 | tf_op jit(solution)/shard_map/all_to_all | solution.py:554
  70.1 0.3 multiply_reduce_fusion.1
  70.5 6.3 %shard_map.97.terms_hbm = bf16[4864,256]{1,0:T(8,128)(2,1)} custom-call(s32[1,256]{1,0:T(1,128)} %copy-done.4, s32[4,1216]{1,0:T(4,128)} %copy-done.3, bf16[24320,512]{1,0:T(8,128)(2,1)} %get-tuple-element.55.shared_hbm), custom_call_target="tpu_custom_call" | custom-call | flops 1275068416 | bytes 19922944 | tf_op jit(solution)/shard_map/pallas_call | solution.py:320
  76.8 2.1 %all-to-all-done.2 = bf16[16,8,768]{2,1,0:T(8,128)(2,1)S(1)} async-done(((bf16[16,8,768]{2,1,0:T(8,128)(2,1)}), bf16[16,8,768]{2,1,0:T(8,128)(2,1)S(1)}, u32[]{:S(2)}, u32[]{:S(2)}) %all-to-all-start.2) | async-done | bytes 196640 | tf_op jit(solution)/shard_map/all_to_all | solution.py:554
  79.3 0.7 broadcast_in_dim.5
  80.0 4.6 %all-to-all-start.3 = ((bf16[16,8,512]{2,1,0:T(8,128)(2,1)}), bf16[16,8,512]{2,1,0:T(8,128)(2,1)S(1)}, u32[]{:S(2)}, u32[]{:S(2)}) async-start(bf16[16,8,512]{2,1,0:T(8,128)(2,1)} %broadcast_in_dim.5), calls=%async_computation.3 | async-start | bytes 262144 | tf_op jit(solution)/shard_map/all_to_all | solution.py:554
  84.7 7.4 %shard_map.98 = bf16[4864,512]{1,0:T(8,128)(2,1)} custom-call(f32[1,256]{1,0:T(1,128)} %copy-done.10, bf16[4864,512]{1,0:T(8,128)(2,1)} %cen_hbm.3, bf16[24320,512]{1,0:T(8,128)(2,1)} %get-tuple-element.55.shared_hbm, bf16[4864,256]{1,0:T(8,128)(2,1)} %shard_map.97.terms_hbm), custom_call_target="tpu_custom_call" | custom-call | flops 2550136832 | bytes 19922944 | tf_op jit(solution)/shard_map/pallas_call | solution.py:393
  92.1 0.4 all-to-all-done.3
  92.5 1.2 %subtract_reduce_fusion = f32[]{:T(128)} fusion(f32[1,256]{1,0:T(1,128)S(1)} %get-tuple-element.58, f32[1,256]{1,0:T(1,128)} %copy-done.10), kind=kLoop, calls=%fused_computation.42 | loop fusion | flops 767 | bytes 2052 | tf_op jit(solution)/shard_map/reduce_sum | solution.py:669
  94.4 4.4 %shard_map.99 = (bf16[3456,768]{1,0:T(8,128)(2,1)}, bf16[768,512]{1,0:T(8,128)(2,1)}) custom-call(bf16[128,512]{1,0:T(8,128)(2,1)S(1)} %bitcast.20, bf16[128,512]{1,0:T(8,128)(2,1)S(1)} %collective-permute-done.8.grad_b, bf16[128,768]{1,0:T(8,128)(2,1)S(1)} %bitcast.18, bf16[128,768]{1,0:T(8,128)(2,1)S(1)} %collective-permute-done.6.hid_b_hbm.hid_b, ...), custom_call_target="tpu_custom_call" | custom-call | flops 1358954496 | bytes 7077888 | tf_op jit(solution)/shard_map/pallas_call | solution.py:493
  (55 shorter events, 1.5 us)
Async XLA Ops:
  2.8 5.9 %collective-permute-start.2 = (bf16[64,3456]{1,0:T(8,128)(2,1)}, bf16[64,3456]{1,0:T(8,128)(2,1)S(1)}, u32[]{:S(2)}, u32[]{:S(2)}) collective-permute-start(bf16[64,3456]{1,0:T(8,128)(2,1)} %get-tuple-element.66), channel_id=1, source_target_pairs={{0,8},{8,0},{16,24},{24,16},{1,9},{9,1},{17,25},{25,17},{2,10},{10... | collective-permute-start | bytes 1327112 | tf_op jit(solution)/shard_map/ppermute | solution.py:586
  3.3 16.7 %collective-permute-start.1 = (bf16[64,3456]{1,0:T(8,128)(2,1)S(1)}, bf16[64,3456]{1,0:T(8,128)(2,1)S(1)}, u32[]{:S(2)}, u32[]{:S(2)}) collective-permute-start(bf16[64,3456]{1,0:T(8,128)(2,1)S(1)} %get-tuple-element.67), channel_id=1, source_target_pairs={{0,24},{8,16},{16,8},{24,0},{1,25},{9,17},{17,9},{25,1},{2,26},{10... | collective-permute-start | bytes 1327112 | tf_op jit(solution)/shard_map/ppermute | solution.py:586
  5.9 20.2 %collective-permute-start = (bf16[64,3456]{1,0:T(8,128)(2,1)S(1)}, bf16[64,3456]{1,0:T(8,128)(2,1)S(1)}, u32[]{:S(2)}, u32[]{:S(2)}) collective-permute-start(bf16[64,3456]{1,0:T(8,128)(2,1)S(1)} %get-tuple-element.68), channel_id=1, source_target_pairs={{0,16},{8,24},{16,0},{24,8},{1,17},{9,25},{17,1},{25,9},{2,18},{10... | collective-permute-start | bytes 1327112 | tf_op jit(solution)/shard_map/ppermute | solution.py:586
  6.7 51.7 %copy-start.3 = (s32[4,1216]{1,0:T(4,128)}, s32[4,1216]{1,0:T(4,128)S(1)}, u32[]{:S(2)}) copy-start(s32[4,1216]{1,0:T(4,128)S(1)} %reshape.44.classes.classes_hbm) | copy-start | bytes 58372
  7.6 50.8 %copy-start.4 = (s32[1,256]{1,0:T(1,128)}, s32[1,256]{1,0:T(1,128)S(1)}, u32[]{:S(2)}) copy-start(s32[1,256]{1,0:T(1,128)S(1)} %broadcast_in_dim_reshape.3.marks.marks_hbm) | copy-start | bytes 3076
  8.7 11.2 %copy-start.6 = (bf16[64,3456]{1,0:T(8,128)(2,1)}, bf16[64,3456]{1,0:T(8,128)(2,1)S(1)}, u32[]{:S(2)}) copy-start(bf16[64,3456]{1,0:T(8,128)(2,1)S(1)} %constant_dynamic-slice_fusion.1.refs_0_) | copy-start | bytes 1327108
  8.7 2.6 %copy-start = (bf16[4864,512]{1,0:T(8,128)(2,1)S(1)}, bf16[4864,512]{1,0:T(8,128)(2,1)}, u32[]{:S(2)}) copy-start(bf16[4864,512]{1,0:T(8,128)(2,1)} %cen_hbm.3) | copy-start | bytes 14942212
  11.3 8.6 %copy-start.7 = (bf16[64,3456]{1,0:T(8,128)(2,1)}, bf16[64,3456]{1,0:T(8,128)(2,1)S(1)}, u32[]{:S(2)}) copy-start(bf16[64,3456]{1,0:T(8,128)(2,1)S(1)} %collective-permute-done.2.refs_1_) | copy-start | bytes 1327108
  11.3 9.1 %copy-start.5 = (bf16[3456,768]{1,0:T(8,128)(2,1)S(1)}, bf16[3456,768]{1,0:T(8,128)(2,1)}, u32[]{:S(2)}) copy-start(bf16[3456,768]{1,0:T(8,128)(2,1)} %param.7) | copy-start | bytes 15925252
  16.2 3.7 %collective-permute-start.3 = (bf16[128,512]{1,0:T(8,128)(2,1)S(1)}, bf16[128,512]{1,0:T(8,128)(2,1)S(1)}, u32[]{:S(2)}, u32[]{:S(2)}) collective-permute-start(bf16[128,512]{1,0:T(8,128)(2,1)S(1)} %slice.32), channel_id=1, source_target_pairs={{0,8},{8,0},{1,9},{9,1},{2,10},{10,2},{3,11},{11,3},{4,12},{12,4},... | collective-permute-start | bytes 393224 | tf_op jit(solution)/shard_map/ppermute | solution.py:550
  19.9 7.1 %copy-start.8 = (bf16[64,3456]{1,0:T(8,128)(2,1)}, bf16[64,3456]{1,0:T(8,128)(2,1)S(1)}, u32[]{:S(2)}) copy-start(bf16[64,3456]{1,0:T(8,128)(2,1)S(1)} %collective-permute-done.1.refs_3_) | copy-start | bytes 1327108
  20.0 1.5 %collective-permute-start.5 = (f32[64,768]{1,0:T(8,128)S(1)}, f32[64,768]{1,0:T(8,128)S(1)}, u32[]{:S(2)}, u32[]{:S(2)}) collective-permute-start(f32[64,768]{1,0:T(8,128)S(1)} %slice.34), channel_id=1, source_target_pairs={{0,8},{8,0},{1,9},{9,1},{2,10},{10,2},{3,11},{11,3},{4,12},{12,4},... | collective-permute-start | bytes 589832 | tf_op jit(solution)/shard_map/ppermute | solution.py:550
  21.3 4.8 %collective-permute-start.4 = (f32[64,768]{1,0:T(8,128)S(1)}, f32[64,768]{1,0:T(8,128)S(1)}, u32[]{:S(2)}, u32[]{:S(2)}) collective-permute-start(f32[64,768]{1,0:T(8,128)S(1)} %fusion.26), channel_id=1, source_target_pairs={{0,8},{8,0},{1,9},{9,1},{2,10},{10,2},{3,11},{11,3},{4,12},{12,4},... | collective-permute-start | bytes 589832 | tf_op jit(solution)/shard_map/ppermute | solution.py:550
  21.5 36.9 %copy-start.1 = (bf16[768,512]{1,0:T(8,128)(2,1)S(1)}, bf16[768,512]{1,0:T(8,128)(2,1)}, u32[]{:S(2)}) copy-start(bf16[768,512]{1,0:T(8,128)(2,1)} %second.1) | copy-start | bytes 2359300
  26.1 8.7 %copy-start.9 = (bf16[64,3456]{1,0:T(8,128)(2,1)}, bf16[64,3456]{1,0:T(8,128)(2,1)S(1)}, u32[]{:S(2)}) copy-start(bf16[64,3456]{1,0:T(8,128)(2,1)S(1)} %collective-permute-done.refs_2_) | copy-start | bytes 1327108
  27.8 17.9 %all-to-all-start = ((bf16[16,8,1280]{2,1,0:T(8,128)(2,1)}), bf16[16,8,1280]{2,1,0:T(8,128)(2,1)S(1)}, u32[]{:S(2)}, u32[]{:S(2)}) async-start(bf16[16,8,1280]{2,1,0:T(8,128)(2,1)} %maximum_bitcast_fusion), calls=%async_computation | async-start | bytes 655360 | tf_op jit(solution)/shard_map/all_to_all | solution.py:554
  57.0 1.4 %collective-permute-start.6 = (bf16[128,768]{1,0:T(8,128)(2,1)S(1)}, bf16[128,768]{1,0:T(8,128)(2,1)S(1)}, u32[]{:S(2)}, u32[]{:S(2)}) collective-permute-start(bf16[128,768]{1,0:T(8,128)(2,1)S(1)} %bitcast.16), channel_id=1, source_target_pairs={{0,8},{8,0},{1,9},{9,1},{2,10},{10,2},{3,11},{11,3},{4,12},{12,4},... | collective-permute-start | bytes 589832 | tf_op jit(solution)/shard_map/ppermute | solution.py:550
  64.1 1.6 %collective-permute-start.7 = (f32[136,512]{1,0:T(8,128)S(1)}, f32[136,512]{1,0:T(8,128)S(1)}, u32[]{:S(2)}, u32[]{:S(2)}) collective-permute-start(f32[136,512]{1,0:T(8,128)S(1)} %get-tuple-element.52), channel_id=1, source_target_pairs={{0,8},{8,0},{1,9},{9,1},{2,10},{10,2},{3,11},{11,3},{4,12},{12,4},... | collective-permute-start | bytes 835592 | tf_op jit(solution)/shard_map/ppermute | solution.py:550
  66.4 12.4 %all-to-all-start.2 = ((bf16[16,8,768]{2,1,0:T(8,128)(2,1)}), bf16[16,8,768]{2,1,0:T(8,128)(2,1)S(1)}, u32[]{:S(2)}, u32[]{:S(2)}) async-start(bf16[16,8,768]{2,1,0:T(8,128)(2,1)} %bitcast.4), calls=%async_computation.2 | async-start | bytes 393216 | tf_op jit(solution)/shard_map/all_to_all | solution.py:554
  79.0 5.7 %copy-start.10 = (f32[1,256]{1,0:T(1,128)}, f32[1,256]{1,0:T(1,128)S(1)}, u32[]{:S(2)}) copy-start(f32[1,256]{1,0:T(1,128)S(1)} %get-tuple-element.57.totals_hbm) | copy-start | bytes 3076
  80.0 12.5 %all-to-all-start.3 = ((bf16[16,8,512]{2,1,0:T(8,128)(2,1)}), bf16[16,8,512]{2,1,0:T(8,128)(2,1)S(1)}, u32[]{:S(2)}, u32[]{:S(2)}) async-start(bf16[16,8,512]{2,1,0:T(8,128)(2,1)} %broadcast_in_dim.5), calls=%async_computation.3 | async-start | bytes 262144 | tf_op jit(solution)/shard_map/all_to_all | solution.py:554
  84.7 9.7 %copy-start.2 = (bf16[3456,256]{1,0:T(8,128)(2,1)S(1)}, bf16[3456,256]{1,0:T(8,128)(2,1)}, u32[]{:S(2)}) copy-start(bf16[3456,256]{1,0:T(8,128)(2,1)} %shard_map.94.features) | copy-start | bytes 5308420
  92.5 1.9 %collective-permute-start.8 = (bf16[128,512]{1,0:T(8,128)(2,1)S(1)}, bf16[128,512]{1,0:T(8,128)(2,1)S(1)}, u32[]{:S(2)}, u32[]{:S(2)}) collective-permute-start(bf16[128,512]{1,0:T(8,128)(2,1)S(1)} %bitcast.19), channel_id=1, source_target_pairs={{0,8},{8,0},{1,9},{9,1},{2,10},{10,2},{3,11},{11,3},{4,12},{12,4},... | collective-permute-start | bytes 393224 | tf_op jit(solution)/shard_map/ppermute | solution.py:550

commit v6 on v5

--- a/solution.py
+++ b/solution.py
@@ -339,12 +339,13 @@
 
 def centres_kernel(
     factor,
-    totals_hbm,
+    sums_hbm,
     cen_hbm,
     shared_hbm,
     terms_hbm,
     out_hbm,
-    totals,
+    loss,
+    sums,
     unit,
     cen,
     terms,
@@ -357,7 +358,7 @@
     count = cen.shape[0]
     tile = count // steps
     firsts = [
-        pltpu.make_async_copy(totals_hbm, totals, first_sem.at[0]),
+        pltpu.make_async_copy(sums_hbm, sums, first_sem.at[0]),
         pltpu.make_async_copy(shared_hbm.at[pl.ds(count, unit.shape[0])], unit, first_sem.at[1]),
     ]
     load, loaded = chunked(steps, tile, [(cen_hbm, cen), (terms_hbm, terms)], in_sem)
@@ -368,7 +369,8 @@
         load(i)
     for copy in firsts:
         copy.wait()
-    share = factor / totals[...]
+    totals, target = sums[0:1, :] * (1.0 / PIECE_SCALE), sums[1:2, :]
+    share = factor / totals
     for i in range(steps):
         loaded(i)
         if i + AHEAD + 1 < steps:
@@ -382,21 +384,25 @@
         along = jnp.sum(grad * block, axis=1, keepdims=True) * (inv * inv)
         out[rows, :] = (inv * (grad - block * along)).astype(BF16)
         store(i)
+    loss[0, 0] = jnp.sum(LOGIT_SCALE + jnp.log(totals) - target) / totals.shape[1]
     for i in range(steps):
         stored(i)
 
 
-def grad_centres(centres, terms, shared, totals):
+def grad_centres(centres, terms, shared, sums):
     count, width = centres.shape
     images = terms.shape[1]
     steps = count // tile_of(count, 640)
     return pl.pallas_call(
         functools.partial(centres_kernel, LOGIT_SCALE / images),
         in_specs=[HBM] * 4,
-        out_specs=HBM,
-        out_shape=jax.ShapeDtypeStruct((count, width), BF16),
+        out_specs=[HBM, pl.BlockSpec(memory_space=pltpu.SMEM)],
+        out_shape=[
+            jax.ShapeDtypeStruct((count, width), BF16),
+            jax.ShapeDtypeStruct((1, 1), F32),
+        ],
         scratch_shapes=[
-            pltpu.VMEM((1, images), F32),
+            pltpu.VMEM((2, images), F32),
             pltpu.VMEM((images, width), BF16),
             pltpu.VMEM((count, width), BF16),
             pltpu.VMEM((count, images), BF16),
@@ -407,7 +413,7 @@
         ],
         compiler_params=params(57),
         cost_estimate=cost(4 * count * width * images, 8 * count * width),
-    )(totals, centres, shared, terms)
+    )(sums, centres, shared, terms)
 
 
 def turn_kernel(rows, place_ref, *refs):
@@ -508,7 +514,7 @@
     )(grad_a, grad_b, hid_a, hid_b, second, turned_features)
 
 
-def assemble_kernel(images, keep, got, out):
+def assemble_kernel(images, keep, got, picked, out):
     width = keep.shape[1]
     half = keep.shape[0] - 8
     each = -(-images // width)
@@ -531,19 +537,20 @@
         both = both - part
     riding = jnp.concatenate(parts + [jnp.zeros_like(both)])
     out[:, :width] = (keep[:half, :] + got[:half, :]).astype(BF16)
-    out[:, width:] = jnp.concatenate([riding] * (half // 8)).astype(BF16)
-
-
-def assemble(images, keep, got):
+    out[:, width : width + images] = jnp.concatenate([riding] * (half // 8)).astype(BF16)
+    out[:, width + images :] = picked[...]
+
+
+def assemble(images, keep, got, picked):
     half, width = keep.shape[0] - 8, keep.shape[1]
     return pl.pallas_call(
         functools.partial(assemble_kernel, images),
-        in_specs=[VMEM] * 2,
+        in_specs=[VMEM] * 3,
         out_specs=VMEM,
-        out_shape=jax.ShapeDtypeStruct((half, width + images), BF16),
+        out_shape=jax.ShapeDtypeStruct((half, width + images + picked.shape[1]), BF16),
         compiler_params=params(16),
         cost_estimate=cost(0, 8 * half * (width + images)),
-    )(keep, got)
+    )(keep, got, picked)
 
 
 def core_swap(x):
@@ -625,14 +632,14 @@
         part = jnp.concatenate([near_keep, far_keep]).reshape(rows, group, -1)
         part = part[(y - jnp.arange(rows)) % rows].reshape(half, -1)
     wide = part.shape[1]
-    part = jnp.concatenate([part.astype(BF16), picked], axis=1)
+    part = part.astype(BF16)
     part = to_chips(part.reshape(chips, own, -1))
     place = jnp.reshape(y, (1,)).astype(jnp.int32)
     order = [(dy, dc) for dy in range(rows) for dc in range(2)]
     turned_features = turned(rows, place, [blocks[n] for n in order])
     part, turned_features = lax.optimization_barrier((part, turned_features))
     part = jnp.sum(part.astype(F32), axis=0)
-    hidden_own, picked = part[:, :wide].astype(BF16), part[:, wide:]
+    hidden_own = part.astype(BF16)
     hid_a = to_all_chips(hidden_own, chips)
     hid_b = core_swap(hid_a)
 
@@ -646,14 +653,15 @@
         hid_a, hid_b, second_weight, marks, classes, normed_half
     )
     width = weighted.shape[1]
-    sent = assemble(image_count, weighted, core_swap(weighted_send))
+    sent = assemble(image_count, weighted, core_swap(weighted_send), picked)
     sent, shared = lax.optimization_barrier((sent, shared))
     terms = turned_terms(classes, marks, shared)
     sent, terms = lax.optimization_barrier((to_chips(sent.reshape(chips, own, -1)), terms))
     sent = jnp.sum(sent.astype(F32), axis=0)
-    weighted = sent[:, :width]
-    sums = sent[:, width:].reshape(4, 2, image_count).sum(axis=0)
-    totals, target = sums[0:1] * (1.0 / PIECE_SCALE), sums[1:2]
+    weighted, riding = sent[:, :width], sent[:, width : width + image_count]
+    picked = sent[:, width + image_count :]
+    sums = riding.reshape(4, 2, image_count).sum(axis=0)
+    totals = sums[0:1] * (1.0 / PIECE_SCALE)
 
     factor = LOGIT_SCALE / image_count
     totals_own = lax.dynamic_slice_in_dim(totals, chip * own, own, axis=1).reshape(own, 1)
@@ -661,14 +669,12 @@
     grad_embed = inv_own * (grad_unit - unit_own * jnp.sum(grad_unit * unit_own, axis=1, keepdims=True))
     grad_embed = grad_embed.astype(BF16)
     grad_embed = jnp.broadcast_to(grad_embed[None], (chips,) + grad_embed.shape)
-    grad_embed, totals, target = lax.optimization_barrier((grad_embed, totals, target))
-    grad_cen = grad_centres(centres, terms, shared, totals)
+    grad_cen, loss = grad_centres(centres, terms, shared, sums)
     grad_a = to_chips(grad_embed).reshape(half, -1)
     grad_a, grad_cen = lax.optimization_barrier((grad_a, grad_cen))
     grad_b = core_swap(grad_a)
-    loss = jnp.mean(LOGIT_SCALE + jnp.log(totals) - target)
     grad_first, grad_second = tail(grad_a, grad_b, hid_a, hid_b, second_weight, turned_features)
-    return loss, grad_first, grad_second, grad_cen
+    return loss.reshape(()), grad_first, grad_second, grad_cen
 
 
 def solution(mesh):

time: 101 us -> 97.9 us (0.969)
  between operations: 2.78 us -> 1.15 us
  other arithmetic: 3.2 us -> 1.96 us
  waiting for transfers between devices: 16.1 us -> 17.2 us
    ppermute x6, waiting for transfers between devices: 2.89 us -> 4.23 us  [core_swap(): return lax.ppermute(x, 'core', [(0, 1), (1, 0)])]
    reduce_sum x2 -> x1, other arithmetic: 1.26 us -> 0.02 us  [shards(): sums = riding.reshape(4, 2, image_count).sum(axis=0)]
    all_to_all x3, starting transfers between devices: 15.3 us -> 14.3 us  [to_chips(): return lax.all_to_all(x, ('row', 'gy'), 0, 0, tiled=True)]
  transfers between devices with their start and end apart: 12 -> 12, of which waited for: 6 -> 6; matrix products, arithmetic and copies ran while one was open for 9% -> 8% of each run, Pallas kernels for 23% -> 25%
where the time goes in v6:
time: 97.9 us; the launch traced here: 97.2 us
  Pallas kernels  34.7 us (35%)
  starting transfers between devices  18.6 us (19%)
  waiting for transfers between devices  17.2 us (18%)
  blocking collectives  11.3 us (12%)
  local copies, waits for them, and re-layouts  6.74 us (7%)
  matrix products  5.56 us (6%)
  other arithmetic  1.96 us (2%)
  between operations  1.15 us (1%)
    all_to_all x3, starting transfers between devices, to_chips(): return lax.all_to_all(x, ('row', 'gy'), 0, 0, tiled=True)  14.3 us
    all_to_all x1, blocking collectives, to_chips(): return lax.all_to_all(x, ('row', 'gy'), 0, 0, tiled=True)  11.3 us
    all_to_all x3, waiting for transfers between devices, to_chips(): return lax.all_to_all(x, ('row', 'gy'), 0, 0, tiled=True)  8.46 us
    pallas_call x1, Pallas kernels, grad_centres(): pl.pallas_call(functools.partial(centres_kernel, LOGIT_SCALE / images), i...  7.91 us
    pallas_call x1, Pallas kernels, turned_terms(): pl.pallas_call(terms_kernel, in_specs=[HBM] * 3, out_specs=HBM, out_shape...  6.33 us
    pallas_call x1, Pallas kernels, softmax_sums(): pl.pallas_call(functools.partial(softmax_kernel, images <= 256), in_specs...  5.61 us
    dot_general x3, matrix products, partial_hidden(): jnp.dot(jnp.concatenate([blocks[n] for n in names]), first_weight, prefer...  5.24 us
    pallas_call x1, Pallas kernels, prep(): pl.pallas_call(functools.partial(prep_kernel, images <= 256), in_specs=[V...  4.9 us
  transfers between devices with their start and end apart: 12, of which 6 were waited for; matrix products, arithmetic and copies ran while one was open for 8% of the time, Pallas kernels for 25%

profile of v6, /device:TPU:0, one launch (start us, length us, event | category | flops | bytes accessed | tf_op | source)
XLA Modules:
  0.0 97.2 jit_solution(1544352148135184137)
XLA Ops:
  0.7 1.4 %constant_dynamic-slice_fusion.2 = (bf16[64,3456]{1,0:T(8,128)(2,1)S(1)}, bf16[64,3456]{1,0:T(8,128)(2,1)S(1)}, bf16[64,3456]{1,0:T(8,128)(2,1)S(1)}) fusion(bf16[64,13824]{1,0:T(8,128)(2,1)} %param.6, s32[]{:T(128)S(6)} %select_n.53, s32[]{:T(128)S(6)} %select_n.51, s32[]{:T(128)S(6)} %select_n.50), kind=kLoop, calls=%fused_computation.36 | loop fusion | bytes 2654220 | tf_op jit(solution)/shard_map/dynamic_slice | solution.py:589
  2.1 0.5 collective-permute-start.2
  2.6 2.6 %collective-permute-start.1 = (bf16[64,3456]{1,0:T(8,128)(2,1)S(1)}, bf16[64,3456]{1,0:T(8,128)(2,1)S(1)}, u32[]{:S(2)}, u32[]{:S(2)}) collective-permute-start(bf16[64,3456]{1,0:T(8,128)(2,1)S(1)} %get-tuple-element.65), channel_id=1, source_target_pairs={{0,24},{8,16},{16,8},{24,0},{1,25},{9,17},{17,9},{25,1},{2,26},{10... | collective-permute-start | bytes 1327112 | tf_op jit(solution)/shard_map/ppermute | solution.py:593
  5.3 0.7 broadcast_add_fusion
  6.1 0.8 reshape.49
  7.0 1.0 %constant_dynamic-slice_fusion.1.refs_0_ = bf16[64,3456]{1,0:T(8,128)(2,1)S(1)} fusion(bf16[64,13824]{1,0:T(8,128)(2,1)} %param.6, s32[]{:T(128)S(6)} %select_n.56), kind=kLoop, calls=%fused_computation.35 | loop fusion | bytes 884740 | tf_op jit(solution)/shard_map/dynamic_slice | solution.py:587
  8.1 2.6 %copy-done = bf16[4864,512]{1,0:T(8,128)(2,1)S(1)} copy-done((bf16[4864,512]{1,0:T(8,128)(2,1)S(1)}, bf16[4864,512]{1,0:T(8,128)(2,1)}, u32[]{:S(2)}) %copy-start) | copy-done | bytes 4980760
  10.6 4.9 %shard_map.93 = (bf16[24320,512]{1,0:T(8,128)(2,1)}, bf16[256,512]{1,0:T(8,128)(2,1)S(1)}) custom-call(s32[1,256]{1,0:T(1,128)S(1)} %broadcast_in_dim_reshape.3.marks.marks_hbm, s32[4,1216]{1,0:T(4,128)S(1)} %reshape.50.classes.classes_hbm, bf16[4864,512]{1,0:T(8,128)(2,1)S(1)} %copy-done), custom_call_target="tpu_custom_call" | custom-call | flops 1275068416 | bytes 19922944 | tf_op jit(solution)/shard_map/pallas_call | solution.py:122
  15.7 3.5 %fusion = f32[128,768]{1,0:T(8,128)S(1)} fusion(bf16[3456,768]{1,0:T(8,128)(2,1)} %param.7, bf16[64,3456]{1,0:T(8,128)(2,1)S(1)} %constant_dynamic-slice_fusion.1.refs_0_, bf16[64,3456]{1,0:T(8,128)(2,1)S(1)} %collective-permute-done.2.refs_1_), kind=kOutput, calls=%fused_computation.1 | convolution fusion | flops 681246720 | bytes 6586368 | tf_op jit(solution)/shard_map/dot_general | solution.py:608
  19.3 0.5 collective-permute-start.5
  19.8 0.9 fusion.26
  20.9 4.5 %collective-permute-done.refs_2_ = bf16[64,3456]{1,0:T(8,128)(2,1)S(1)} collective-permute-done((bf16[64,3456]{1,0:T(8,128)(2,1)S(1)}, bf16[64,3456]{1,0:T(8,128)(2,1)S(1)}, u32[]{:S(2)}, u32[]{:S(2)}) %collective-permute-start) | collective-permute-done | bytes 442400 | tf_op jit(solution)/shard_map/ppermute | solution.py:593
  25.4 0.9 convolution_add_fusion
  26.3 0.7 fusion.5
  27.0 7.1 %all-to-all-start = ((bf16[16,8,768]{2,1,0:T(8,128)(2,1)}), bf16[16,8,768]{2,1,0:T(8,128)(2,1)S(1)}, u32[]{:S(2)}, u32[]{:S(2)}) async-start(bf16[16,8,768]{2,1,0:T(8,128)(2,1)} %fusion.5), calls=%async_computation | async-start | bytes 393216 | tf_op jit(solution)/shard_map/all_to_all | solution.py:561
  34.1 4.7 %shard_map.94.features = bf16[3456,256]{1,0:T(8,128)(2,1)} custom-call(s32[1]{0:T(128)} %bitcast.2.place_ref, bf16[64,3456]{1,0:T(8,128)(2,1)} %copy-done.6, bf16[64,3456]{1,0:T(8,128)(2,1)} %copy-done.7, bf16[64,3456]{1,0:T(8,128)(2,1)} %copy-done.9, bf16[64,3456]{1,0:T(8,128)(2,1)} %copy-done.8), custom_call_target="tpu_custom_call" | custom-call | bytes 3538944 | tf_op jit(solution)/shard_map/pallas_call | solution.py:444
  38.8 3.5 %all-to-all-done = bf16[16,8,768]{2,1,0:T(8,128)(2,1)S(1)} async-done(((bf16[16,8,768]{2,1,0:T(8,128)(2,1)}), bf16[16,8,768]{2,1,0:T(8,128)(2,1)S(1)}, u32[]{:S(2)}, u32[]{:S(2)}) %all-to-all-start) | async-done | bytes 196640 | tf_op jit(solution)/shard_map/all_to_all | solution.py:561
  42.4 11.3 %all_to_all.20 = bf16[16,8,768]{2,1,0:T(8,128)(2,1)S(1)} all-to-all(bf16[16,8,768]{2,1,0:T(8,128)(2,1)S(1)} %broadcast_in_dim.4), channel_id=1, replica_groups=mesh['row'=2,'core'=2,'gy'=8] {'row','gy'}, dimensions={0} | all-to-all | bytes 393216 | tf_op jit(solution)/shard_map/all_to_all | solution.py:561
  53.7 1.4 %collective-permute-done.6.hid_b_hbm.hid_b = bf16[128,768]{1,0:T(8,128)(2,1)S(1)} collective-permute-done((bf16[128,768]{1,0:T(8,128)(2,1)S(1)}, bf16[128,768]{1,0:T(8,128)(2,1)S(1)}, u32[]{:S(2)}, u32[]{:S(2)}) %collective-permute-start.6) | collective-permute-done | bytes 196640 | tf_op jit(solution)/shard_map/ppermute | solution.py:557
  55.1 5.6 %shard_map.95 = (f32[136,512]{1,0:T(8,128)S(1)}, f32[136,512]{1,0:T(8,128)S(1)}, bf16[24320,512]{1,0:T(8,128)(2,1)}) custom-call(bf16[128,768]{1,0:T(8,128)(2,1)S(1)} %bitcast.18, bf16[128,768]{1,0:T(8,128)(2,1)S(1)} %collective-permute-done.6.hid_b_hbm.hid_b, bf16[768,512]{1,0:T(8,128)(2,1)S(1)} %copy-done.1, ...), custom_call_target="tpu_custom_call", output_to_operand_aliasing={{2}: (5, {})} | custom-call | flops 2550136832 | bytes 9961472 | tf_op jit(solution)/shard_map/pallas_call | solution.py:229
  60.8 0.2 collective-permute-start.7
  61.0 1.4 %collective-permute-done.7.got = f32[136,512]{1,0:T(8,128)S(1)} collective-permute-done((f32[136,512]{1,0:T(8,128)S(1)}, f32[136,512]{1,0:T(8,128)S(1)}, u32[]{:S(2)}, u32[]{:S(2)}) %collective-permute-start.7) | collective-permute-done | bytes 278560 | tf_op jit(solution)/shard_map/ppermute | solution.py:557
  62.4 0.8 shard_map.96
  63.2 3.7 %all-to-all-start.2 = ((bf16[16,8,1280]{2,1,0:T(8,128)(2,1)}), bf16[16,8,1280]{2,1,0:T(8,128)(2,1)S(1)}, u32[]{:S(2)}, u32[]{:S(2)}) async-start(bf16[16,8,1280]{2,1,0:T(8,128)(2,1)} %bitcast.4), calls=%async_computation.2 | async-start | bytes 655360 | tf_op jit(solution)/shard_map/all_to_all | solution.py:561
  66.9 0.3 multiply_reduce_fusion.1
  67.2 6.3 %shard_map.97.terms_hbm = bf16[4864,256]{1,0:T(8,128)(2,1)} custom-call(s32[1,256]{1,0:T(1,128)} %copy-done.4, s32[4,1216]{1,0:T(4,128)} %copy-done.3, bf16[24320,512]{1,0:T(8,128)(2,1)} %get-tuple-element.54.shared_hbm), custom_call_target="tpu_custom_call" | custom-call | flops 1275068416 | bytes 19922944 | tf_op jit(solution)/shard_map/pallas_call | solution.py:320
  73.6 5.0 %all-to-all-done.2 = bf16[16,8,1280]{2,1,0:T(8,128)(2,1)S(1)} async-done(((bf16[16,8,1280]{2,1,0:T(8,128)(2,1)}), bf16[16,8,1280]{2,1,0:T(8,128)(2,1)S(1)}, u32[]{:S(2)}, u32[]{:S(2)}) %all-to-all-start.2) | async-done | bytes 327712 | tf_op jit(solution)/shard_map/all_to_all | solution.py:561
  79.1 0.7 broadcast_in_dim.5
  79.7 3.5 %all-to-all-start.3 = ((bf16[16,8,512]{2,1,0:T(8,128)(2,1)}), bf16[16,8,512]{2,1,0:T(8,128)(2,1)S(1)}, u32[]{:S(2)}, u32[]{:S(2)}) async-start(bf16[16,8,512]{2,1,0:T(8,128)(2,1)} %broadcast_in_dim.5), calls=%async_computation.3 | async-start | bytes 262144 | tf_op jit(solution)/shard_map/all_to_all | solution.py:561
  83.3 7.9 %shard_map.98 = (bf16[4864,512]{1,0:T(8,128)(2,1)}, f32[1,1]{1,0:T(1,128)}) custom-call(f32[2,256]{1,0:T(2,128)} %copy-done.10, bf16[4864,512]{1,0:T(8,128)(2,1)} %cen_hbm.3, bf16[24320,512]{1,0:T(8,128)(2,1)} %get-tuple-element.54.shared_hbm, bf16[4864,256]{1,0:T(8,128)(2,1)} %shard_map.97.terms_hbm), custom_call_target="tpu_custom_call" | custom-call | flops 2550136832 | bytes 19922944 | tf_op jit(solution)/shard_map/pallas_call | solution.py:396
  91.3 1.3 %collective-permute-done.8.grad_b = bf16[128,512]{1,0:T(8,128)(2,1)S(1)} collective-permute-done((bf16[128,512]{1,0:T(8,128)(2,1)S(1)}, bf16[128,512]{1,0:T(8,128)(2,1)S(1)}, u32[]{:S(2)}, u32[]{:S(2)}) %collective-permute-start.8) | collective-permute-done | bytes 131104 | tf_op jit(solution)/shard_map/ppermute | solution.py:557
  92.6 4.4 %shard_map.99 = (bf16[3456,768]{1,0:T(8,128)(2,1)}, bf16[768,512]{1,0:T(8,128)(2,1)}) custom-call(bf16[128,512]{1,0:T(8,128)(2,1)S(1)} %bitcast.21, bf16[128,512]{1,0:T(8,128)(2,1)S(1)} %collective-permute-done.8.grad_b, bf16[128,768]{1,0:T(8,128)(2,1)S(1)} %bitcast.19, bf16[128,768]{1,0:T(8,128)(2,1)S(1)} %collective-permute-done.6.hid_b_hbm.hid_b, ...), custom_call_target="tpu_custom_call" | custom-call | flops 1358954496 | bytes 7077888 | tf_op jit(solution)/shard_map/pallas_call | solution.py:499
  (52 shorter events, 1.3 us)
Async XLA Ops:
  2.1 6.0 %collective-permute-start.2 = (bf16[64,3456]{1,0:T(8,128)(2,1)S(1)}, bf16[64,3456]{1,0:T(8,128)(2,1)S(1)}, u32[]{:S(2)}, u32[]{:S(2)}) collective-permute-start(bf16[64,3456]{1,0:T(8,128)(2,1)S(1)} %get-tuple-element.64), channel_id=1, source_target_pairs={{0,8},{8,0},{16,24},{24,16},{1,9},{9,1},{17,25},{25,17},{2,10},{10... | collective-permute-start | bytes 1327112 | tf_op jit(solution)/shard_map/ppermute | solution.py:593
  2.6 16.7 %collective-permute-start.1 = (bf16[64,3456]{1,0:T(8,128)(2,1)S(1)}, bf16[64,3456]{1,0:T(8,128)(2,1)S(1)}, u32[]{:S(2)}, u32[]{:S(2)}) collective-permute-start(bf16[64,3456]{1,0:T(8,128)(2,1)S(1)} %get-tuple-element.65), channel_id=1, source_target_pairs={{0,24},{8,16},{16,8},{24,0},{1,25},{9,17},{17,9},{25,1},{2,26},{10... | collective-permute-start | bytes 1327112 | tf_op jit(solution)/shard_map/ppermute | solution.py:593
  5.2 20.2 %collective-permute-start = (bf16[64,3456]{1,0:T(8,128)(2,1)S(1)}, bf16[64,3456]{1,0:T(8,128)(2,1)S(1)}, u32[]{:S(2)}, u32[]{:S(2)}) collective-permute-start(bf16[64,3456]{1,0:T(8,128)(2,1)S(1)} %get-tuple-element.66), channel_id=1, source_target_pairs={{0,16},{8,24},{16,0},{24,8},{1,17},{9,25},{17,1},{25,9},{2,18},{10... | collective-permute-start | bytes 1327112 | tf_op jit(solution)/shard_map/ppermute | solution.py:593
  6.1 49.0 %copy-start.3 = (s32[4,1216]{1,0:T(4,128)}, s32[4,1216]{1,0:T(4,128)S(1)}, u32[]{:S(2)}) copy-start(s32[4,1216]{1,0:T(4,128)S(1)} %reshape.50.classes.classes_hbm) | copy-start | bytes 58372
  7.0 48.1 %copy-start.4 = (s32[1,256]{1,0:T(1,128)}, s32[1,256]{1,0:T(1,128)S(1)}, u32[]{:S(2)}) copy-start(s32[1,256]{1,0:T(1,128)S(1)} %broadcast_in_dim_reshape.3.marks.marks_hbm) | copy-start | bytes 3076
  8.0 11.2 %copy-start.6 = (bf16[64,3456]{1,0:T(8,128)(2,1)}, bf16[64,3456]{1,0:T(8,128)(2,1)S(1)}, u32[]{:S(2)}) copy-start(bf16[64,3456]{1,0:T(8,128)(2,1)S(1)} %constant_dynamic-slice_fusion.1.refs_0_) | copy-start | bytes 1327108
  8.1 2.6 %copy-start = (bf16[4864,512]{1,0:T(8,128)(2,1)S(1)}, bf16[4864,512]{1,0:T(8,128)(2,1)}, u32[]{:S(2)}) copy-start(bf16[4864,512]{1,0:T(8,128)(2,1)} %cen_hbm.3) | copy-start | bytes 14942212
  10.6 8.6 %copy-start.7 = (bf16[64,3456]{1,0:T(8,128)(2,1)}, bf16[64,3456]{1,0:T(8,128)(2,1)S(1)}, u32[]{:S(2)}) copy-start(bf16[64,3456]{1,0:T(8,128)(2,1)S(1)} %collective-permute-done.2.refs_1_) | copy-start | bytes 1327108
  10.6 9.1 %copy-start.5 = (bf16[3456,768]{1,0:T(8,128)(2,1)S(1)}, bf16[3456,768]{1,0:T(8,128)(2,1)}, u32[]{:S(2)}) copy-start(bf16[3456,768]{1,0:T(8,128)(2,1)} %param.7) | copy-start | bytes 15925252
  15.6 3.7 %collective-permute-start.3 = (bf16[128,512]{1,0:T(8,128)(2,1)S(1)}, bf16[128,512]{1,0:T(8,128)(2,1)S(1)}, u32[]{:S(2)}, u32[]{:S(2)}) collective-permute-start(bf16[128,512]{1,0:T(8,128)(2,1)S(1)} %slice.25), channel_id=1, source_target_pairs={{0,8},{8,0},{1,9},{9,1},{2,10},{10,2},{3,11},{11,3},{4,12},{12,4},... | collective-permute-start | bytes 393224 | tf_op jit(solution)/shard_map/ppermute | solution.py:557
  19.3 7.1 %copy-start.8 = (bf16[64,3456]{1,0:T(8,128)(2,1)}, bf16[64,3456]{1,0:T(8,128)(2,1)S(1)}, u32[]{:S(2)}) copy-start(bf16[64,3456]{1,0:T(8,128)(2,1)S(1)} %collective-permute-done.1.refs_3_) | copy-start | bytes 1327108
  19.3 1.6 %collective-permute-start.5 = (f32[64,768]{1,0:T(8,128)S(1)}, f32[64,768]{1,0:T(8,128)S(1)}, u32[]{:S(2)}, u32[]{:S(2)}) collective-permute-start(f32[64,768]{1,0:T(8,128)S(1)} %slice.27), channel_id=1, source_target_pairs={{0,8},{8,0},{1,9},{9,1},{2,10},{10,2},{3,11},{11,3},{4,12},{12,4},... | collective-permute-start | bytes 589832 | tf_op jit(solution)/shard_map/ppermute | solution.py:557
  20.7 4.8 %collective-permute-start.4 = (f32[64,768]{1,0:T(8,128)S(1)}, f32[64,768]{1,0:T(8,128)S(1)}, u32[]{:S(2)}, u32[]{:S(2)}) collective-permute-start(f32[64,768]{1,0:T(8,128)S(1)} %fusion.26), channel_id=1, source_target_pairs={{0,8},{8,0},{1,9},{9,1},{2,10},{10,2},{3,11},{11,3},{4,12},{12,4},... | collective-permute-start | bytes 589832 | tf_op jit(solution)/shard_map/ppermute | solution.py:557
  20.9 34.3 %copy-start.1 = (bf16[768,512]{1,0:T(8,128)(2,1)S(1)}, bf16[768,512]{1,0:T(8,128)(2,1)}, u32[]{:S(2)}) copy-start(bf16[768,512]{1,0:T(8,128)(2,1)} %second.1) | copy-start | bytes 2359300
  25.4 8.7 %copy-start.9 = (bf16[64,3456]{1,0:T(8,128)(2,1)}, bf16[64,3456]{1,0:T(8,128)(2,1)S(1)}, u32[]{:S(2)}) copy-start(bf16[64,3456]{1,0:T(8,128)(2,1)S(1)} %collective-permute-done.refs_2_) | copy-start | bytes 1327108
  27.0 15.3 %all-to-all-start = ((bf16[16,8,768]{2,1,0:T(8,128)(2,1)}), bf16[16,8,768]{2,1,0:T(8,128)(2,1)S(1)}, u32[]{:S(2)}, u32[]{:S(2)}) async-start(bf16[16,8,768]{2,1,0:T(8,128)(2,1)} %fusion.5), calls=%async_computation | async-start | bytes 393216 | tf_op jit(solution)/shard_map/all_to_all | solution.py:561
  53.7 1.4 %collective-permute-start.6 = (bf16[128,768]{1,0:T(8,128)(2,1)S(1)}, bf16[128,768]{1,0:T(8,128)(2,1)S(1)}, u32[]{:S(2)}, u32[]{:S(2)}) collective-permute-start(bf16[128,768]{1,0:T(8,128)(2,1)S(1)} %bitcast.17), channel_id=1, source_target_pairs={{0,8},{8,0},{1,9},{9,1},{2,10},{10,2},{3,11},{11,3},{4,12},{12,4},... | collective-permute-start | bytes 589832 | tf_op jit(solution)/shard_map/ppermute | solution.py:557
  60.8 1.6 %collective-permute-start.7 = (f32[136,512]{1,0:T(8,128)S(1)}, f32[136,512]{1,0:T(8,128)S(1)}, u32[]{:S(2)}, u32[]{:S(2)}) collective-permute-start(f32[136,512]{1,0:T(8,128)S(1)} %get-tuple-element.50), channel_id=1, source_target_pairs={{0,8},{8,0},{1,9},{9,1},{2,10},{10,2},{3,11},{11,3},{4,12},{12,4},... | collective-permute-start | bytes 835592 | tf_op jit(solution)/shard_map/ppermute | solution.py:557
  63.2 15.4 %all-to-all-start.2 = ((bf16[16,8,1280]{2,1,0:T(8,128)(2,1)}), bf16[16,8,1280]{2,1,0:T(8,128)(2,1)S(1)}, u32[]{:S(2)}, u32[]{:S(2)}) async-start(bf16[16,8,1280]{2,1,0:T(8,128)(2,1)} %bitcast.4), calls=%async_computation.2 | async-start | bytes 655360 | tf_op jit(solution)/shard_map/all_to_all | solution.py:561
  78.7 4.6 %copy-start.10 = (f32[2,256]{1,0:T(2,128)}, f32[2,256]{1,0:T(2,128)S(1)}, u32[]{:S(2)}) copy-start(f32[2,256]{1,0:T(2,128)S(1)} %reduce_sum.50.sums_hbm) | copy-start | bytes 6148
  79.7 11.5 %all-to-all-start.3 = ((bf16[16,8,512]{2,1,0:T(8,128)(2,1)}), bf16[16,8,512]{2,1,0:T(8,128)(2,1)S(1)}, u32[]{:S(2)}, u32[]{:S(2)}) async-start(bf16[16,8,512]{2,1,0:T(8,128)(2,1)} %broadcast_in_dim.5), calls=%async_computation.3 | async-start | bytes 262144 | tf_op jit(solution)/shard_map/all_to_all | solution.py:561
  83.3 9.4 %copy-start.2 = (bf16[3456,256]{1,0:T(8,128)(2,1)S(1)}, bf16[3456,256]{1,0:T(8,128)(2,1)}, u32[]{:S(2)}) copy-start(bf16[3456,256]{1,0:T(8,128)(2,1)} %shard_map.94.features) | copy-start | bytes 5308420
  91.2 1.4 %collective-permute-start.8 = (bf16[128,512]{1,0:T(8,128)(2,1)S(1)}, bf16[128,512]{1,0:T(8,128)(2,1)S(1)}, u32[]{:S(2)}, u32[]{:S(2)}) collective-permute-start(bf16[128,512]{1,0:T(8,128)(2,1)S(1)} %bitcast.20), channel_id=1, source_target_pairs={{0,8},{8,0},{1,9},{9,1},{2,10},{10,2},{3,11},{11,3},{4,12},{12,4},... | collective-permute-start | bytes 393224 | tf_op jit(solution)/shard_map/ppermute | solution.py:557

commit v7 on v6

--- a/solution.py
+++ b/solution.py
@@ -339,13 +339,13 @@
 
 def centres_kernel(
     factor,
-    sums_hbm,
+    sent_hbm,
     cen_hbm,
     shared_hbm,
     terms_hbm,
     out_hbm,
     loss,
-    sums,
+    sent,
     unit,
     cen,
     terms,
@@ -358,7 +358,7 @@
     count = cen.shape[0]
     tile = count // steps
     firsts = [
-        pltpu.make_async_copy(sums_hbm, sums, first_sem.at[0]),
+        pltpu.make_async_copy(sent_hbm, sent, first_sem.at[0]),
         pltpu.make_async_copy(shared_hbm.at[pl.ds(count, unit.shape[0])], unit, first_sem.at[1]),
     ]
     load, loaded = chunked(steps, tile, [(cen_hbm, cen), (terms_hbm, terms)], in_sem)
@@ -369,7 +369,10 @@
         load(i)
     for copy in firsts:
         copy.wait()
-    totals, target = sums[0:1, :] * (1.0 / PIECE_SCALE), sums[1:2, :]
+    width = unit.shape[1]
+    riding = sent[:, width : width + unit.shape[0] // 2]
+    halves = [riding[r : r + 1, :] + riding[r + 2 : r + 3, :] + riding[r + 4 : r + 5, :] for r in range(2)]
+    totals = jnp.concatenate(halves, axis=1) * (1.0 / PIECE_SCALE)
     share = factor / totals
     for i in range(steps):
         loaded(i)
@@ -384,12 +387,12 @@
         along = jnp.sum(grad * block, axis=1, keepdims=True) * (inv * inv)
         out[rows, :] = (inv * (grad - block * along)).astype(BF16)
         store(i)
-    loss[0, 0] = jnp.sum(LOGIT_SCALE + jnp.log(totals) - target) / totals.shape[1]
+    loss[0, 0] = (jnp.sum(LOGIT_SCALE + jnp.log(totals)) - jnp.sum(riding[6:7, :])) / totals.shape[1]
     for i in range(steps):
         stored(i)
 
 
-def grad_centres(centres, terms, shared, sums):
+def grad_centres(centres, terms, shared, sent):
     count, width = centres.shape
     images = terms.shape[1]
     steps = count // tile_of(count, 640)
@@ -402,7 +405,7 @@
             jax.ShapeDtypeStruct((1, 1), F32),
         ],
         scratch_shapes=[
-            pltpu.VMEM((2, images), F32),
+            pltpu.VMEM(sent.shape, F32),
             pltpu.VMEM((images, width), BF16),
             pltpu.VMEM((count, width), BF16),
             pltpu.VMEM((count, images), BF16),
@@ -413,7 +416,7 @@
         ],
         compiler_params=params(57),
         cost_estimate=cost(4 * count * width * images, 8 * count * width),
-    )(sums, centres, shared, terms)
+    )(sent, centres, shared, terms)
 
 
 def turn_kernel(rows, place_ref, *refs):
@@ -528,17 +531,21 @@
 
     other = sums(got)
     both = sums(keep) + jnp.concatenate([other[:, images // 2 :], other[:, : images // 2]], axis=1)
-    scale = jnp.where(lax.broadcasted_iota(jnp.int32, both.shape, 0) == 0, PIECE_SCALE, 1.0)
-    both = both * scale
-    parts = []
-    for _ in range(3):
-        part = both.astype(BF16).astype(F32)
-        parts.append(part)
-        both = both - part
-    riding = jnp.concatenate(parts + [jnp.zeros_like(both)])
+    total = both[0:1, :] * PIECE_SCALE
+    target = jnp.broadcast_to(jnp.sum(both[1:2, :], axis=1, keepdims=True), (1, half))
+    lane = lax.broadcasted_iota(jnp.int32, (1, half), 1)
+    lines, last = [], jnp.zeros((1, half), F32)
+    for i in range(3):
+        part = total.astype(BF16).astype(F32)
+        lines += [part[:, :half], part[:, half:]]
+        total = total - part
+        part = target.astype(BF16).astype(F32)
+        last = jnp.where(lane == i, part, last)
+        target = target - part
+    riding = jnp.concatenate(lines + [last, jnp.zeros_like(last)])
     out[:, :width] = (keep[:half, :] + got[:half, :]).astype(BF16)
-    out[:, width : width + images] = jnp.concatenate([riding] * (half // 8)).astype(BF16)
-    out[:, width + images :] = picked[...]
+    out[:, width : width + half] = jnp.concatenate([riding] * (half // 8)).astype(BF16)
+    out[:, width + half :] = picked[...]
 
 
 def assemble(images, keep, got, picked):
@@ -547,7 +554,7 @@
         functools.partial(assemble_kernel, images),
         in_specs=[VMEM] * 3,
         out_specs=VMEM,
-        out_shape=jax.ShapeDtypeStruct((half, width + images + picked.shape[1]), BF16),
+        out_shape=jax.ShapeDtypeStruct((half, width + half + picked.shape[1]), BF16),
         compiler_params=params(16),
         cost_estimate=cost(0, 8 * half * (width + images)),
     )(keep, got, picked)
@@ -658,10 +665,10 @@
     terms = turned_terms(classes, marks, shared)
     sent, terms = lax.optimization_barrier((to_chips(sent.reshape(chips, own, -1)), terms))
     sent = jnp.sum(sent.astype(F32), axis=0)
-    weighted, riding = sent[:, :width], sent[:, width : width + image_count]
-    picked = sent[:, width + image_count :]
-    sums = riding.reshape(4, 2, image_count).sum(axis=0)
-    totals = sums[0:1] * (1.0 / PIECE_SCALE)
+    weighted, riding = sent[:, :width], sent[:, width : width + half]
+    picked = sent[:, width + half :]
+    totals = riding[:6].reshape(3, image_count).sum(axis=0, keepdims=True)
+    totals = totals * (1.0 / PIECE_SCALE)
 
     factor = LOGIT_SCALE / image_count
     totals_own = lax.dynamic_slice_in_dim(totals, chip * own, own, axis=1).reshape(own, 1)
@@ -669,9 +676,9 @@
     grad_embed = inv_own * (grad_unit - unit_own * jnp.sum(grad_unit * unit_own, axis=1, keepdims=True))
     grad_embed = grad_embed.astype(BF16)
     grad_embed = jnp.broadcast_to(grad_embed[None], (chips,) + grad_embed.shape)
-    grad_cen, loss = grad_centres(centres, terms, shared, sums)
+    grad_cen, loss = grad_centres(centres, terms, shared, sent)
     grad_a = to_chips(grad_embed).reshape(half, -1)
-    grad_a, grad_cen = lax.optimization_barrier((grad_a, grad_cen))
+    grad_a, grad_cen, turned_features = lax.optimization_barrier((grad_a, grad_cen, turned_features))
     grad_b = core_swap(grad_a)
     grad_first, grad_second = tail(grad_a, grad_b, hid_a, hid_b, second_weight, turned_features)
     return loss.reshape(()), grad_first, grad_second, grad_cen

time: 97.9 us -> 97.3 us (level)
  no operation moved by 1% of the time
where the time goes in v7:
time: 97.3 us; the launch traced here: 96.5 us
  Pallas kernels  34.7 us (36%)
  starting transfers between devices  18.6 us (19%)
  waiting for transfers between devices  16.6 us (17%)
  blocking collectives  11.3 us (12%)
  local copies, waits for them, and re-layouts  6.81 us (7%)
  matrix products  5.54 us (6%)
  other arithmetic  1.88 us (2%)
  between operations  1.13 us (1%)
    all_to_all x3, starting transfers between devices, to_chips(): return lax.all_to_all(x, ('row', 'gy'), 0, 0, tiled=True)  14.3 us
    all_to_all x1, blocking collectives, to_chips(): return lax.all_to_all(x, ('row', 'gy'), 0, 0, tiled=True)  11.3 us
    pallas_call x1, Pallas kernels, grad_centres(): pl.pallas_call(functools.partial(centres_kernel, LOGIT_SCALE / images), i...  7.93 us
    all_to_all x3, waiting for transfers between devices, to_chips(): return lax.all_to_all(x, ('row', 'gy'), 0, 0, tiled=True)  7.83 us
    pallas_call x1, Pallas kernels, turned_terms(): pl.pallas_call(terms_kernel, in_specs=[HBM] * 3, out_specs=HBM, out_shape...  6.33 us
    pallas_call x1, Pallas kernels, softmax_sums(): pl.pallas_call(functools.partial(softmax_kernel, images <= 256), in_specs...  5.61 us
    dot_general x3, matrix products, partial_hidden(): jnp.dot(jnp.concatenate([blocks[n] for n in names]), first_weight, prefer...  5.22 us
    pallas_call x1, Pallas kernels, prep(): pl.pallas_call(functools.partial(prep_kernel, images <= 256), in_specs=[V...  4.9 us
  transfers between devices with their start and end apart: 12, of which 6 were waited for; matrix products, arithmetic and copies ran while one was open for 8% of the time, Pallas kernels for 25%

profile of v7, /device:TPU:0, one launch (start us, length us, event | category | flops | bytes accessed | tf_op | source)
XLA Modules:
  0.0 96.5 jit_solution(12155472109647873634)
XLA Ops:
  0.7 1.4 %constant_dynamic-slice_fusion.1 = (bf16[64,3456]{1,0:T(8,128)(2,1)S(1)}, bf16[64,3456]{1,0:T(8,128)(2,1)S(1)}, bf16[64,3456]{1,0:T(8,128)(2,1)S(1)}) fusion(bf16[64,13824]{1,0:T(8,128)(2,1)} %param.6, s32[]{:T(128)S(6)} %select_n.53, s32[]{:T(128)S(6)} %select_n.51, s32[]{:T(128)S(6)} %select_n.50), kind=kLoop, calls=%fused_computation.35 | loop fusion | bytes 2654220 | tf_op jit(solution)/shard_map/dynamic_slice | solution.py:596
  2.1 0.5 collective-permute-start.2
  2.6 2.6 %collective-permute-start.1 = (bf16[64,3456]{1,0:T(8,128)(2,1)S(1)}, bf16[64,3456]{1,0:T(8,128)(2,1)S(1)}, u32[]{:S(2)}, u32[]{:S(2)}) collective-permute-start(bf16[64,3456]{1,0:T(8,128)(2,1)S(1)} %get-tuple-element.67), channel_id=1, source_target_pairs={{0,24},{8,16},{16,8},{24,0},{1,25},{9,17},{17,9},{25,1},{2,26},{10... | collective-permute-start | bytes 1327112 | tf_op jit(solution)/shard_map/ppermute | solution.py:600
  5.3 0.7 broadcast_add_fusion
  6.1 0.8 reshape.61
  7.0 1.0 %constant_dynamic-slice_fusion.refs_0_ = bf16[64,3456]{1,0:T(8,128)(2,1)S(1)} fusion(bf16[64,13824]{1,0:T(8,128)(2,1)} %param.6, s32[]{:T(128)S(6)} %select_n.56), kind=kLoop, calls=%fused_computation.34 | loop fusion | bytes 884740 | tf_op jit(solution)/shard_map/dynamic_slice | solution.py:594
  8.1 2.6 %copy-done = bf16[4864,512]{1,0:T(8,128)(2,1)S(1)} copy-done((bf16[4864,512]{1,0:T(8,128)(2,1)S(1)}, bf16[4864,512]{1,0:T(8,128)(2,1)}, u32[]{:S(2)}) %copy-start) | copy-done | bytes 4980760
  10.6 4.9 %shard_map.93 = (bf16[24320,512]{1,0:T(8,128)(2,1)}, bf16[256,512]{1,0:T(8,128)(2,1)S(1)}) custom-call(s32[1,256]{1,0:T(1,128)S(1)} %broadcast_in_dim_reshape.3.marks.marks_hbm, s32[4,1216]{1,0:T(4,128)S(1)} %reshape.62.classes.classes_hbm, bf16[4864,512]{1,0:T(8,128)(2,1)S(1)} %copy-done), custom_call_target="tpu_custom_call" | custom-call | flops 1275068416 | bytes 19922944 | tf_op jit(solution)/shard_map/pallas_call | solution.py:122
  15.7 3.4 %fusion = f32[128,768]{1,0:T(8,128)S(1)} fusion(bf16[3456,768]{1,0:T(8,128)(2,1)} %param.7, bf16[64,3456]{1,0:T(8,128)(2,1)S(1)} %constant_dynamic-slice_fusion.refs_0_, bf16[64,3456]{1,0:T(8,128)(2,1)S(1)} %collective-permute-done.2.refs_1_), kind=kOutput, calls=%fused_computation.1 | convolution fusion | flops 681246720 | bytes 6586368 | tf_op jit(solution)/shard_map/dot_general | solution.py:615
  19.3 0.5 collective-permute-start.5
  19.8 0.9 fusion.24
  20.9 4.5 %collective-permute-done.refs_2_ = bf16[64,3456]{1,0:T(8,128)(2,1)S(1)} collective-permute-done((bf16[64,3456]{1,0:T(8,128)(2,1)S(1)}, bf16[64,3456]{1,0:T(8,128)(2,1)S(1)}, u32[]{:S(2)}, u32[]{:S(2)}) %collective-permute-start) | collective-permute-done | bytes 442400 | tf_op jit(solution)/shard_map/ppermute | solution.py:600
  25.4 0.9 convolution_add_fusion
  26.3 0.7 fusion.5
  27.0 7.1 %all-to-all-start = ((bf16[16,8,768]{2,1,0:T(8,128)(2,1)}), bf16[16,8,768]{2,1,0:T(8,128)(2,1)S(1)}, u32[]{:S(2)}, u32[]{:S(2)}) async-start(bf16[16,8,768]{2,1,0:T(8,128)(2,1)} %fusion.5), calls=%async_computation | async-start | bytes 393216 | tf_op jit(solution)/shard_map/all_to_all | solution.py:568
  34.1 4.7 %shard_map.94.features = bf16[3456,256]{1,0:T(8,128)(2,1)} custom-call(s32[1]{0:T(128)} %bitcast.2.place_ref, bf16[64,3456]{1,0:T(8,128)(2,1)} %copy-done.6, bf16[64,3456]{1,0:T(8,128)(2,1)} %copy-done.7, bf16[64,3456]{1,0:T(8,128)(2,1)} %copy-done.9, bf16[64,3456]{1,0:T(8,128)(2,1)} %copy-done.8), custom_call_target="tpu_custom_call" | custom-call | bytes 3538944 | tf_op jit(solution)/shard_map/pallas_call | solution.py:447
  38.8 3.5 %all-to-all-done = bf16[16,8,768]{2,1,0:T(8,128)(2,1)S(1)} async-done(((bf16[16,8,768]{2,1,0:T(8,128)(2,1)}), bf16[16,8,768]{2,1,0:T(8,128)(2,1)S(1)}, u32[]{:S(2)}, u32[]{:S(2)}) %all-to-all-start) | async-done | bytes 196640 | tf_op jit(solution)/shard_map/all_to_all | solution.py:568
  42.4 11.3 %all_to_all.20 = bf16[16,8,768]{2,1,0:T(8,128)(2,1)S(1)} all-to-all(bf16[16,8,768]{2,1,0:T(8,128)(2,1)S(1)} %broadcast_in_dim.4), channel_id=1, replica_groups=mesh['row'=2,'core'=2,'gy'=8] {'row','gy'}, dimensions={0} | all-to-all | bytes 393216 | tf_op jit(solution)/shard_map/all_to_all | solution.py:568
  53.7 1.4 %collective-permute-done.6.hid_b_hbm.hid_b = bf16[128,768]{1,0:T(8,128)(2,1)S(1)} collective-permute-done((bf16[128,768]{1,0:T(8,128)(2,1)S(1)}, bf16[128,768]{1,0:T(8,128)(2,1)S(1)}, u32[]{:S(2)}, u32[]{:S(2)}) %collective-permute-start.6) | collective-permute-done | bytes 196640 | tf_op jit(solution)/shard_map/ppermute | solution.py:564
  55.1 5.6 %shard_map.95 = (f32[136,512]{1,0:T(8,128)S(1)}, f32[136,512]{1,0:T(8,128)S(1)}, bf16[24320,512]{1,0:T(8,128)(2,1)}) custom-call(bf16[128,768]{1,0:T(8,128)(2,1)S(1)} %bitcast.16, bf16[128,768]{1,0:T(8,128)(2,1)S(1)} %collective-permute-done.6.hid_b_hbm.hid_b, bf16[768,512]{1,0:T(8,128)(2,1)S(1)} %copy-done.1, ...), custom_call_target="tpu_custom_call", output_to_operand_aliasing={{2}: (5, {})} | custom-call | flops 2550136832 | bytes 9961472 | tf_op jit(solution)/shard_map/pallas_call | solution.py:229
  60.8 0.2 collective-permute-start.7
  61.0 1.4 %collective-permute-done.7.got = f32[136,512]{1,0:T(8,128)S(1)} collective-permute-done((f32[136,512]{1,0:T(8,128)S(1)}, f32[136,512]{1,0:T(8,128)S(1)}, u32[]{:S(2)}, u32[]{:S(2)}) %collective-permute-start.7) | collective-permute-done | bytes 278560 | tf_op jit(solution)/shard_map/ppermute | solution.py:564
  62.4 0.8 shard_map.96
  63.2 3.7 %all-to-all-start.2 = ((bf16[16,8,1152]{2,1,0:T(8,128)(2,1)}), bf16[16,8,1152]{2,1,0:T(8,128)(2,1)S(1)}, u32[]{:S(2)}, u32[]{:S(2)}) async-start(bf16[16,8,1152]{2,1,0:T(8,128)(2,1)} %bitcast.4), calls=%async_computation.2 | async-start | bytes 589824 | tf_op jit(solution)/shard_map/all_to_all | solution.py:568
  66.9 0.3 multiply_reduce_fusion.1
  67.3 6.3 %shard_map.97.terms_hbm = bf16[4864,256]{1,0:T(8,128)(2,1)} custom-call(s32[1,256]{1,0:T(1,128)} %copy-done.4, s32[4,1216]{1,0:T(4,128)} %copy-done.3, bf16[24320,512]{1,0:T(8,128)(2,1)} %get-tuple-element.55.shared_hbm), custom_call_target="tpu_custom_call" | custom-call | flops 1275068416 | bytes 19922944 | tf_op jit(solution)/shard_map/pallas_call | solution.py:320
  73.6 4.4 %all-to-all-done.2 = bf16[16,8,1152]{2,1,0:T(8,128)(2,1)S(1)} async-done(((bf16[16,8,1152]{2,1,0:T(8,128)(2,1)}), bf16[16,8,1152]{2,1,0:T(8,128)(2,1)S(1)}, u32[]{:S(2)}, u32[]{:S(2)}) %all-to-all-start.2) | async-done | bytes 294944 | tf_op jit(solution)/shard_map/all_to_all | solution.py:568
  78.4 0.7 broadcast_in_dim.5
  79.1 3.5 %all-to-all-start.3 = ((bf16[16,8,512]{2,1,0:T(8,128)(2,1)}), bf16[16,8,512]{2,1,0:T(8,128)(2,1)S(1)}, u32[]{:S(2)}, u32[]{:S(2)}) async-start(bf16[16,8,512]{2,1,0:T(8,128)(2,1)} %broadcast_in_dim.5), calls=%async_computation.3 | async-start | bytes 262144 | tf_op jit(solution)/shard_map/all_to_all | solution.py:568
  82.6 7.9 %shard_map.98 = (bf16[4864,512]{1,0:T(8,128)(2,1)}, f32[1,1]{1,0:T(1,128)}) custom-call(f32[8,1152]{1,0:T(8,128)} %copy-done.10, bf16[4864,512]{1,0:T(8,128)(2,1)} %cen_hbm.3, bf16[24320,512]{1,0:T(8,128)(2,1)} %get-tuple-element.55.shared_hbm, bf16[4864,256]{1,0:T(8,128)(2,1)} %shard_map.97.terms_hbm), custom_call_target="tpu_custom_call" | custom-call | flops 2550136832 | bytes 19922944 | tf_op jit(solution)/shard_map/pallas_call | solution.py:399
  90.7 1.3 %collective-permute-done.8.grad_b = bf16[128,512]{1,0:T(8,128)(2,1)S(1)} collective-permute-done((bf16[128,512]{1,0:T(8,128)(2,1)S(1)}, bf16[128,512]{1,0:T(8,128)(2,1)S(1)}, u32[]{:S(2)}, u32[]{:S(2)}) %collective-permute-start.8) | collective-permute-done | bytes 131104 | tf_op jit(solution)/shard_map/ppermute | solution.py:564
  92.0 4.4 %shard_map.99 = (bf16[3456,768]{1,0:T(8,128)(2,1)}, bf16[768,512]{1,0:T(8,128)(2,1)}) custom-call(bf16[128,512]{1,0:T(8,128)(2,1)S(1)} %bitcast.19, bf16[128,512]{1,0:T(8,128)(2,1)S(1)} %collective-permute-done.8.grad_b, bf16[128,768]{1,0:T(8,128)(2,1)S(1)} %bitcast.17, bf16[128,768]{1,0:T(8,128)(2,1)S(1)} %collective-permute-done.6.hid_b_hbm.hid_b, ...), custom_call_target="tpu_custom_call" | custom-call | flops 1358954496 | bytes 7077888 | tf_op jit(solution)/shard_map/pallas_call | solution.py:502
  (52 shorter events, 1.3 us)
Async XLA Ops:
  2.1 6.0 %collective-permute-start.2 = (bf16[64,3456]{1,0:T(8,128)(2,1)S(1)}, bf16[64,3456]{1,0:T(8,128)(2,1)S(1)}, u32[]{:S(2)}, u32[]{:S(2)}) collective-permute-start(bf16[64,3456]{1,0:T(8,128)(2,1)S(1)} %get-tuple-element.66), channel_id=1, source_target_pairs={{0,8},{8,0},{16,24},{24,16},{1,9},{9,1},{17,25},{25,17},{2,10},{10... | collective-permute-start | bytes 1327112 | tf_op jit(solution)/shard_map/ppermute | solution.py:600
  2.6 16.7 %collective-permute-start.1 = (bf16[64,3456]{1,0:T(8,128)(2,1)S(1)}, bf16[64,3456]{1,0:T(8,128)(2,1)S(1)}, u32[]{:S(2)}, u32[]{:S(2)}) collective-permute-start(bf16[64,3456]{1,0:T(8,128)(2,1)S(1)} %get-tuple-element.67), channel_id=1, source_target_pairs={{0,24},{8,16},{16,8},{24,0},{1,25},{9,17},{17,9},{25,1},{2,26},{10... | collective-permute-start | bytes 1327112 | tf_op jit(solution)/shard_map/ppermute | solution.py:600
  5.2 20.2 %collective-permute-start = (bf16[64,3456]{1,0:T(8,128)(2,1)S(1)}, bf16[64,3456]{1,0:T(8,128)(2,1)S(1)}, u32[]{:S(2)}, u32[]{:S(2)}) collective-permute-start(bf16[64,3456]{1,0:T(8,128)(2,1)S(1)} %get-tuple-element.68), channel_id=1, source_target_pairs={{0,16},{8,24},{16,0},{24,8},{1,17},{9,25},{17,1},{25,9},{2,18},{10... | collective-permute-start | bytes 1327112 | tf_op jit(solution)/shard_map/ppermute | solution.py:600
  6.1 49.0 %copy-start.3 = (s32[4,1216]{1,0:T(4,128)}, s32[4,1216]{1,0:T(4,128)S(1)}, u32[]{:S(2)}) copy-start(s32[4,1216]{1,0:T(4,128)S(1)} %reshape.62.classes.classes_hbm) | copy-start | bytes 58372
  7.0 48.1 %copy-start.4 = (s32[1,256]{1,0:T(1,128)}, s32[1,256]{1,0:T(1,128)S(1)}, u32[]{:S(2)}) copy-start(s32[1,256]{1,0:T(1,128)S(1)} %broadcast_in_dim_reshape.3.marks.marks_hbm) | copy-start | bytes 3076
  8.0 11.1 %copy-start.6 = (bf16[64,3456]{1,0:T(8,128)(2,1)}, bf16[64,3456]{1,0:T(8,128)(2,1)S(1)}, u32[]{:S(2)}) copy-start(bf16[64,3456]{1,0:T(8,128)(2,1)S(1)} %constant_dynamic-slice_fusion.refs_0_) | copy-start | bytes 1327108
  8.1 2.6 %copy-start = (bf16[4864,512]{1,0:T(8,128)(2,1)S(1)}, bf16[4864,512]{1,0:T(8,128)(2,1)}, u32[]{:S(2)}) copy-start(bf16[4864,512]{1,0:T(8,128)(2,1)} %cen_hbm.3) | copy-start | bytes 14942212
  10.6 8.6 %copy-start.7 = (bf16[64,3456]{1,0:T(8,128)(2,1)}, bf16[64,3456]{1,0:T(8,128)(2,1)S(1)}, u32[]{:S(2)}) copy-start(bf16[64,3456]{1,0:T(8,128)(2,1)S(1)} %collective-permute-done.2.refs_1_) | copy-start | bytes 1327108
  10.6 9.1 %copy-start.5 = (bf16[3456,768]{1,0:T(8,128)(2,1)S(1)}, bf16[3456,768]{1,0:T(8,128)(2,1)}, u32[]{:S(2)}) copy-start(bf16[3456,768]{1,0:T(8,128)(2,1)} %param.7) | copy-start | bytes 15925252
  15.6 3.6 %collective-permute-start.3 = (bf16[128,512]{1,0:T(8,128)(2,1)S(1)}, bf16[128,512]{1,0:T(8,128)(2,1)S(1)}, u32[]{:S(2)}, u32[]{:S(2)}) collective-permute-start(bf16[128,512]{1,0:T(8,128)(2,1)S(1)} %slice.24), channel_id=1, source_target_pairs={{0,8},{8,0},{1,9},{9,1},{2,10},{10,2},{3,11},{11,3},{4,12},{12,4},... | collective-permute-start | bytes 393224 | tf_op jit(solution)/shard_map/ppermute | solution.py:564
  19.2 7.1 %copy-start.8 = (bf16[64,3456]{1,0:T(8,128)(2,1)}, bf16[64,3456]{1,0:T(8,128)(2,1)S(1)}, u32[]{:S(2)}) copy-start(bf16[64,3456]{1,0:T(8,128)(2,1)S(1)} %collective-permute-done.1.refs_3_) | copy-start | bytes 1327108
  19.3 1.6 %collective-permute-start.5 = (f32[64,768]{1,0:T(8,128)S(1)}, f32[64,768]{1,0:T(8,128)S(1)}, u32[]{:S(2)}, u32[]{:S(2)}) collective-permute-start(f32[64,768]{1,0:T(8,128)S(1)} %slice.26), channel_id=1, source_target_pairs={{0,8},{8,0},{1,9},{9,1},{2,10},{10,2},{3,11},{11,3},{4,12},{12,4},... | collective-permute-start | bytes 589832 | tf_op jit(solution)/shard_map/ppermute | solution.py:564
  20.6 4.8 %collective-permute-start.4 = (f32[64,768]{1,0:T(8,128)S(1)}, f32[64,768]{1,0:T(8,128)S(1)}, u32[]{:S(2)}, u32[]{:S(2)}) collective-permute-start(f32[64,768]{1,0:T(8,128)S(1)} %fusion.24), channel_id=1, source_target_pairs={{0,8},{8,0},{1,9},{9,1},{2,10},{10,2},{3,11},{11,3},{4,12},{12,4},... | collective-permute-start | bytes 589832 | tf_op jit(solution)/shard_map/ppermute | solution.py:564
  20.8 34.3 %copy-start.1 = (bf16[768,512]{1,0:T(8,128)(2,1)S(1)}, bf16[768,512]{1,0:T(8,128)(2,1)}, u32[]{:S(2)}) copy-start(bf16[768,512]{1,0:T(8,128)(2,1)} %second.1) | copy-start | bytes 2359300
  25.4 8.7 %copy-start.9 = (bf16[64,3456]{1,0:T(8,128)(2,1)}, bf16[64,3456]{1,0:T(8,128)(2,1)S(1)}, u32[]{:S(2)}) copy-start(bf16[64,3456]{1,0:T(8,128)(2,1)S(1)} %collective-permute-done.refs_2_) | copy-start | bytes 1327108
  27.0 15.3 %all-to-all-start = ((bf16[16,8,768]{2,1,0:T(8,128)(2,1)}), bf16[16,8,768]{2,1,0:T(8,128)(2,1)S(1)}, u32[]{:S(2)}, u32[]{:S(2)}) async-start(bf16[16,8,768]{2,1,0:T(8,128)(2,1)} %fusion.5), calls=%async_computation | async-start | bytes 393216 | tf_op jit(solution)/shard_map/all_to_all | solution.py:568
  53.7 1.4 %collective-permute-start.6 = (bf16[128,768]{1,0:T(8,128)(2,1)S(1)}, bf16[128,768]{1,0:T(8,128)(2,1)S(1)}, u32[]{:S(2)}, u32[]{:S(2)}) collective-permute-start(bf16[128,768]{1,0:T(8,128)(2,1)S(1)} %bitcast.15), channel_id=1, source_target_pairs={{0,8},{8,0},{1,9},{9,1},{2,10},{10,2},{3,11},{11,3},{4,12},{12,4},... | collective-permute-start | bytes 589832 | tf_op jit(solution)/shard_map/ppermute | solution.py:564
  60.8 1.6 %collective-permute-start.7 = (f32[136,512]{1,0:T(8,128)S(1)}, f32[136,512]{1,0:T(8,128)S(1)}, u32[]{:S(2)}, u32[]{:S(2)}) collective-permute-start(f32[136,512]{1,0:T(8,128)S(1)} %get-tuple-element.51), channel_id=1, source_target_pairs={{0,8},{8,0},{1,9},{9,1},{2,10},{10,2},{3,11},{11,3},{4,12},{12,4},... | collective-permute-start | bytes 835592 | tf_op jit(solution)/shard_map/ppermute | solution.py:564
  63.2 14.8 %all-to-all-start.2 = ((bf16[16,8,1152]{2,1,0:T(8,128)(2,1)}), bf16[16,8,1152]{2,1,0:T(8,128)(2,1)S(1)}, u32[]{:S(2)}, u32[]{:S(2)}) async-start(bf16[16,8,1152]{2,1,0:T(8,128)(2,1)} %bitcast.4), calls=%async_computation.2 | async-start | bytes 589824 | tf_op jit(solution)/shard_map/all_to_all | solution.py:568
  78.0 4.6 %copy-start.10 = (f32[8,1152]{1,0:T(8,128)}, f32[8,1152]{1,0:T(8,128)S(1)}, u32[]{:S(2)}) copy-start(f32[8,1152]{1,0:T(8,128)S(1)} %convert_reduce_fusion.sent_hbm) | copy-start | bytes 110596
  79.1 11.5 %all-to-all-start.3 = ((bf16[16,8,512]{2,1,0:T(8,128)(2,1)}), bf16[16,8,512]{2,1,0:T(8,128)(2,1)S(1)}, u32[]{:S(2)}, u32[]{:S(2)}) async-start(bf16[16,8,512]{2,1,0:T(8,128)(2,1)} %broadcast_in_dim.5), calls=%async_computation.3 | async-start | bytes 262144 | tf_op jit(solution)/shard_map/all_to_all | solution.py:568
  82.6 9.4 %copy-start.2 = (bf16[3456,256]{1,0:T(8,128)(2,1)S(1)}, bf16[3456,256]{1,0:T(8,128)(2,1)}, u32[]{:S(2)}) copy-start(bf16[3456,256]{1,0:T(8,128)(2,1)} %shard_map.94.features) | copy-start | bytes 5308420
  90.6 1.4 %collective-permute-start.8 = (bf16[128,512]{1,0:T(8,128)(2,1)S(1)}, bf16[128,512]{1,0:T(8,128)(2,1)S(1)}, u32[]{:S(2)}, u32[]{:S(2)}) collective-permute-start(bf16[128,512]{1,0:T(8,128)(2,1)S(1)} %bitcast.18), channel_id=1, source_target_pairs={{0,8},{8,0},{1,9},{9,1},{2,10},{10,2},{3,11},{11,3},{4,12},{12,4},... | collective-permute-start | bytes 393224 | tf_op jit(solution)/shard_map/ppermute | solution.py:564

commit v8 on v7

--- a/solution.py
+++ b/solution.py
@@ -209,14 +209,20 @@
             total, target = step(i, (total, target))
     else:
         total, target = lax.fori_loop(0, steps, step, (total, target))
-    sums = [jnp.broadcast_to(x, (images, 128)).T[:1] for x in (total, LOGIT_SCALE * target)]
+    sums = [jnp.broadcast_to(x, (images, 128)).T[:1] for x in (total * PIECE_SCALE, LOGIT_SCALE * target)]
     width = keep.shape[1]
     rows = [x[:, c : c + width] for x in sums for c in range(0, images, width)]
     rows = [jnp.pad(x, ((0, 0), (0, width - x.shape[1]))) for x in rows]
     rows = jnp.concatenate(rows + [jnp.zeros((8 - len(rows), width), F32)])
-    for ref, part in ((keep, weighted[:group]), (send, weighted[group:])):
-        ref[:group, :] = part
-        ref[group:, :] = rows
+    keep[:group, :] = weighted[:group]
+    keep[group:, :] = rows
+    send[:group, :] = weighted[group:].astype(BF16)
+    cut = []
+    for _ in range(3):
+        part = rows.astype(BF16).astype(F32)
+        cut.append(part)
+        rows = rows - part
+    send[group:, :] = jnp.concatenate(cut + [jnp.zeros_like(rows)]).astype(BF16)
     store.wait()
 
 
@@ -233,7 +239,7 @@
         input_output_aliases={5: 2},
         out_shape=[
             jax.ShapeDtypeStruct((group + 8, width), F32),
-            jax.ShapeDtypeStruct((group + 8, width), F32),
+            jax.ShapeDtypeStruct((group + 32, width), BF16),
             jax.ShapeDtypeStruct(half.shape, BF16),
         ],
         scratch_shapes=[
@@ -522,16 +528,17 @@
     half = keep.shape[0] - 8
     each = -(-images // width)
 
-    def sums(ref):
+    def sums(rows):
         lines = [
-            jnp.concatenate([ref[half + each * q + r : half + each * q + r + 1, :] for r in range(each)], axis=1)
+            jnp.concatenate([rows[each * q + r : each * q + r + 1, :] for r in range(each)], axis=1)
             for q in range(2)
         ]
         return jnp.concatenate(lines)[:, :images]
 
-    other = sums(got)
-    both = sums(keep) + jnp.concatenate([other[:, images // 2 :], other[:, : images // 2]], axis=1)
-    total = both[0:1, :] * PIECE_SCALE
+    cut = got[half:, :].astype(F32)
+    other = sums(cut[:8] + cut[8:16] + cut[16:24])
+    both = sums(keep[half:, :]) + jnp.concatenate([other[:, images // 2 :], other[:, : images // 2]], axis=1)
+    total = both[0:1, :]
     target = jnp.broadcast_to(jnp.sum(both[1:2, :], axis=1, keepdims=True), (1, half))
     lane = lax.broadcasted_iota(jnp.int32, (1, half), 1)
     lines, last = [], jnp.zeros((1, half), F32)
@@ -543,7 +550,7 @@
         last = jnp.where(lane == i, part, last)
         target = target - part
     riding = jnp.concatenate(lines + [last, jnp.zeros_like(last)])
-    out[:, :width] = (keep[:half, :] + got[:half, :]).astype(BF16)
+    out[:, :width] = (keep[:half, :] + got[:half, :].astype(F32)).astype(BF16)
     out[:, width : width + half] = jnp.concatenate([riding] * (half // 8)).astype(BF16)
     out[:, width + half :] = picked[...]
 

time: 97.3 us -> 97.1 us (level)
  no operation moved by 1% of the time
where the time goes in v8:
time: 97.1 us; the launch traced here: 96.4 us
  Pallas kernels  34.7 us (36%)
  starting transfers between devices  18.5 us (19%)
  waiting for transfers between devices  16.5 us (17%)
  blocking collectives  11.3 us (12%)
  local copies, waits for them, and re-layouts  6.81 us (7%)
  matrix products  5.54 us (6%)
  other arithmetic  1.88 us (2%)
  between operations  1.13 us (1%)
    all_to_all x3, starting transfers between devices, to_chips(): return lax.all_to_all(x, ('row', 'gy'), 0, 0, tiled=True)  14.3 us
    all_to_all x1, blocking collectives, to_chips(): return lax.all_to_all(x, ('row', 'gy'), 0, 0, tiled=True)  11.3 us
    pallas_call x1, Pallas kernels, grad_centres(): pl.pallas_call(functools.partial(centres_kernel, LOGIT_SCALE / images), i...  7.93 us
    all_to_all x3, waiting for transfers between devices, to_chips(): return lax.all_to_all(x, ('row', 'gy'), 0, 0, tiled=True)  7.84 us
    pallas_call x1, Pallas kernels, turned_terms(): pl.pallas_call(terms_kernel, in_specs=[HBM] * 3, out_specs=HBM, out_shape...  6.33 us
    pallas_call x1, Pallas kernels, softmax_sums(): pl.pallas_call(functools.partial(softmax_kernel, images <= 256), in_specs...  5.63 us
    dot_general x3, matrix products, partial_hidden(): jnp.dot(jnp.concatenate([blocks[n] for n in names]), first_weight, prefer...  5.22 us
    pallas_call x1, Pallas kernels, prep(): pl.pallas_call(functools.partial(prep_kernel, images <= 256), in_specs=[V...  4.9 us
  transfers between devices with their start and end apart: 12, of which 6 were waited for; matrix products, arithmetic and copies ran while one was open for 8% of the time, Pallas kernels for 25%

profile of v8, /device:TPU:0, one launch (start us, length us, event | category | flops | bytes accessed | tf_op | source)
XLA Modules:
  0.0 96.4 jit_solution(13462580789648924701)
XLA Ops:
  0.7 1.4 %constant_dynamic-slice_fusion.1 = (bf16[64,3456]{1,0:T(8,128)(2,1)S(1)}, bf16[64,3456]{1,0:T(8,128)(2,1)S(1)}, bf16[64,3456]{1,0:T(8,128)(2,1)S(1)}) fusion(bf16[64,13824]{1,0:T(8,128)(2,1)} %param.6, s32[]{:T(128)S(6)} %select_n.53, s32[]{:T(128)S(6)} %select_n.51, s32[]{:T(128)S(6)} %select_n.50), kind=kLoop, calls=%fused_computation.35 | loop fusion | bytes 2654220 | tf_op jit(solution)/shard_map/dynamic_slice | solution.py:603
  2.1 0.5 collective-permute-start.2
  2.6 2.6 %collective-permute-start.1 = (bf16[64,3456]{1,0:T(8,128)(2,1)S(1)}, bf16[64,3456]{1,0:T(8,128)(2,1)S(1)}, u32[]{:S(2)}, u32[]{:S(2)}) collective-permute-start(bf16[64,3456]{1,0:T(8,128)(2,1)S(1)} %get-tuple-element.67), channel_id=1, source_target_pairs={{0,24},{8,16},{16,8},{24,0},{1,25},{9,17},{17,9},{25,1},{2,26},{10... | collective-permute-start | bytes 1327112 | tf_op jit(solution)/shard_map/ppermute | solution.py:607
  5.3 0.7 broadcast_add_fusion
  6.1 0.8 reshape.61
  7.0 1.0 %constant_dynamic-slice_fusion.refs_0_ = bf16[64,3456]{1,0:T(8,128)(2,1)S(1)} fusion(bf16[64,13824]{1,0:T(8,128)(2,1)} %param.6, s32[]{:T(128)S(6)} %select_n.56), kind=kLoop, calls=%fused_computation.34 | loop fusion | bytes 884740 | tf_op jit(solution)/shard_map/dynamic_slice | solution.py:601
  8.1 2.6 %copy-done = bf16[4864,512]{1,0:T(8,128)(2,1)S(1)} copy-done((bf16[4864,512]{1,0:T(8,128)(2,1)S(1)}, bf16[4864,512]{1,0:T(8,128)(2,1)}, u32[]{:S(2)}) %copy-start) | copy-done | bytes 4980760
  10.6 4.9 %shard_map.93 = (bf16[24320,512]{1,0:T(8,128)(2,1)}, bf16[256,512]{1,0:T(8,128)(2,1)S(1)}) custom-call(s32[1,256]{1,0:T(1,128)S(1)} %broadcast_in_dim_reshape.3.marks.marks_hbm, s32[4,1216]{1,0:T(4,128)S(1)} %reshape.62.classes.classes_hbm, bf16[4864,512]{1,0:T(8,128)(2,1)S(1)} %copy-done), custom_call_target="tpu_custom_call" | custom-call | flops 1275068416 | bytes 19922944 | tf_op jit(solution)/shard_map/pallas_call | solution.py:122
  15.7 3.4 %fusion = f32[128,768]{1,0:T(8,128)S(1)} fusion(bf16[3456,768]{1,0:T(8,128)(2,1)} %param.7, bf16[64,3456]{1,0:T(8,128)(2,1)S(1)} %constant_dynamic-slice_fusion.refs_0_, bf16[64,3456]{1,0:T(8,128)(2,1)S(1)} %collective-permute-done.2.refs_1_), kind=kOutput, calls=%fused_computation.1 | convolution fusion | flops 681246720 | bytes 6586368 | tf_op jit(solution)/shard_map/dot_general | solution.py:622
  19.3 0.5 collective-permute-start.5
  19.8 0.9 fusion.24
  20.9 4.5 %collective-permute-done.refs_2_ = bf16[64,3456]{1,0:T(8,128)(2,1)S(1)} collective-permute-done((bf16[64,3456]{1,0:T(8,128)(2,1)S(1)}, bf16[64,3456]{1,0:T(8,128)(2,1)S(1)}, u32[]{:S(2)}, u32[]{:S(2)}) %collective-permute-start) | collective-permute-done | bytes 442400 | tf_op jit(solution)/shard_map/ppermute | solution.py:607
  25.4 0.9 convolution_add_fusion
  26.3 0.7 fusion.5
  27.0 7.1 %all-to-all-start = ((bf16[16,8,768]{2,1,0:T(8,128)(2,1)}), bf16[16,8,768]{2,1,0:T(8,128)(2,1)S(1)}, u32[]{:S(2)}, u32[]{:S(2)}) async-start(bf16[16,8,768]{2,1,0:T(8,128)(2,1)} %fusion.5), calls=%async_computation | async-start | bytes 393216 | tf_op jit(solution)/shard_map/all_to_all | solution.py:575
  34.1 4.7 %shard_map.94.features = bf16[3456,256]{1,0:T(8,128)(2,1)} custom-call(s32[1]{0:T(128)} %bitcast.2.place_ref, bf16[64,3456]{1,0:T(8,128)(2,1)} %copy-done.6, bf16[64,3456]{1,0:T(8,128)(2,1)} %copy-done.7, bf16[64,3456]{1,0:T(8,128)(2,1)} %copy-done.9, bf16[64,3456]{1,0:T(8,128)(2,1)} %copy-done.8), custom_call_target="tpu_custom_call" | custom-call | bytes 3538944 | tf_op jit(solution)/shard_map/pallas_call | solution.py:453
  38.8 3.5 %all-to-all-done = bf16[16,8,768]{2,1,0:T(8,128)(2,1)S(1)} async-done(((bf16[16,8,768]{2,1,0:T(8,128)(2,1)}), bf16[16,8,768]{2,1,0:T(8,128)(2,1)S(1)}, u32[]{:S(2)}, u32[]{:S(2)}) %all-to-all-start) | async-done | bytes 196640 | tf_op jit(solution)/shard_map/all_to_all | solution.py:575
  42.4 11.3 %all_to_all.20 = bf16[16,8,768]{2,1,0:T(8,128)(2,1)S(1)} all-to-all(bf16[16,8,768]{2,1,0:T(8,128)(2,1)S(1)} %broadcast_in_dim.4), channel_id=1, replica_groups=mesh['row'=2,'core'=2,'gy'=8] {'row','gy'}, dimensions={0} | all-to-all | bytes 393216 | tf_op jit(solution)/shard_map/all_to_all | solution.py:575
  53.7 1.4 %collective-permute-done.6.hid_b_hbm.hid_b = bf16[128,768]{1,0:T(8,128)(2,1)S(1)} collective-permute-done((bf16[128,768]{1,0:T(8,128)(2,1)S(1)}, bf16[128,768]{1,0:T(8,128)(2,1)S(1)}, u32[]{:S(2)}, u32[]{:S(2)}) %collective-permute-start.6) | collective-permute-done | bytes 196640 | tf_op jit(solution)/shard_map/ppermute | solution.py:571
  55.1 5.6 %shard_map.95 = (f32[136,512]{1,0:T(8,128)S(1)}, bf16[160,512]{1,0:T(8,128)(2,1)S(1)}, bf16[24320,512]{1,0:T(8,128)(2,1)}) custom-call(bf16[128,768]{1,0:T(8,128)(2,1)S(1)} %bitcast.16, bf16[128,768]{1,0:T(8,128)(2,1)S(1)} %collective-permute-done.6.hid_b_hbm.hid_b, bf16[768,512]{1,0:T(8,128)(2,1)S(1)} %copy-done.1, ...), custom_call_target="tpu_custom_call", output_to_operand_aliasing={{2}: (5, {})} | custom-call | flops 2550136832 | bytes 9961472 | tf_op jit(solution)/shard_map/pallas_call | solution.py:235
  61.0 1.3 %collective-permute-done.7.got = bf16[160,512]{1,0:T(8,128)(2,1)S(1)} collective-permute-done((bf16[160,512]{1,0:T(8,128)(2,1)S(1)}, bf16[160,512]{1,0:T(8,128)(2,1)S(1)}, u32[]{:S(2)}, u32[]{:S(2)}) %collective-permute-start.7) | collective-permute-done | bytes 163872 | tf_op jit(solution)/shard_map/ppermute | solution.py:571
  62.2 0.8 shard_map.96
  63.0 3.7 %all-to-all-start.2 = ((bf16[16,8,1152]{2,1,0:T(8,128)(2,1)}), bf16[16,8,1152]{2,1,0:T(8,128)(2,1)S(1)}, u32[]{:S(2)}, u32[]{:S(2)}) async-start(bf16[16,8,1152]{2,1,0:T(8,128)(2,1)} %bitcast.4), calls=%async_computation.2 | async-start | bytes 589824 | tf_op jit(solution)/shard_map/all_to_all | solution.py:575
  66.8 0.3 multiply_reduce_fusion.1
  67.1 6.3 %shard_map.97.terms_hbm = bf16[4864,256]{1,0:T(8,128)(2,1)} custom-call(s32[1,256]{1,0:T(1,128)} %copy-done.4, s32[4,1216]{1,0:T(4,128)} %copy-done.3, bf16[24320,512]{1,0:T(8,128)(2,1)} %get-tuple-element.55.shared_hbm), custom_call_target="tpu_custom_call" | custom-call | flops 1275068416 | bytes 19922944 | tf_op jit(solution)/shard_map/pallas_call | solution.py:326
  73.4 4.4 %all-to-all-done.2 = bf16[16,8,1152]{2,1,0:T(8,128)(2,1)S(1)} async-done(((bf16[16,8,1152]{2,1,0:T(8,128)(2,1)}), bf16[16,8,1152]{2,1,0:T(8,128)(2,1)S(1)}, u32[]{:S(2)}, u32[]{:S(2)}) %all-to-all-start.2) | async-done | bytes 294944 | tf_op jit(solution)/shard_map/all_to_all | solution.py:575
  78.0 0.2 multiply_reduce_fusion
  78.3 0.7 broadcast_in_dim.5
  79.0 3.5 %all-to-all-start.3 = ((bf16[16,8,512]{2,1,0:T(8,128)(2,1)}), bf16[16,8,512]{2,1,0:T(8,128)(2,1)S(1)}, u32[]{:S(2)}, u32[]{:S(2)}) async-start(bf16[16,8,512]{2,1,0:T(8,128)(2,1)} %broadcast_in_dim.5), calls=%async_computation.3 | async-start | bytes 262144 | tf_op jit(solution)/shard_map/all_to_all | solution.py:575
  82.5 7.9 %shard_map.98 = (bf16[4864,512]{1,0:T(8,128)(2,1)}, f32[1,1]{1,0:T(1,128)}) custom-call(f32[8,1152]{1,0:T(8,128)} %copy-done.10, bf16[4864,512]{1,0:T(8,128)(2,1)} %cen_hbm.3, bf16[24320,512]{1,0:T(8,128)(2,1)} %get-tuple-element.55.shared_hbm, bf16[4864,256]{1,0:T(8,128)(2,1)} %shard_map.97.terms_hbm), custom_call_target="tpu_custom_call" | custom-call | flops 2550136832 | bytes 19922944 | tf_op jit(solution)/shard_map/pallas_call | solution.py:405
  90.5 1.3 %collective-permute-done.8.grad_b = bf16[128,512]{1,0:T(8,128)(2,1)S(1)} collective-permute-done((bf16[128,512]{1,0:T(8,128)(2,1)S(1)}, bf16[128,512]{1,0:T(8,128)(2,1)S(1)}, u32[]{:S(2)}, u32[]{:S(2)}) %collective-permute-start.8) | collective-permute-done | bytes 131104 | tf_op jit(solution)/shard_map/ppermute | solution.py:571
  91.9 4.4 %shard_map.99 = (bf16[3456,768]{1,0:T(8,128)(2,1)}, bf16[768,512]{1,0:T(8,128)(2,1)}) custom-call(bf16[128,512]{1,0:T(8,128)(2,1)S(1)} %bitcast.19, bf16[128,512]{1,0:T(8,128)(2,1)S(1)} %collective-permute-done.8.grad_b, bf16[128,768]{1,0:T(8,128)(2,1)S(1)} %bitcast.17, bf16[128,768]{1,0:T(8,128)(2,1)S(1)} %collective-permute-done.6.hid_b_hbm.hid_b, ...), custom_call_target="tpu_custom_call" | custom-call | flops 1358954496 | bytes 7077888 | tf_op jit(solution)/shard_map/pallas_call | solution.py:508
  (52 shorter events, 1.3 us)
Async XLA Ops:
  2.1 6.0 %collective-permute-start.2 = (bf16[64,3456]{1,0:T(8,128)(2,1)S(1)}, bf16[64,3456]{1,0:T(8,128)(2,1)S(1)}, u32[]{:S(2)}, u32[]{:S(2)}) collective-permute-start(bf16[64,3456]{1,0:T(8,128)(2,1)S(1)} %get-tuple-element.66), channel_id=1, source_target_pairs={{0,8},{8,0},{16,24},{24,16},{1,9},{9,1},{17,25},{25,17},{2,10},{10... | collective-permute-start | bytes 1327112 | tf_op jit(solution)/shard_map/ppermute | solution.py:607
  2.6 16.7 %collective-permute-start.1 = (bf16[64,3456]{1,0:T(8,128)(2,1)S(1)}, bf16[64,3456]{1,0:T(8,128)(2,1)S(1)}, u32[]{:S(2)}, u32[]{:S(2)}) collective-permute-start(bf16[64,3456]{1,0:T(8,128)(2,1)S(1)} %get-tuple-element.67), channel_id=1, source_target_pairs={{0,24},{8,16},{16,8},{24,0},{1,25},{9,17},{17,9},{25,1},{2,26},{10... | collective-permute-start | bytes 1327112 | tf_op jit(solution)/shard_map/ppermute | solution.py:607
  5.2 20.2 %collective-permute-start = (bf16[64,3456]{1,0:T(8,128)(2,1)S(1)}, bf16[64,3456]{1,0:T(8,128)(2,1)S(1)}, u32[]{:S(2)}, u32[]{:S(2)}) collective-permute-start(bf16[64,3456]{1,0:T(8,128)(2,1)S(1)} %get-tuple-element.68), channel_id=1, source_target_pairs={{0,16},{8,24},{16,0},{24,8},{1,17},{9,25},{17,1},{25,9},{2,18},{10... | collective-permute-start | bytes 1327112 | tf_op jit(solution)/shard_map/ppermute | solution.py:607
  6.1 49.0 %copy-start.3 = (s32[4,1216]{1,0:T(4,128)}, s32[4,1216]{1,0:T(4,128)S(1)}, u32[]{:S(2)}) copy-start(s32[4,1216]{1,0:T(4,128)S(1)} %reshape.62.classes.classes_hbm) | copy-start | bytes 58372
  7.0 48.1 %copy-start.4 = (s32[1,256]{1,0:T(1,128)}, s32[1,256]{1,0:T(1,128)S(1)}, u32[]{:S(2)}) copy-start(s32[1,256]{1,0:T(1,128)S(1)} %broadcast_in_dim_reshape.3.marks.marks_hbm) | copy-start | bytes 3076
  8.0 11.1 %copy-start.6 = (bf16[64,3456]{1,0:T(8,128)(2,1)}, bf16[64,3456]{1,0:T(8,128)(2,1)S(1)}, u32[]{:S(2)}) copy-start(bf16[64,3456]{1,0:T(8,128)(2,1)S(1)} %constant_dynamic-slice_fusion.refs_0_) | copy-start | bytes 1327108
  8.1 2.6 %copy-start = (bf16[4864,512]{1,0:T(8,128)(2,1)S(1)}, bf16[4864,512]{1,0:T(8,128)(2,1)}, u32[]{:S(2)}) copy-start(bf16[4864,512]{1,0:T(8,128)(2,1)} %cen_hbm.3) | copy-start | bytes 14942212
  10.6 8.6 %copy-start.7 = (bf16[64,3456]{1,0:T(8,128)(2,1)}, bf16[64,3456]{1,0:T(8,128)(2,1)S(1)}, u32[]{:S(2)}) copy-start(bf16[64,3456]{1,0:T(8,128)(2,1)S(1)} %collective-permute-done.2.refs_1_) | copy-start | bytes 1327108
  10.6 9.1 %copy-start.5 = (bf16[3456,768]{1,0:T(8,128)(2,1)S(1)}, bf16[3456,768]{1,0:T(8,128)(2,1)}, u32[]{:S(2)}) copy-start(bf16[3456,768]{1,0:T(8,128)(2,1)} %param.7) | copy-start | bytes 15925252
  15.6 3.6 %collective-permute-start.3 = (bf16[128,512]{1,0:T(8,128)(2,1)S(1)}, bf16[128,512]{1,0:T(8,128)(2,1)S(1)}, u32[]{:S(2)}, u32[]{:S(2)}) collective-permute-start(bf16[128,512]{1,0:T(8,128)(2,1)S(1)} %slice.24), channel_id=1, source_target_pairs={{0,8},{8,0},{1,9},{9,1},{2,10},{10,2},{3,11},{11,3},{4,12},{12,4},... | collective-permute-start | bytes 393224 | tf_op jit(solution)/shard_map/ppermute | solution.py:571
  19.2 7.1 %copy-start.8 = (bf16[64,3456]{1,0:T(8,128)(2,1)}, bf16[64,3456]{1,0:T(8,128)(2,1)S(1)}, u32[]{:S(2)}) copy-start(bf16[64,3456]{1,0:T(8,128)(2,1)S(1)} %collective-permute-done.1.refs_3_) | copy-start | bytes 1327108
  19.3 1.6 %collective-permute-start.5 = (f32[64,768]{1,0:T(8,128)S(1)}, f32[64,768]{1,0:T(8,128)S(1)}, u32[]{:S(2)}, u32[]{:S(2)}) collective-permute-start(f32[64,768]{1,0:T(8,128)S(1)} %slice.26), channel_id=1, source_target_pairs={{0,8},{8,0},{1,9},{9,1},{2,10},{10,2},{3,11},{11,3},{4,12},{12,4},... | collective-permute-start | bytes 589832 | tf_op jit(solution)/shard_map/ppermute | solution.py:571
  20.6 4.8 %collective-permute-start.4 = (f32[64,768]{1,0:T(8,128)S(1)}, f32[64,768]{1,0:T(8,128)S(1)}, u32[]{:S(2)}, u32[]{:S(2)}) collective-permute-start(f32[64,768]{1,0:T(8,128)S(1)} %fusion.24), channel_id=1, source_target_pairs={{0,8},{8,0},{1,9},{9,1},{2,10},{10,2},{3,11},{11,3},{4,12},{12,4},... | collective-permute-start | bytes 589832 | tf_op jit(solution)/shard_map/ppermute | solution.py:571
  20.8 34.3 %copy-start.1 = (bf16[768,512]{1,0:T(8,128)(2,1)S(1)}, bf16[768,512]{1,0:T(8,128)(2,1)}, u32[]{:S(2)}) copy-start(bf16[768,512]{1,0:T(8,128)(2,1)} %second.1) | copy-start | bytes 2359300
  25.4 8.7 %copy-start.9 = (bf16[64,3456]{1,0:T(8,128)(2,1)}, bf16[64,3456]{1,0:T(8,128)(2,1)S(1)}, u32[]{:S(2)}) copy-start(bf16[64,3456]{1,0:T(8,128)(2,1)S(1)} %collective-permute-done.refs_2_) | copy-start | bytes 1327108
  27.0 15.3 %all-to-all-start = ((bf16[16,8,768]{2,1,0:T(8,128)(2,1)}), bf16[16,8,768]{2,1,0:T(8,128)(2,1)S(1)}, u32[]{:S(2)}, u32[]{:S(2)}) async-start(bf16[16,8,768]{2,1,0:T(8,128)(2,1)} %fusion.5), calls=%async_computation | async-start | bytes 393216 | tf_op jit(solution)/shard_map/all_to_all | solution.py:575
  53.7 1.4 %collective-permute-start.6 = (bf16[128,768]{1,0:T(8,128)(2,1)S(1)}, bf16[128,768]{1,0:T(8,128)(2,1)S(1)}, u32[]{:S(2)}, u32[]{:S(2)}) collective-permute-start(bf16[128,768]{1,0:T(8,128)(2,1)S(1)} %bitcast.15), channel_id=1, source_target_pairs={{0,8},{8,0},{1,9},{9,1},{2,10},{10,2},{3,11},{11,3},{4,12},{12,4},... | collective-permute-start | bytes 589832 | tf_op jit(solution)/shard_map/ppermute | solution.py:571
  60.8 1.5 %collective-permute-start.7 = (bf16[160,512]{1,0:T(8,128)(2,1)S(1)}, bf16[160,512]{1,0:T(8,128)(2,1)S(1)}, u32[]{:S(2)}, u32[]{:S(2)}) collective-permute-start(bf16[160,512]{1,0:T(8,128)(2,1)S(1)} %get-tuple-element.51), channel_id=1, source_target_pairs={{0,8},{8,0},{1,9},{9,1},{2,10},{10,2},{3,11},{11,3},{4,12},{12,4},... | collective-permute-start | bytes 491528 | tf_op jit(solution)/shard_map/ppermute | solution.py:571
  63.0 14.8 %all-to-all-start.2 = ((bf16[16,8,1152]{2,1,0:T(8,128)(2,1)}), bf16[16,8,1152]{2,1,0:T(8,128)(2,1)S(1)}, u32[]{:S(2)}, u32[]{:S(2)}) async-start(bf16[16,8,1152]{2,1,0:T(8,128)(2,1)} %bitcast.4), calls=%async_computation.2 | async-start | bytes 589824 | tf_op jit(solution)/shard_map/all_to_all | solution.py:575
  77.9 4.6 %copy-start.10 = (f32[8,1152]{1,0:T(8,128)}, f32[8,1152]{1,0:T(8,128)S(1)}, u32[]{:S(2)}) copy-start(f32[8,1152]{1,0:T(8,128)S(1)} %convert_reduce_fusion.sent_hbm) | copy-start | bytes 110596
  79.0 11.5 %all-to-all-start.3 = ((bf16[16,8,512]{2,1,0:T(8,128)(2,1)}), bf16[16,8,512]{2,1,0:T(8,128)(2,1)S(1)}, u32[]{:S(2)}, u32[]{:S(2)}) async-start(bf16[16,8,512]{2,1,0:T(8,128)(2,1)} %broadcast_in_dim.5), calls=%async_computation.3 | async-start | bytes 262144 | tf_op jit(solution)/shard_map/all_to_all | solution.py:575
  82.5 9.4 %copy-start.2 = (bf16[3456,256]{1,0:T(8,128)(2,1)S(1)}, bf16[3456,256]{1,0:T(8,128)(2,1)}, u32[]{:S(2)}) copy-start(bf16[3456,256]{1,0:T(8,128)(2,1)} %shard_map.94.features) | copy-start | bytes 5308420
  90.4 1.4 %collective-permute-start.8 = (bf16[128,512]{1,0:T(8,128)(2,1)S(1)}, bf16[128,512]{1,0:T(8,128)(2,1)S(1)}, u32[]{:S(2)}, u32[]{:S(2)}) collective-permute-start(bf16[128,512]{1,0:T(8,128)(2,1)S(1)} %bitcast.18), channel_id=1, source_target_pairs={{0,8},{8,0},{1,9},{9,1},{2,10},{10,2},{3,11},{11,3},{4,12},{12,4},... | collective-permute-start | bytes 393224 | tf_op jit(solution)/shard_map/ppermute | solution.py:571
